TPU v7x, 512 devices: a whole 4x4x16 slice. The times are simulated.
512 devices in a mesh: depth: 4 (over z_hi, core), row: 16 (over x, y), col: 8 (over z_lo).
Axes of the slice: x: 4, y: 4, z: 16 (z_hi: 2, z_lo: 8; z = z_hi * 8 + z_lo), core: 2. Of those that a mesh axis runs over, the one named last changes fastest.
Arguments:
- gate: bfloat16 [4096, 14336], P(('depth', 'col'), 'row'), may hold values from -6 to 6
- up: bfloat16 [4096, 14336], P(('depth', 'col'), 'row'), may hold values from -6 to 6
- down_weight: bfloat16 [14336, 8192], P('row', 'col'), may hold values from -0.046875 to 0.046875
- cotangent: bfloat16 [4096, 8192], P(('depth', 'row'), 'col'), may hold values from -6 to 6
Outputs:
- output: bfloat16 [4096, 8192], P(('depth', 'row'), 'col')
- grad_gate: bfloat16 [4096, 14336], P(('depth', 'col'), 'row')
- grad_up: bfloat16 [4096, 14336], P(('depth', 'col'), 'row')
- grad_weight: bfloat16 [14336, 8192], P('row', 'col')
All inputs are finite; a program needn't handle non-finite values.
Results may differ from a plain program's by a relative error of at most 0.022.
Values may be sent and summed in bfloat16 or wider, within the bound.
No kernel may reach another device: no remote copies, remote signals or barrier semaphores. Data moves between devices by JAX's collectives and lax.ppermute only.
A program may use at most 64 MiB of HBM per device.

v0:
```python
import jax
import jax.numpy as jnp
from jax import lax
from jax.sharding import PartitionSpec as P


def per_device(gate, up, down_weight, cotangent):
    gate_f = gate.astype(jnp.float32)
    up_f = up.astype(jnp.float32)
    sig = jax.nn.sigmoid(gate_f)
    silu_v = gate_f * sig
    hidden = (silu_v * up_f).astype(jnp.bfloat16)
    plane_hidden = lax.all_gather(hidden, "col", axis=0, tiled=True)
    output = lax.psum_scatter(
        jnp.dot(plane_hidden, down_weight, preferred_element_type=jnp.float32).astype(jnp.bfloat16),
        "row",
        scatter_dimension=0,
        tiled=True,
    )
    plane_grad = lax.all_gather(cotangent, "row", axis=0, tiled=True)
    hidden_term = lax.dot_general(
        plane_grad, down_weight, (((1,), (1,)), ((), ())), preferred_element_type=jnp.float32
    )
    weight_term = lax.dot_general(
        plane_hidden, plane_grad, (((0,), (0,)), ((), ())), preferred_element_type=jnp.float32
    )
    grad_hidden = lax.psum_scatter(
        hidden_term.astype(jnp.bfloat16), "col", scatter_dimension=0, tiled=True
    ).astype(jnp.float32)
    grad_gate = (grad_hidden * up_f * sig * (1.0 + gate_f * (1.0 - sig))).astype(jnp.bfloat16)
    grad_up = (grad_hidden * silu_v).astype(jnp.bfloat16)
    grad_weight = lax.psum(weight_term.astype(jnp.bfloat16), "depth")
    return (output, grad_gate, grad_up, grad_weight)


def solution(mesh):
    in_specs = (
        P(("depth", "col"), "row"),
        P(("depth", "col"), "row"),
        P("row", "col"),
        P(("depth", "row"), "col"),
    )
    out_specs = (
        P(("depth", "row"), "col"),
        P(("depth", "col"), "row"),
        P(("depth", "col"), "row"),
        P("row", "col"),
    )
    return jax.shard_map(
        per_device, mesh=mesh, in_specs=in_specs, out_specs=out_specs, check_vma=False
    )
```

profile of v0, /device:TPU:6, one launch (start us, length us, event | category | flops | bytes accessed | tf_op | source)
XLA Modules:
  0.0 485.4 jit_solution(8133214267114056516)
XLA Ops:
  7.2 0.0 copy-start
  7.2 0.0 all-gather.5.cloned.1.call-start
  7.2 0.7 all-gather.5.cloned.1.call-update
  7.9 0.0 reduce-scatter.5.cloned.1.call-start
  8.0 67.4 %all-gather.5.cloned.1.call-done = bf16[1024,1024]{1,0:T(8,128)(2,1)} async-done(((bf16[64,1024]{1,0:T(8,128)(2,1)}), bf16[1024,1024]{1,0:T(8,128)(2,1)}) %all-gather.5.cloned.1.call-update) | async-done | bytes 2097168 | tf_op jit(solution)/shard_map/all_gather | solution.py:20
  75.4 0.0 copy-done
  75.4 5.2 %convolution_convert_fusion.2 = bf16[1024,896]{1,0:T(8,128)(2,1)} fusion(bf16[1024,1024]{1,0:T(8,128)(2,1)} %all-gather.5.cloned.1.call-done, bf16[896,1024]{1,0:T(8,128)(2,1)S(1)} %copy-done), kind=kOutput, calls=%fused_computation.2 | convolution fusion | flops 1879965696 | bytes 5767168 | tf_op jit(solution)/shard_map/dot_general | solution.py:21
  80.6 0.0 copy-start.1
  80.6 0.0 copy-start.2
  80.6 0.0 reduce-scatter.5.cloned.1.call-update
  80.6 0.0 all-gather.3.cloned.1.call-start
  80.7 71.7 %reduce-scatter.5.cloned.1.call-done = bf16[128,896]{1,0:T(8,128)(2,1)} async-done(((bf16[1024,896]{1,0:T(8,128)(2,1)}), bf16[128,896]{1,0:T(8,128)(2,1)}) %reduce-scatter.5.cloned.1.call-update) | async-done | bytes 229392 | tf_op jit(solution)/shard_map/reduce_scatter | solution.py:27
  152.3 0.0 copy-done.1
  152.4 0.0 copy-done.2
  152.4 2.0 fusion.4
  154.4 0.0 all-gather.3.cloned.1.call-update
  154.4 0.0 all-reduce.2.cloned.1.call-start
  154.5 65.9 %all-gather.3.cloned.1.call-done = bf16[1024,896]{1,0:T(8,128)(2,1)} async-done(((bf16[128,896]{1,0:T(8,128)(2,1)}), bf16[1024,896]{1,0:T(8,128)(2,1)}) %all-gather.3.cloned.1.call-update) | async-done | bytes 1835024 | tf_op jit(solution)/shard_map/all_gather | solution.py:13
  220.3 5.5 %convolution_convert_fusion.1 = bf16[896,1024]{1,0:T(8,128)(2,1)} fusion(bf16[1024,896]{1,0:T(8,128)(2,1)} %all-gather.3.cloned.1.call-done, bf16[1024,1024]{1,0:T(8,128)(2,1)} %all-gather.5.cloned.1.call-done), kind=kOutput, calls=%fused_computation.1 | convolution fusion | flops 1879965696 | bytes 5767168 | tf_op jit(solution)/shard_map/dot_general | solution.py:24
  225.8 0.0 all-reduce.2.cloned.1.call-update
  225.8 0.0 reduce-scatter.3.cloned.1.call-start
  225.9 5.2 %convolution_convert_fusion = bf16[1024,1024]{1,0:T(8,128)(2,1)} fusion(bf16[1024,896]{1,0:T(8,128)(2,1)} %all-gather.3.cloned.1.call-done, bf16[896,1024]{1,0:T(8,128)(2,1)S(1)} %copy-done), kind=kOutput, calls=%fused_computation | convolution fusion | flops 1880096768 | bytes 5767168 | tf_op jit(solution)/shard_map/dot_general | solution.py:15
  231.0 0.0 reduce-scatter.3.cloned.1.call-update
  231.0 159.1 %all-reduce.2.cloned.1.call-done = bf16[896,1024]{1,0:T(8,128)(2,1)} async-done(((bf16[896,1024]{1,0:T(8,128)(2,1)}), bf16[896,1024]{1,0:T(8,128)(2,1)}) %all-reduce.2.cloned.1.call-update) | async-done | bytes 1835024 | tf_op jit(solution)/shard_map/psum | solution.py:32
  390.2 85.9 %reduce-scatter.3.cloned.1.call-done = bf16[64,1024]{1,0:T(8,128)(2,1)} async-done(((bf16[1024,1024]{1,0:T(8,128)(2,1)}), bf16[64,1024]{1,0:T(8,128)(2,1)}) %reduce-scatter.3.cloned.1.call-update) | async-done | bytes 131088 | tf_op jit(solution)/shard_map/reduce_scatter | solution.py:14
  476.0 2.9 copy.9
Async XLA Ops:
  7.2 68.2 %copy-start = (bf16[896,1024]{1,0:T(8,128)(2,1)S(1)}, bf16[896,1024]{1,0:T(8,128)(2,1)}, u32[]{:S(2)}) copy-start(bf16[896,1024]{1,0:T(8,128)(2,1)} %param.6) | copy-start | bytes 5505028
  7.2 68.2 %all-gather.5.cloned.1.call-start = ((), (), s32[]{:S(2)}) async-start(), calls=%async_computation.4 | async-start | bytes 2228224 | tf_op jit(solution)/shard_map/all_gather | solution.py:20
  7.9 144.4 %reduce-scatter.5.cloned.1.call-start = ((), (), s32[]{:S(2)}) async-start(), calls=%async_computation.5 | async-start | bytes 2064384 | tf_op jit(solution)/shard_map/reduce_scatter | solution.py:27
  80.6 71.8 %copy-start.1 = (bf16[128,896]{1,0:T(8,128)(2,1)S(1)}, bf16[128,896]{1,0:T(8,128)(2,1)}, u32[]{:S(2)}) copy-start(bf16[128,896]{1,0:T(8,128)(2,1)} %param.4) | copy-start | bytes 688132
  80.6 71.8 %copy-start.2 = (bf16[128,896]{1,0:T(8,128)(2,1)S(1)}, bf16[128,896]{1,0:T(8,128)(2,1)}, u32[]{:S(2)}) copy-start(bf16[128,896]{1,0:T(8,128)(2,1)} %param.5) | copy-start | bytes 688132
  80.6 139.7 %all-gather.3.cloned.1.call-start = ((), (), s32[]{:S(2)}) async-start(), calls=%async_computation.2 | async-start | bytes 2064384 | tf_op jit(solution)/shard_map/all_gather | solution.py:13
  154.4 235.8 %all-reduce.2.cloned.1.call-start = ((), (), s32[]{:S(2)}) async-start(), calls=%async_computation.6 | async-start | bytes 3670016 | tf_op jit(solution)/shard_map/psum | solution.py:32
  225.8 250.2 %reduce-scatter.3.cloned.1.call-start = ((), (), s32[]{:S(2)}) async-start(), calls=%async_computation.3 | async-start | bytes 2228224 | tf_op jit(solution)/shard_map/reduce_scatter | solution.py:14
Sparse Core Ops, SparseCore 0:
  11.0 64.3 all-gather.4
  80.7 71.5 reduce-scatter.4
  155.0 65.2 all-gather.2
  225.9 164.1 all-reduce.1
  394.7 81.2 reduce-scatter.2
where the time goes:
time: 486 us; the launch traced here: 485 us
  waiting for transfers between devices  451 us (93%)
  matrix products  15.8 us (3%)
  between operations  13.8 us (3%)
    psum x1, waiting for transfers between devices, per_device(): grad_weight = lax.psum(weight_term.astype(jnp.bfloat16), 'depth')  159 us
    reduce_scatter x1, waiting for transfers between devices, per_device(): lax.psum_scatter(jnp.dot(plane_hidden, down_weight, preferred_element_typ...  85.9 us
    reduce_scatter x1, waiting for transfers between devices, per_device(): lax.psum_scatter(hidden_term.astype(jnp.bfloat16), 'col', scatter_dimensi...  71.7 us
    all_gather x1, waiting for transfers between devices, per_device(): plane_grad = lax.all_gather(cotangent, 'row', axis=0, tiled=True)  67.4 us
    all_gather x1, waiting for transfers between devices, per_device(): plane_hidden = lax.all_gather(hidden, 'col', axis=0, tiled=True)  65.9 us
  transfers between devices with their start and end apart: 5, of which 5 were waited for; matrix products, arithmetic and copies ran while one was open for 1% of the time, Pallas kernels for 0%

commit v1 on v0

v1 whole, which is shorter than its diff:
```python
import functools

import jax
import jax.numpy as jnp
from jax import lax
from jax.experimental import pallas as pl
from jax.experimental.pallas import tpu as pltpu
from jax.sharding import Mesh
from jax.sharding import PartitionSpec as P

BF, F32 = jnp.bfloat16, jnp.float32
AXES = ("zhi", "core", "x", "y", "col")
DIMS = (2, 2, 4, 4, 8)
RING = ("zhi", "col")
VMEM_LIMIT = 40 * 2**20


def flat(c):
    n = 0
    for v, d in zip(c, DIMS):
        n = n * d + v % d
    return n


def pairs(move):
    out = []
    for h in range(2):
        for k in range(2):
            for x in range(4):
                for y in range(4):
                    for c in range(8):
                        out.append((flat((h, k, x, y, c)), flat(move(h, k, x, y, c))))
    return out


def ring_move(s):
    def move(h, k, x, y, c):
        z = (h * 8 + c + s) % 16
        return (z // 8, k, x, y, z % 8)

    return pairs(move)


def plane_move(first, s):
    def move(h, k, x, y, c):
        if (k == 0) == first:
            return (h, k, x + s, y, c)
        return (h, k, x, y + s, c)

    return pairs(move)


SWAP_Z = pairs(lambda h, k, x, y, c: (1 - h, k, x, y, c))
SWAP_CORE = pairs(lambda h, k, x, y, c: (h, 1 - k, x, y, c))


def send(a, perm):
    return lax.ppermute(a, AXES, perm)


def place(pos_ref):
    return pos_ref[0], pos_ref[1], pos_ref[2], pos_ref[3], pos_ref[4]


def cot_rows(cots, pos, zh, x, y):
    h0, core, x0, y0, _ = pos
    kx, ky = (x - x0 + 4) % 4, (y - y0 + 4) % 4
    k1 = jnp.where(core == 0, kx, ky)
    k2 = jnp.where(core == 0, ky, kx)
    zr = (zh + h0) % 2
    return cots[k2, k1, zr]


def term_kernel(pos_ref, cot_ref, w_ref, *out_refs):
    pos = place(pos_ref)
    z = pos[0] * 8 + pos[4]

    def rows(k, halves):
        t = (z + k + 16) % 16
        tl = t % 8
        return [cot_rows(cot_ref, pos, t // 8, tl // 2, (tl % 2) * 2 + h) for h in halves]

    def dot(a):
        return lax.dot_general(
            a, w_ref[...], (((1,), (1,)), ((), ())), preferred_element_type=F32
        ).astype(BF)

    r = dot(jnp.concatenate(rows(4, (0,)) + rows(-4, (1,)) + rows(3, (0, 1)), axis=0))
    out_refs[0][...] = r[:64]
    out_refs[1][...] = r[64:128]
    out_refs[2][...] = r[128:]
    for n, (k, l) in enumerate(((-3, 2), (-2, 1), (-1, 0))):
        r = dot(jnp.concatenate(rows(k, (0, 1)) + rows(l, (0, 1)), axis=0))
        out_refs[3 + 2 * n][...] = r[:128]
        out_refs[4 + 2 * n][...] = r[128:]


def out_kernel(pos_ref, hid_ref, w_ref, *out_refs):
    h0, core, x0, y0, _ = place(pos_ref)
    for j in range(4):
        parts = []
        for i in range(4):
            dx = jnp.where(core == 0, j, i)
            dy = jnp.where(core == 0, i, j)
            row = ((x0 + dx) % 4) * 4 + (y0 + dy) % 4
            parts.append(hid_ref[h0 * 16 + row])
        out_refs[j][...] = jnp.dot(
            jnp.concatenate(parts, axis=0), w_ref[...], preferred_element_type=F32
        ).astype(BF)


def grad_kernel(pos_ref, hid_ref, cot_ref, out_ref, flat_ref):
    pos = place(pos_ref)

    @pl.when(pl.program_id(0) == 0)
    def _():
        for zh in range(2):
            for x in range(4):
                for y in range(4):
                    at = ((zh * 4 + x) * 4 + y) * 64
                    flat_ref[at : at + 64, :] = cot_rows(cot_ref, pos, zh, x, y)

    n = pl.multiple_of(pl.program_id(0) * 256, 256)
    out_ref[...] = lax.dot_general(
        hid_ref[...], flat_ref[:, pl.ds(n, 256)], (((0,), (0,)), ((), ())), preferred_element_type=F32
    ).astype(BF)


SMEM = pl.BlockSpec(memory_space=pltpu.SMEM)
VMEM = pl.BlockSpec(memory_space=pltpu.VMEM)
PARAMS = pltpu.CompilerParams(vmem_limit_bytes=VMEM_LIMIT)


def terms_of(pos, cots, w):
    rows = (64, 64) + (128,) * 7
    return pl.pallas_call(
        term_kernel,
        out_shape=[jax.ShapeDtypeStruct((n, 896), BF) for n in rows],
        in_specs=[SMEM, VMEM, VMEM],
        out_specs=[VMEM] * 9,
        compiler_params=PARAMS,
        cost_estimate=pl.CostEstimate(flops=2 * 1024 * 896 * 1024, bytes_accessed=8 * 2**20, transcendentals=0),
        name="hidden_terms",
    )(pos, cots, w)


def out_of(pos, hid, w):
    return pl.pallas_call(
        out_kernel,
        out_shape=[jax.ShapeDtypeStruct((256, 1024), BF)] * 4,
        in_specs=[SMEM, VMEM, VMEM],
        out_specs=[VMEM] * 4,
        compiler_params=PARAMS,
        cost_estimate=pl.CostEstimate(flops=2 * 1024 * 896 * 1024, bytes_accessed=8 * 2**20, transcendentals=0),
        name="output_terms",
    )(pos, hid.reshape(32, 64, 896), w)


def grad_of(pos, hid, cots):
    return pl.pallas_call(
        grad_kernel,
        grid=(4,),
        out_shape=jax.ShapeDtypeStruct((896, 1024), BF),
        in_specs=[SMEM, VMEM, VMEM],
        out_specs=pl.BlockSpec((896, 256), lambda n: (0, n)),
        scratch_shapes=[pltpu.VMEM((2048, 1024), BF)],
        compiler_params=PARAMS,
        cost_estimate=pl.CostEstimate(flops=2 * 2048 * 896 * 1024, bytes_accessed=10 * 2**20, transcendentals=0),
        name="weight_terms",
    )(pos, hid, cots)


def gather_step(a, first):
    return [a, send(a, plane_move(first, -1)), send(a, plane_move(first, 2)), send(a, plane_move(first, 1))]


def per_device(gate, up, w, cot):
    pos = jnp.stack([lax.axis_index(a) for a in AXES]).astype(jnp.int32)
    gate_f, up_f = gate.astype(F32), up.astype(F32)
    sig = jax.nn.sigmoid(gate_f)
    silu_v = gate_f * sig
    hidden = lax.optimization_barrier((silu_v * up_f).astype(BF))
    hid_all = lax.all_gather(hidden, RING, axis=0, tiled=True)

    both = jnp.stack([cot, send(cot, SWAP_Z)])
    line = jnp.stack(gather_step(both, True))
    cots = jnp.stack(gather_step(line, False))

    terms = terms_of(pos, cots, w)
    p4, m4, p3, m3, p2, m2, p1, m1, own = terms[0], terms[1], terms[2], terms[3], terms[4], terms[5], terms[6], terms[7], terms[8]
    right, left = ring_move(1), ring_move(-1)
    a, b = send(p4, right), send(m4, left)
    a = jnp.concatenate([(p3[:64].astype(F32) + a.astype(F32)).astype(BF), p3[64:]], axis=0)
    b = jnp.concatenate([m3[:64], (m3[64:].astype(F32) + b.astype(F32)).astype(BF)], axis=0)
    a, b = send(a, right), send(b, left)
    for p, m in ((p2, m2), (p1, m1)):
        a = send((a.astype(F32) + p.astype(F32)).astype(BF), right)
        b = send((b.astype(F32) + m.astype(F32)).astype(BF), left)
    grad_hidden = own.astype(F32) + a.astype(F32) + b.astype(F32)
    grad_gate = (grad_hidden * up_f * sig * (1.0 + gate_f * (1.0 - sig))).astype(BF)
    grad_up = (grad_hidden * silu_v).astype(BF)

    o = out_of(pos, hid_all, w)
    got = (o[0], send(o[1], plane_move(True, 1)), send(o[2], plane_move(True, 2)), send(o[3], plane_move(True, -1)))

    def piece(i):
        s = slice(64 * i, 64 * i + 64)
        return sum(g[s].astype(F32) for g in got)

    got2 = [send(piece(i).astype(BF), plane_move(False, s)) for i, s in ((1, 1), (2, 2), (3, -1))]
    output = (piece(0) + sum(g.astype(F32) for g in got2)).astype(BF)

    mine = grad_of(pos, hid_all, cots)
    other = send(mine, SWAP_CORE)
    grad_weight = (mine.astype(F32) + other.astype(F32)).astype(BF)
    return output, grad_gate, grad_up, grad_weight


def solution(mesh):
    mesh = Mesh(mesh.devices.reshape(DIMS), AXES)
    depth, row = ("zhi", "core"), ("x", "y")
    by_col, by_row = P(depth + ("col",), row), P(depth + row, "col")
    weight = P(row, "col")
    return jax.shard_map(
        per_device,
        mesh=mesh,
        in_specs=(by_col, by_col, weight, by_row),
        out_specs=(by_row, by_col, by_col, weight),
        check_vma=False,
    )
```

time: 486 us -> 276 us (0.57)
  waiting for transfers between devices: 451 us -> 134 us
  starting transfers between devices: 0.2 us -> 102 us
  matrix products: 15.8 us -> 0 us
  Pallas kernels: 0 us -> 11.6 us
  other arithmetic: 2.03 us -> 7.94 us
    psum x1 -> x0, waiting for transfers between devices: 159 us -> none  [per_device(): grad_weight = lax.psum(weight_term.astype(jnp.bfloat16), 'depth')]
    reduce_scatter x2 -> x0, waiting for transfers between devices: 158 us -> none  [the longest x1 85.9 us: per_device(): lax.psum_scatter(jnp.dot(plane_hidden, down_weight, preferred_element_typ...]
    ppermute x0 -> x22, starting transfers between devices: none -> 102 us  [send(): return lax.ppermute(a, AXES, perm)]
    ppermute x0 -> x22, waiting for transfers between devices: none -> 57.4 us  [send(): return lax.ppermute(a, AXES, perm)]
    all_gather x2 -> x1, waiting for transfers between devices: 133 us -> 76.7 us  [per_device(): hid_all = lax.all_gather(hidden, RING, axis=0, tiled=True)]
    dot_general x3 -> x0, matrix products: 15.8 us -> none  [the longest x1 5.47 us: per_device(): lax.dot_general(plane_hidden, plane_grad, (((0,), (0,)), ((), ())), prefe...]
    pallas_call x0 -> x3, Pallas kernels: none -> 11.6 us  [the longest x1 5.84 us: grad_of(): pl.pallas_call(grad_kernel, grid=(4,), out_shape=jax.ShapeDtypeStruct((89...]
  transfers between devices with their start and end apart: 5 -> 23, of which waited for: 5 -> 19; matrix products, arithmetic and copies ran while one was open for 1% -> 1% of each run, Pallas kernels for 0% -> 1%
where the time goes in v1:
time: 276 us; the launch traced here: 274 us
  waiting for transfers between devices  134 us (49%)
  starting transfers between devices  102 us (37%)
  between operations  14.4 us (5%)
  Pallas kernels  11.6 us (4%)
  other arithmetic  7.94 us (3%)
  local copies, waits for them, and re-layouts  4.54 us (2%)
    ppermute x22, starting transfers between devices, send(): return lax.ppermute(a, AXES, perm)  102 us
    all_gather x1, waiting for transfers between devices, per_device(): hid_all = lax.all_gather(hidden, RING, axis=0, tiled=True)  76.7 us
    ppermute x22, waiting for transfers between devices, send(): return lax.ppermute(a, AXES, perm)  57.4 us
    pallas_call x1, Pallas kernels, grad_of(): pl.pallas_call(grad_kernel, grid=(4,), out_shape=jax.ShapeDtypeStruct((89...  5.84 us
  transfers between devices with their start and end apart: 23, of which 19 were waited for; matrix products, arithmetic and copies ran while one was open for 1% of the time, Pallas kernels for 1%

profile of v1, /device:TPU:6, one launch (start us, length us, event | category | flops | bytes accessed | tf_op | source)
XLA Modules:
  0.0 274.3 jit_solution(13688977128842820099)
XLA Ops:
  7.2 15.7 %collective-permute-start.6 = (bf16[64,1024]{1,0:T(8,128)(2,1)}, bf16[64,1024]{1,0:T(8,128)(2,1)S(1)}, u32[]{:S(2)}, u32[]{:S(2)}) collective-permute-start(bf16[64,1024]{1,0:T(8,128)(2,1)} %param.7), channel_id=1, source_target_pairs={{0,256},{1,257},{2,258},{3,259},{4,260},{5,261},{6,262},{7,263},{8... | collective-permute-start | bytes 393224 | tf_op jit(solution)/shard_map/ppermute | solution.py:58
  22.9 4.0 %collective-permute-done.6 = bf16[64,1024]{1,0:T(8,128)(2,1)S(1)} collective-permute-done((bf16[64,1024]{1,0:T(8,128)(2,1)}, bf16[64,1024]{1,0:T(8,128)(2,1)S(1)}, u32[]{:S(2)}, u32[]{:S(2)}) %collective-permute-start.6) | collective-permute-done | bytes 131104 | tf_op jit(solution)/shard_map/ppermute | solution.py:58
  26.9 0.9 fusion.8
  27.9 3.3 %collective-permute-start.8 = (bf16[2,64,1024]{2,1,0:T(8,128)(2,1)S(1)}, bf16[2,64,1024]{2,1,0:T(8,128)(2,1)S(1)}, u32[]{:S(2)}, u32[]{:S(2)}) collective-permute-start(bf16[2,64,1024]{2,1,0:T(8,128)(2,1)S(1)} %get-tuple-element.39), channel_id=1, source_target_pairs={{0,64},{1,65},{2,66},{3,67},{4,68},{5,69},{6,70},{7,71},{8,72},{9,... | collective-permute-start | bytes 786440 | tf_op jit(solution)/shard_map/ppermute | solution.py:58
  31.2 3.6 %collective-permute-start.7 = (bf16[2,64,1024]{2,1,0:T(8,128)(2,1)S(1)}, bf16[2,64,1024]{2,1,0:T(8,128)(2,1)S(1)}, u32[]{:S(2)}, u32[]{:S(2)}) collective-permute-start(bf16[2,64,1024]{2,1,0:T(8,128)(2,1)S(1)} %get-tuple-element.39), channel_id=1, source_target_pairs={{0,96},{1,97},{2,98},{3,99},{4,100},{5,101},{6,102},{7,103},{8,104... | collective-permute-start | bytes 786440 | tf_op jit(solution)/shard_map/ppermute | solution.py:58
  34.8 3.5 %collective-permute-start.9 = (bf16[2,64,1024]{2,1,0:T(8,128)(2,1)S(1)}, bf16[2,64,1024]{2,1,0:T(8,128)(2,1)S(1)}, u32[]{:S(2)}, u32[]{:S(2)}) collective-permute-start(bf16[2,64,1024]{2,1,0:T(8,128)(2,1)S(1)} %get-tuple-element.39), channel_id=1, source_target_pairs={{0,32},{1,33},{2,34},{3,35},{4,36},{5,37},{6,38},{7,39},{8,40},{9,... | collective-permute-start | bytes 786440 | tf_op jit(solution)/shard_map/ppermute | solution.py:58
  38.3 2.4 collective-permute-done.7
  40.7 2.4 collective-permute-done.9
  43.2 4.2 %collective-permute-start.11 = (bf16[4,2,64,1024]{3,2,1,0:T(8,128)(2,1)S(1)}, bf16[4,2,64,1024]{3,2,1,0:T(8,128)(2,1)}, u32[]{:S(2)}, u32[]{:S(2)}) collective-permute-start(bf16[4,2,64,1024]{3,2,1,0:T(8,128)(2,1)S(1)} %get-tuple-element.34), channel_id=1, source_target_pairs={{0,16},{1,17},{2,18},{3,19},{4,20},{5,21},{6,22},{7,23},{8,24},{9,... | collective-permute-start | bytes 3145736 | tf_op jit(solution)/shard_map/ppermute | solution.py:58
  47.4 3.0 %collective-permute-start.10 = (bf16[4,2,64,1024]{3,2,1,0:T(8,128)(2,1)S(1)}, bf16[4,2,64,1024]{3,2,1,0:T(8,128)(2,1)}, u32[]{:S(2)}, u32[]{:S(2)}) collective-permute-start(bf16[4,2,64,1024]{3,2,1,0:T(8,128)(2,1)S(1)} %get-tuple-element.34), channel_id=1, source_target_pairs={{0,24},{1,25},{2,26},{3,27},{4,28},{5,29},{6,30},{7,31},{8,0},{9,1... | collective-permute-start | bytes 3145736 | tf_op jit(solution)/shard_map/ppermute | solution.py:58
  50.4 2.9 %collective-permute-start.12 = (bf16[4,2,64,1024]{3,2,1,0:T(8,128)(2,1)S(1)}, bf16[4,2,64,1024]{3,2,1,0:T(8,128)(2,1)}, u32[]{:S(2)}, u32[]{:S(2)}) collective-permute-start(bf16[4,2,64,1024]{3,2,1,0:T(8,128)(2,1)S(1)} %get-tuple-element.34), channel_id=1, source_target_pairs={{0,8},{1,9},{2,10},{3,11},{4,12},{5,13},{6,14},{7,15},{8,16},{9,17... | collective-permute-start | bytes 3145736 | tf_op jit(solution)/shard_map/ppermute | solution.py:58
  53.4 8.3 %collective-permute-done.11 = bf16[4,2,64,1024]{3,2,1,0:T(8,128)(2,1)} collective-permute-done((bf16[4,2,64,1024]{3,2,1,0:T(8,128)(2,1)S(1)}, bf16[4,2,64,1024]{3,2,1,0:T(8,128)(2,1)}, u32[]{:S(2)}, u32[]{:S(2)}) %collective-permute-start.11) | collective-permute-done | bytes 1048608 | tf_op jit(solution)/shard_map/ppermute | solution.py:58
  61.6 10.6 %collective-permute-done.10 = bf16[4,2,64,1024]{3,2,1,0:T(8,128)(2,1)} collective-permute-done((bf16[4,2,64,1024]{3,2,1,0:T(8,128)(2,1)S(1)}, bf16[4,2,64,1024]{3,2,1,0:T(8,128)(2,1)}, u32[]{:S(2)}, u32[]{:S(2)}) %collective-permute-start.10) | collective-permute-done | bytes 1048608 | tf_op jit(solution)/shard_map/ppermute | solution.py:58
  72.2 0.5 collective-permute-done.12
  72.8 2.2 pad_maximum_fusion.cot_ref
  75.2 2.9 %hidden_terms.1 = (bf16[64,896]{1,0:T(8,128)(2,1)S(1)}, bf16[64,896]{1,0:T(8,128)(2,1)S(1)}, bf16[128,896]{1,0:T(8,128)(2,1)S(1)}, bf16[128,896]{1,0:T(8,128)(2,...) custom-call(s32[5]{0:T(128)S(1)} %stack.62.pos_ref, ...), custom_call_target="tpu_custom_call" | custom-call | flops 1879048192 | bytes 8388608 | tf_op jit(solution)/shard_map/hidden_terms/pallas_call | solution.py:136
  78.2 11.5 %collective-permute-start.17 = (bf16[64,896]{1,0:T(8,128)(2,1)S(1)}, bf16[64,896]{1,0:T(8,128)(2,1)S(1)}, u32[]{:S(2)}, u32[]{:S(2)}) collective-permute-start(bf16[64,896]{1,0:T(8,128)(2,1)S(1)} %get-tuple-element.27), channel_id=1, source_target_pairs={{0,263},{1,0},{2,1},{3,2},{4,3},{5,4},{6,5},{7,6},{8,271},{9,8},{1... | collective-permute-start | bytes 344072 | tf_op jit(solution)/shard_map/ppermute | solution.py:58
  89.7 1.9 collective-permute-start.13
  91.6 0.5 collective-permute-done.17
  92.2 7.1 %collective-permute-start.18 = (bf16[128,896]{1,0:T(8,128)(2,1)S(1)}, bf16[128,896]{1,0:T(8,128)(2,1)S(1)}, u32[]{:S(2)}, u32[]{:S(2)}) collective-permute-start(bf16[128,896]{1,0:T(8,128)(2,1)S(1)} %pad_maximum_fusion.4), channel_id=1, source_target_pairs={{0,263},{1,0},{2,1},{3,2},{4,3},{5,4},{6,5},{7,6},{8,271},{9,8},{1... | collective-permute-start | bytes 688136 | tf_op jit(solution)/shard_map/ppermute | solution.py:58
  99.7 1.9 collective-permute-start.14
  101.6 1.4 collective-permute-done.18
  103.1 5.6 %collective-permute-start.19 = (bf16[128,896]{1,0:T(8,128)(2,1)S(1)}, bf16[128,896]{1,0:T(8,128)(2,1)S(1)}, u32[]{:S(2)}, u32[]{:S(2)}) collective-permute-start(bf16[128,896]{1,0:T(8,128)(2,1)S(1)} %add_convert_fusion.2), channel_id=1, source_target_pairs={{0,263},{1,0},{2,1},{3,2},{4,3},{5,4},{6,5},{7,6},{8,271},{9,8},{1... | collective-permute-start | bytes 688136 | tf_op jit(solution)/shard_map/ppermute | solution.py:58
  108.9 1.9 collective-permute-start.15
  110.8 1.4 collective-permute-done.19
  112.3 12.3 %collective-permute-start.20 = (bf16[128,896]{1,0:T(8,128)(2,1)S(1)}, bf16[128,896]{1,0:T(8,128)(2,1)S(1)}, u32[]{:S(2)}, u32[]{:S(2)}) collective-permute-start(bf16[128,896]{1,0:T(8,128)(2,1)S(1)} %add_convert_fusion.1), channel_id=1, source_target_pairs={{0,263},{1,0},{2,1},{3,2},{4,3},{5,4},{6,5},{7,6},{8,271},{9,8},{1... | collective-permute-start | bytes 688136 | tf_op jit(solution)/shard_map/ppermute | solution.py:58
  125.2 1.9 collective-permute-start.16
  127.1 1.0 collective-permute-done.20
  128.2 7.2 %collective-permute-done.16 = bf16[128,896]{1,0:T(8,128)(2,1)S(1)} collective-permute-done((bf16[128,896]{1,0:T(8,128)(2,1)S(1)}, bf16[128,896]{1,0:T(8,128)(2,1)S(1)}, u32[]{:S(2)}, u32[]{:S(2)}) %collective-permute-start.16) | collective-permute-done | bytes 229408 | tf_op jit(solution)/shard_map/ppermute | solution.py:58
  135.4 1.1 multiply_convert_fusion
  136.6 76.7 %all-gather.2.cloned.1.call-done.hid_ref = bf16[2048,896]{1,0:T(8,128)(2,1)} async-done(((bf16[128,896]{1,0:T(8,128)(2,1)}), bf16[2048,896]{1,0:T(8,128)(2,1)}) %all-gather.2.cloned.1.call-update) | async-done | bytes 3670032 | tf_op jit(solution)/shard_map/all_gather | solution.py:183
  213.3 2.2 copy-done.1
  215.5 2.0 copy-done.2
  217.5 5.8 %weight_terms.1 = bf16[896,1024]{1,0:T(8,128)(2,1)S(1)} custom-call(s32[5]{0:T(128)S(1)} %stack.62.pos_ref, bf16[2048,896]{1,0:T(8,128)(2,1)S(1)} %copy-done.2, bf16[4,4,2,64,1024]{4,3,2,1,0:T(8,128)(2,1)S(1)} %copy-done.1), custom_call_target="tpu_custom_call" | custom-call | flops 3758096384 | bytes 10485760 | tf_op jit(solution)/shard_map/weight_terms/pallas_call | solution.py:160
  223.4 1.9 collective-permute-start.21
  225.3 2.9 %output_terms.1 = (bf16[256,1024]{1,0:T(8,128)(2,1)S(1)}, bf16[256,1024]{1,0:T(8,128)(2,1)S(1)}, bf16[256,1024]{1,0:T(8,128)(2,1)S(1)}, bf16[256,1024]{1,0:T(8,128)(2,1)S(1)}) custom-call(s32[5]{0:T(128)S(1)} %stack.62.pos_ref, bf16[32,64,896]{2,1,0:T(8,128)(2,1)S(1)} %bitcast.18, bf16[896,1024]{1,0:T(8,128)(2,1)S(1)} %copy-done.4), custom_call_target="tpu_custom_call" | custom-call | flops 1879048192 | bytes 8388608 | tf_op jit(solution)/shard_map/output_terms/pallas_call | solution.py:148
  228.2 2.5 collective-permute-start
  230.6 4.3 %collective-permute-start.1 = (bf16[256,1024]{1,0:T(8,128)(2,1)S(1)}, bf16[256,1024]{1,0:T(8,128)(2,1)S(1)}, u32[]{:S(2)}, u32[]{:S(2)}) collective-permute-start(bf16[256,1024]{1,0:T(8,128)(2,1)S(1)} %get-tuple-element.19), channel_id=1, source_target_pairs={{0,64},{1,65},{2,66},{3,67},{4,68},{5,69},{6,70},{7,71},{8,72},{9,... | collective-permute-start | bytes 1572872 | tf_op jit(solution)/shard_map/ppermute | solution.py:58
  234.9 1.9 collective-permute-start.2
  236.9 2.4 collective-permute-done
  239.2 4.1 %collective-permute-done.1 = bf16[256,1024]{1,0:T(8,128)(2,1)S(1)} collective-permute-done((bf16[256,1024]{1,0:T(8,128)(2,1)S(1)}, bf16[256,1024]{1,0:T(8,128)(2,1)S(1)}, u32[]{:S(2)}, u32[]{:S(2)}) %collective-permute-start.1) | collective-permute-done | bytes 524320 | tf_op jit(solution)/shard_map/ppermute | solution.py:58
  243.3 5.5 %collective-permute-done.2 = bf16[256,1024]{1,0:T(8,128)(2,1)S(1)} collective-permute-done((bf16[256,1024]{1,0:T(8,128)(2,1)S(1)}, bf16[256,1024]{1,0:T(8,128)(2,1)S(1)}, u32[]{:S(2)}, u32[]{:S(2)}) %collective-permute-start.2) | collective-permute-done | bytes 524320 | tf_op jit(solution)/shard_map/ppermute | solution.py:58
  249.1 3.4 %collective-permute-start.3 = (bf16[64,1024]{1,0:T(8,128)(2,1)S(1)}, bf16[64,1024]{1,0:T(8,128)(2,1)S(1)}, u32[]{:S(2)}, u32[]{:S(2)}) collective-permute-start(bf16[64,1024]{1,0:T(8,128)(2,1)S(1)} %get-tuple-element.30), channel_id=1, source_target_pairs={{0,8},{1,9},{2,10},{3,11},{4,12},{5,13},{6,14},{7,15},{8,16},{9,17... | collective-permute-start | bytes 393224 | tf_op jit(solution)/shard_map/ppermute | solution.py:58
  252.5 3.7 %collective-permute-start.5 = (bf16[64,1024]{1,0:T(8,128)(2,1)S(1)}, bf16[64,1024]{1,0:T(8,128)(2,1)S(1)}, u32[]{:S(2)}, u32[]{:S(2)}) collective-permute-start(bf16[64,1024]{1,0:T(8,128)(2,1)S(1)} %get-tuple-element.31), channel_id=1, source_target_pairs={{0,24},{1,25},{2,26},{3,27},{4,28},{5,29},{6,30},{7,31},{8,0},{9,1... | collective-permute-start | bytes 393224 | tf_op jit(solution)/shard_map/ppermute | solution.py:58
  256.2 3.7 %collective-permute-start.4 = (bf16[64,1024]{1,0:T(8,128)(2,1)S(1)}, bf16[64,1024]{1,0:T(8,128)(2,1)S(1)}, u32[]{:S(2)}, u32[]{:S(2)}) collective-permute-start(bf16[64,1024]{1,0:T(8,128)(2,1)S(1)} %get-tuple-element.32), channel_id=1, source_target_pairs={{0,16},{1,17},{2,18},{3,19},{4,20},{5,21},{6,22},{7,23},{8,24},{9,... | collective-permute-start | bytes 393224 | tf_op jit(solution)/shard_map/ppermute | solution.py:58
  259.9 4.6 %collective-permute-done.4 = bf16[64,1024]{1,0:T(8,128)(2,1)S(1)} collective-permute-done((bf16[64,1024]{1,0:T(8,128)(2,1)S(1)}, bf16[64,1024]{1,0:T(8,128)(2,1)S(1)}, u32[]{:S(2)}, u32[]{:S(2)}) %collective-permute-start.4) | collective-permute-done | bytes 131104 | tf_op jit(solution)/shard_map/ppermute | solution.py:58
  264.5 0.8 add_convert_fusion.5
  265.3 2.1 add_convert_fusion
  (34 shorter events, 2.1 us)
Async XLA Ops:
  7.2 206.1 %all-gather.2.cloned.1.call-start = ((), (), s32[]{:S(2)}) async-start(), calls=%async_computation | async-start | bytes 3899392 | tf_op jit(solution)/shard_map/all_gather | solution.py:183
  7.2 19.7 %collective-permute-start.6 = (bf16[64,1024]{1,0:T(8,128)(2,1)}, bf16[64,1024]{1,0:T(8,128)(2,1)S(1)}, u32[]{:S(2)}, u32[]{:S(2)}) collective-permute-start(bf16[64,1024]{1,0:T(8,128)(2,1)} %param.7), channel_id=1, source_target_pairs={{0,256},{1,257},{2,258},{3,259},{4,260},{5,261},{6,262},{7,263},{8... | collective-permute-start | bytes 393224 | tf_op jit(solution)/shard_map/ppermute | solution.py:58
  27.9 10.4 %collective-permute-start.8 = (bf16[2,64,1024]{2,1,0:T(8,128)(2,1)S(1)}, bf16[2,64,1024]{2,1,0:T(8,128)(2,1)S(1)}, u32[]{:S(2)}, u32[]{:S(2)}) collective-permute-start(bf16[2,64,1024]{2,1,0:T(8,128)(2,1)S(1)} %get-tuple-element.39), channel_id=1, source_target_pairs={{0,64},{1,65},{2,66},{3,67},{4,68},{5,69},{6,70},{7,71},{8,72},{9,... | collective-permute-start | bytes 786440 | tf_op jit(solution)/shard_map/ppermute | solution.py:58
  31.2 9.5 %collective-permute-start.7 = (bf16[2,64,1024]{2,1,0:T(8,128)(2,1)S(1)}, bf16[2,64,1024]{2,1,0:T(8,128)(2,1)S(1)}, u32[]{:S(2)}, u32[]{:S(2)}) collective-permute-start(bf16[2,64,1024]{2,1,0:T(8,128)(2,1)S(1)} %get-tuple-element.39), channel_id=1, source_target_pairs={{0,96},{1,97},{2,98},{3,99},{4,100},{5,101},{6,102},{7,103},{8,104... | collective-permute-start | bytes 786440 | tf_op jit(solution)/shard_map/ppermute | solution.py:58
  34.8 8.3 %collective-permute-start.9 = (bf16[2,64,1024]{2,1,0:T(8,128)(2,1)S(1)}, bf16[2,64,1024]{2,1,0:T(8,128)(2,1)S(1)}, u32[]{:S(2)}, u32[]{:S(2)}) collective-permute-start(bf16[2,64,1024]{2,1,0:T(8,128)(2,1)S(1)} %get-tuple-element.39), channel_id=1, source_target_pairs={{0,32},{1,33},{2,34},{3,35},{4,36},{5,37},{6,38},{7,39},{8,40},{9,... | collective-permute-start | bytes 786440 | tf_op jit(solution)/shard_map/ppermute | solution.py:58
  43.2 18.4 %collective-permute-start.11 = (bf16[4,2,64,1024]{3,2,1,0:T(8,128)(2,1)S(1)}, bf16[4,2,64,1024]{3,2,1,0:T(8,128)(2,1)}, u32[]{:S(2)}, u32[]{:S(2)}) collective-permute-start(bf16[4,2,64,1024]{3,2,1,0:T(8,128)(2,1)S(1)} %get-tuple-element.34), channel_id=1, source_target_pairs={{0,16},{1,17},{2,18},{3,19},{4,20},{5,21},{6,22},{7,23},{8,24},{9,... | collective-permute-start | bytes 3145736 | tf_op jit(solution)/shard_map/ppermute | solution.py:58
  47.4 24.8 %collective-permute-start.10 = (bf16[4,2,64,1024]{3,2,1,0:T(8,128)(2,1)S(1)}, bf16[4,2,64,1024]{3,2,1,0:T(8,128)(2,1)}, u32[]{:S(2)}, u32[]{:S(2)}) collective-permute-start(bf16[4,2,64,1024]{3,2,1,0:T(8,128)(2,1)S(1)} %get-tuple-element.34), channel_id=1, source_target_pairs={{0,24},{1,25},{2,26},{3,27},{4,28},{5,29},{6,30},{7,31},{8,0},{9,1... | collective-permute-start | bytes 3145736 | tf_op jit(solution)/shard_map/ppermute | solution.py:58
  50.4 22.4 %collective-permute-start.12 = (bf16[4,2,64,1024]{3,2,1,0:T(8,128)(2,1)S(1)}, bf16[4,2,64,1024]{3,2,1,0:T(8,128)(2,1)}, u32[]{:S(2)}, u32[]{:S(2)}) collective-permute-start(bf16[4,2,64,1024]{3,2,1,0:T(8,128)(2,1)S(1)} %get-tuple-element.34), channel_id=1, source_target_pairs={{0,8},{1,9},{2,10},{3,11},{4,12},{5,13},{6,14},{7,15},{8,16},{9,17... | collective-permute-start | bytes 3145736 | tf_op jit(solution)/shard_map/ppermute | solution.py:58
  72.8 2.4 copy-start.4
  75.2 14.5 %copy-start = (bf16[4,4,2,64,1024]{4,3,2,1,0:T(8,128)(2,1)}, bf16[4,4,2,64,1024]{4,3,2,1,0:T(8,128)(2,1)S(1)}, u32[]{:S(2)}) copy-start(bf16[4,4,2,64,1024]{4,3,2,1,0:T(8,128)(2,1)S(1)} %pad_maximum_fusion.cot_ref) | copy-start | bytes 12582916
  78.1 57.3 %copy-start.5 = (bf16[128,896]{1,0:T(8,128)(2,1)S(1)}, bf16[128,896]{1,0:T(8,128)(2,1)}, u32[]{:S(2)}) copy-start(bf16[128,896]{1,0:T(8,128)(2,1)} %param.4) | copy-start | bytes 688132
  78.1 57.3 %copy-start.6 = (bf16[128,896]{1,0:T(8,128)(2,1)S(1)}, bf16[128,896]{1,0:T(8,128)(2,1)}, u32[]{:S(2)}) copy-start(bf16[128,896]{1,0:T(8,128)(2,1)} %param.5) | copy-start | bytes 688132
  78.2 13.9 %collective-permute-start.17 = (bf16[64,896]{1,0:T(8,128)(2,1)S(1)}, bf16[64,896]{1,0:T(8,128)(2,1)S(1)}, u32[]{:S(2)}, u32[]{:S(2)}) collective-permute-start(bf16[64,896]{1,0:T(8,128)(2,1)S(1)} %get-tuple-element.27), channel_id=1, source_target_pairs={{0,263},{1,0},{2,1},{3,2},{4,3},{5,4},{6,5},{7,6},{8,271},{9,8},{1... | collective-permute-start | bytes 344072 | tf_op jit(solution)/shard_map/ppermute | solution.py:58
  89.7 10.0 %collective-permute-start.13 = (bf16[64,896]{1,0:T(8,128)(2,1)S(1)}, bf16[64,896]{1,0:T(8,128)(2,1)S(1)}, u32[]{:S(2)}, u32[]{:S(2)}) collective-permute-start(bf16[64,896]{1,0:T(8,128)(2,1)S(1)} %get-tuple-element.23), channel_id=1, source_target_pairs={{0,1},{1,2},{2,3},{3,4},{4,5},{5,6},{6,7},{7,256},{8,9},{9,10},{10... | collective-permute-start | bytes 344072 | tf_op jit(solution)/shard_map/ppermute | solution.py:58
  92.2 10.9 %collective-permute-start.18 = (bf16[128,896]{1,0:T(8,128)(2,1)S(1)}, bf16[128,896]{1,0:T(8,128)(2,1)S(1)}, u32[]{:S(2)}, u32[]{:S(2)}) collective-permute-start(bf16[128,896]{1,0:T(8,128)(2,1)S(1)} %pad_maximum_fusion.4), channel_id=1, source_target_pairs={{0,263},{1,0},{2,1},{3,2},{4,3},{5,4},{6,5},{7,6},{8,271},{9,8},{1... | collective-permute-start | bytes 688136 | tf_op jit(solution)/shard_map/ppermute | solution.py:58
  99.7 9.1 %collective-permute-start.14 = (bf16[128,896]{1,0:T(8,128)(2,1)S(1)}, bf16[128,896]{1,0:T(8,128)(2,1)S(1)}, u32[]{:S(2)}, u32[]{:S(2)}) collective-permute-start(bf16[128,896]{1,0:T(8,128)(2,1)S(1)} %pad_maximum_fusion.3), channel_id=1, source_target_pairs={{0,1},{1,2},{2,3},{3,4},{4,5},{5,6},{6,7},{7,256},{8,9},{9,10},{10... | collective-permute-start | bytes 688136 | tf_op jit(solution)/shard_map/ppermute | solution.py:58
  103.1 9.1 %collective-permute-start.19 = (bf16[128,896]{1,0:T(8,128)(2,1)S(1)}, bf16[128,896]{1,0:T(8,128)(2,1)S(1)}, u32[]{:S(2)}, u32[]{:S(2)}) collective-permute-start(bf16[128,896]{1,0:T(8,128)(2,1)S(1)} %add_convert_fusion.2), channel_id=1, source_target_pairs={{0,263},{1,0},{2,1},{3,2},{4,3},{5,4},{6,5},{7,6},{8,271},{9,8},{1... | collective-permute-start | bytes 688136 | tf_op jit(solution)/shard_map/ppermute | solution.py:58
  108.9 16.2 %collective-permute-start.15 = (bf16[128,896]{1,0:T(8,128)(2,1)S(1)}, bf16[128,896]{1,0:T(8,128)(2,1)S(1)}, u32[]{:S(2)}, u32[]{:S(2)}) collective-permute-start(bf16[128,896]{1,0:T(8,128)(2,1)S(1)} %add_convert_fusion.4), channel_id=1, source_target_pairs={{0,1},{1,2},{2,3},{3,4},{4,5},{5,6},{6,7},{7,256},{8,9},{9,10},{10... | collective-permute-start | bytes 688136 | tf_op jit(solution)/shard_map/ppermute | solution.py:58
  112.3 15.8 %collective-permute-start.20 = (bf16[128,896]{1,0:T(8,128)(2,1)S(1)}, bf16[128,896]{1,0:T(8,128)(2,1)S(1)}, u32[]{:S(2)}, u32[]{:S(2)}) collective-permute-start(bf16[128,896]{1,0:T(8,128)(2,1)S(1)} %add_convert_fusion.1), channel_id=1, source_target_pairs={{0,263},{1,0},{2,1},{3,2},{4,3},{5,4},{6,5},{7,6},{8,271},{9,8},{1... | collective-permute-start | bytes 688136 | tf_op jit(solution)/shard_map/ppermute | solution.py:58
  125.2 10.2 %collective-permute-start.16 = (bf16[128,896]{1,0:T(8,128)(2,1)S(1)}, bf16[128,896]{1,0:T(8,128)(2,1)S(1)}, u32[]{:S(2)}, u32[]{:S(2)}) collective-permute-start(bf16[128,896]{1,0:T(8,128)(2,1)S(1)} %add_convert_fusion.3), channel_id=1, source_target_pairs={{0,1},{1,2},{2,3},{3,4},{4,5},{5,6},{6,7},{7,256},{8,9},{9,10},{10... | collective-permute-start | bytes 688136 | tf_op jit(solution)/shard_map/ppermute | solution.py:58
  213.3 2.2 copy-start.1
  215.5 2.0 copy-start.2
  217.5 7.8 %copy-start.3 = (bf16[2048,896]{1,0:T(8,128)(2,1)S(1)}, bf16[2048,896]{1,0:T(8,128)(2,1)}, u32[]{:S(2)}) copy-start(bf16[2048,896]{1,0:T(8,128)(2,1)} %all-gather.2.cloned.1.call-done.hid_ref) | copy-start | bytes 11010052
  223.4 42.0 %collective-permute-start.21 = (bf16[896,1024]{1,0:T(8,128)(2,1)S(1)}, bf16[896,1024]{1,0:T(8,128)(2,1)S(1)}, u32[]{:S(2)}, u32[]{:S(2)}) collective-permute-start(bf16[896,1024]{1,0:T(8,128)(2,1)S(1)} %weight_terms.1), channel_id=1, source_target_pairs={{0,128},{1,129},{2,130},{3,131},{4,132},{5,133},{6,134},{7,135},{8... | collective-permute-start | bytes 5505032 | tf_op jit(solution)/shard_map/ppermute | solution.py:58
  228.2 11.1 %collective-permute-start = (bf16[256,1024]{1,0:T(8,128)(2,1)S(1)}, bf16[256,1024]{1,0:T(8,128)(2,1)S(1)}, u32[]{:S(2)}, u32[]{:S(2)}) collective-permute-start(bf16[256,1024]{1,0:T(8,128)(2,1)S(1)} %get-tuple-element.18), channel_id=1, source_target_pairs={{0,32},{1,33},{2,34},{3,35},{4,36},{5,37},{6,38},{7,39},{8,40},{9,... | collective-permute-start | bytes 1572872 | tf_op jit(solution)/shard_map/ppermute | solution.py:58
  230.6 12.7 %collective-permute-start.1 = (bf16[256,1024]{1,0:T(8,128)(2,1)S(1)}, bf16[256,1024]{1,0:T(8,128)(2,1)S(1)}, u32[]{:S(2)}, u32[]{:S(2)}) collective-permute-start(bf16[256,1024]{1,0:T(8,128)(2,1)S(1)} %get-tuple-element.19), channel_id=1, source_target_pairs={{0,64},{1,65},{2,66},{3,67},{4,68},{5,69},{6,70},{7,71},{8,72},{9,... | collective-permute-start | bytes 1572872 | tf_op jit(solution)/shard_map/ppermute | solution.py:58
  234.9 13.9 %collective-permute-start.2 = (bf16[256,1024]{1,0:T(8,128)(2,1)S(1)}, bf16[256,1024]{1,0:T(8,128)(2,1)S(1)}, u32[]{:S(2)}, u32[]{:S(2)}) collective-permute-start(bf16[256,1024]{1,0:T(8,128)(2,1)S(1)} %get-tuple-element.20), channel_id=1, source_target_pairs={{0,96},{1,97},{2,98},{3,99},{4,100},{5,101},{6,102},{7,103},{8,104... | collective-permute-start | bytes 1572872 | tf_op jit(solution)/shard_map/ppermute | solution.py:58
  249.1 10.8 %collective-permute-start.3 = (bf16[64,1024]{1,0:T(8,128)(2,1)S(1)}, bf16[64,1024]{1,0:T(8,128)(2,1)S(1)}, u32[]{:S(2)}, u32[]{:S(2)}) collective-permute-start(bf16[64,1024]{1,0:T(8,128)(2,1)S(1)} %get-tuple-element.30), channel_id=1, source_target_pairs={{0,8},{1,9},{2,10},{3,11},{4,12},{5,13},{6,14},{7,15},{8,16},{9,17... | collective-permute-start | bytes 393224 | tf_op jit(solution)/shard_map/ppermute | solution.py:58
  252.5 7.4 %collective-permute-start.5 = (bf16[64,1024]{1,0:T(8,128)(2,1)S(1)}, bf16[64,1024]{1,0:T(8,128)(2,1)S(1)}, u32[]{:S(2)}, u32[]{:S(2)}) collective-permute-start(bf16[64,1024]{1,0:T(8,128)(2,1)S(1)} %get-tuple-element.31), channel_id=1, source_target_pairs={{0,24},{1,25},{2,26},{3,27},{4,28},{5,29},{6,30},{7,31},{8,0},{9,1... | collective-permute-start | bytes 393224 | tf_op jit(solution)/shard_map/ppermute | solution.py:58
  256.2 8.4 %collective-permute-start.4 = (bf16[64,1024]{1,0:T(8,128)(2,1)S(1)}, bf16[64,1024]{1,0:T(8,128)(2,1)S(1)}, u32[]{:S(2)}, u32[]{:S(2)}) collective-permute-start(bf16[64,1024]{1,0:T(8,128)(2,1)S(1)} %get-tuple-element.32), channel_id=1, source_target_pairs={{0,16},{1,17},{2,18},{3,19},{4,20},{5,21},{6,22},{7,23},{8,24},{9,... | collective-permute-start | bytes 393224 | tf_op jit(solution)/shard_map/ppermute | solution.py:58
Sparse Core Ops, SparseCore 0:
  136.7 76.5 all-gather.1

commit v2 on v0

v2 whole, which is shorter than its diff:
```python
import functools

import jax
import jax.numpy as jnp
from jax import lax
from jax.experimental import pallas as pl
from jax.experimental.pallas import tpu as pltpu
from jax.sharding import Mesh
from jax.sharding import PartitionSpec as P

BF, F32 = jnp.bfloat16, jnp.float32
AXES = ("zhi", "core", "x", "y", "col")
DIMS = (2, 2, 4, 4, 8)
RING = ("zhi", "col")
PLANE = ("x", "y")
VMEM_LIMIT = 20 * 2**20


def flat(c):
    n = 0
    for v, d in zip(c, DIMS):
        n = n * d + v % d
    return n


def pairs(move):
    out = []
    for h in range(2):
        for k in range(2):
            for x in range(4):
                for y in range(4):
                    for c in range(8):
                        out.append((flat((h, k, x, y, c)), flat(move(h, k, x, y, c))))
    return out


def ring_move(s):
    def move(h, k, x, y, c):
        z = (h * 8 + c + s) % 16
        return (z // 8, k, x, y, z % 8)

    return pairs(move)


def half_of(h0, col, row):
    k = (row // 2 - col + 11) % 8 - 3
    return (h0 * 8 + col + k + 16) % 16 // 8


def swap_z(wanted):
    out = []
    for h in range(2):
        for k in range(2):
            for x in range(4):
                for y in range(4):
                    for c in range(8):
                        if (half_of(h, c, x * 4 + y) == h) == wanted:
                            out.append((flat((h, k, x, y, c)), flat((1 - h, k, x, y, c))))
    return out


SWAP_CORE = pairs(lambda h, k, x, y, c: (h, 1 - k, x, y, c))
SMEM = pl.BlockSpec(memory_space=pltpu.SMEM)
VMEM = pl.BlockSpec(memory_space=pltpu.VMEM)
ANY = pl.BlockSpec(memory_space=pl.ANY)
PARAMS = pltpu.CompilerParams(vmem_limit_bytes=VMEM_LIMIT)


def cost(flops, mib):
    return pl.CostEstimate(flops=flops, bytes_accessed=int(mib * 2**20), transcendentals=0)


def send(a, perm):
    return lax.ppermute(a, AXES, perm)


def hidden_kernel(gate_ref, up_ref, out_ref):
    g = gate_ref[...].astype(F32)
    out_ref[...] = (g * jax.nn.sigmoid(g) * up_ref[...].astype(F32)).astype(BF)


def hidden_of(gate, up):
    return pl.pallas_call(
        hidden_kernel,
        out_shape=jax.ShapeDtypeStruct(gate.shape, BF),
        grid=(4,),
        in_specs=[pl.BlockSpec((32, 896), lambda i: (i, 0))] * 2,
        out_specs=pl.BlockSpec((32, 896), lambda i: (i, 0)),
        compiler_params=PARAMS,
        cost_estimate=cost(2**20, 1),
        name="hidden",
    )(gate, up)


def copies_kernel(far_wanted, pos_ref, cot_ref, far_ref, *refs):
    mine = half_of(pos_ref[0], pos_ref[4], pos_ref[2] * 4 + pos_ref[3]) == pos_ref[0]

    def fill(ref):
        for i in range(16):
            refs[-1][i] = ref[...]

    pl.when(mine if far_wanted else jnp.logical_not(mine))(lambda: fill(far_ref))
    pl.when(jnp.logical_not(mine) if far_wanted else mine)(lambda: fill(cot_ref))


def copies_of(pos, cot, far_wanted, *after):
    return pl.pallas_call(
        functools.partial(copies_kernel, far_wanted),
        out_shape=jax.ShapeDtypeStruct((16, 64, 1024), BF),
        in_specs=[SMEM, VMEM, VMEM] + [ANY] * len(after),
        out_specs=VMEM,
        compiler_params=PARAMS,
        cost_estimate=cost(0, 2),
        name="copies",
    )(pos, cot, send(cot, swap_z(far_wanted)), *after)


def exchange(blocks):
    return lax.all_to_all(blocks, PLANE, 0, 0, tiled=True)


def term_kernel(pos_ref, near_ref, w_ref, *refs):
    p43, m32, p2, p1, m1, here = refs[-6:]
    col = pos_ref[4]

    def dot(k, l):
        a = jnp.concatenate([near_ref[(col + k + 8) % 8], near_ref[(col + l + 8) % 8]], axis=0)
        return lax.dot_general(
            a, w_ref[...], (((1,), (1,)), ((), ())), preferred_element_type=F32
        ).astype(BF)

    p43[...] = dot(4, 3)
    m32[...] = dot(-3, -2)
    r = dot(2, 1)
    p2[...] = r[:128]
    p1[...] = r[128:]
    r = dot(-1, 0)
    m1[...] = r[:128]
    here[...] = r[128:]


def terms_of(pos, near, w, *after):
    return pl.pallas_call(
        term_kernel,
        out_shape=[jax.ShapeDtypeStruct((n, 896), BF) for n in (256, 256, 128, 128, 128, 128)],
        in_specs=[SMEM, VMEM, VMEM] + [ANY] * len(after),
        out_specs=[VMEM] * 6,
        compiler_params=PARAMS,
        cost_estimate=cost(2 * 1024 * 896 * 1024, 8),
        name="hidden_terms",
    )(pos, near.reshape(8, 128, 1024), w, *after)


def out_kernel(pos_ref, hid_ref, w_ref, out_ref):
    at = pos_ref[0] * 1024
    for i in range(4):
        a = hid_ref[pl.ds(pl.multiple_of(at + 256 * i, 256), 256), :]
        out_ref[256 * i : 256 * i + 256] = jnp.dot(a, w_ref[...], preferred_element_type=F32).astype(BF)


def out_of(pos, hid, w):
    return pl.pallas_call(
        out_kernel,
        out_shape=jax.ShapeDtypeStruct((1024, 1024), BF),
        in_specs=[SMEM, VMEM, VMEM],
        out_specs=VMEM,
        compiler_params=PARAMS,
        cost_estimate=cost(2 * 1024 * 896 * 1024, 8),
        name="output_terms",
    )(pos, hid, w)


def total_kernel(got_ref, out_ref):
    total = got_ref[0].astype(F32)
    for i in range(1, 16):
        total = total + got_ref[i].astype(F32)
    out_ref[...] = total.astype(BF)


def total_of(got):
    return pl.pallas_call(
        total_kernel,
        grid=(4,),
        out_shape=jax.ShapeDtypeStruct((64, 1024), BF),
        in_specs=[pl.BlockSpec((16, 16, 1024), lambda i: (0, i, 0))],
        out_specs=pl.BlockSpec((16, 1024), lambda i: (i, 0)),
        compiler_params=PARAMS,
        cost_estimate=cost(2**20, 2),
        name="output_sum",
    )(got)


def grad_kernel(pos_ref, hid_ref, near_ref, rest_ref, *refs):
    out_ref, cot_ref = refs[-2:]
    h0, col = pos_ref[0], pos_ref[4]

    @pl.when(pl.program_id(0) == 0)
    def _():
        for r in range(16):
            h = half_of(h0, col, r)
            cot_ref[pl.ds(pl.multiple_of(h * 1024 + r * 64, 64), 64), :] = near_ref[r]
            cot_ref[pl.ds(pl.multiple_of((1 - h) * 1024 + r * 64, 64), 64), :] = rest_ref[r]

    n = pl.multiple_of(pl.program_id(0) * 256, 256)
    out_ref[...] = lax.dot_general(
        hid_ref[...], cot_ref[:, pl.ds(n, 256)], (((0,), (0,)), ((), ())), preferred_element_type=F32
    ).astype(BF)


def grad_of(pos, hid, near, rest, *after):
    return pl.pallas_call(
        grad_kernel,
        grid=(4,),
        out_shape=jax.ShapeDtypeStruct((896, 1024), BF),
        in_specs=[SMEM, VMEM, VMEM, VMEM] + [ANY] * len(after),
        out_specs=pl.BlockSpec((896, 256), lambda n: (0, n)),
        scratch_shapes=[pltpu.VMEM((2048, 1024), BF)],
        compiler_params=PARAMS,
        cost_estimate=cost(2 * 2048 * 896 * 1024, 10),
        name="weight_terms",
    )(pos, hid, near, rest, *after)


def add(a, b):
    return (a.astype(F32) + b.astype(F32)).astype(BF)


def sum_kernel(a_ref, b_ref, p2_ref, p1_ref, m1_ref, *refs):
    c, d, e = refs[-3:]
    c[...] = (a_ref[:128].astype(F32) + p2_ref[...].astype(F32)).astype(BF)
    d[...] = (a_ref[128:].astype(F32) + p1_ref[...].astype(F32)).astype(BF)
    e[...] = (b_ref[:128].astype(F32) + m1_ref[...].astype(F32)).astype(BF)


def sums_of(a, b, p2, p1, m1, *after):
    return pl.pallas_call(
        sum_kernel,
        out_shape=[jax.ShapeDtypeStruct((128, 896), BF)] * 3,
        in_specs=[VMEM] * 5 + [ANY] * len(after),
        out_specs=[VMEM] * 3,
        compiler_params=PARAMS,
        cost_estimate=cost(2**18, 1),
        name="sums",
    )(a, b, p2, p1, m1, *after)


def per_device(gate, up, w, cot):
    pos = jnp.stack([lax.axis_index(a) for a in AXES]).astype(jnp.int32)
    hid = lax.all_gather(hidden_of(gate, up), RING, axis=0, tiled=True)
    near = exchange(copies_of(pos, cot, False))
    rest = copies_of(pos, cot, True, near)
    p43, m32, p2, p1, m1, here = terms_of(pos, near, w, rest)
    rest = exchange(rest)

    right, left, right2, left2 = ring_move(1), ring_move(-1), ring_move(2), ring_move(-2)
    a, b = send(p43, right2), send(m32, left2)
    o = out_of(pos, hid, w)
    c, d, e = sums_of(a, b, p2, p1, m1, o)
    c, d, e = send(c, right2), send(d, right), send(e, left)
    grad_hidden = (
        here.astype(F32) + b[128:].astype(F32) + c.astype(F32) + (d.astype(F32) + e.astype(F32))
    )
    gate_f, up_f = gate.astype(F32), up.astype(F32)
    sig = jax.nn.sigmoid(gate_f)
    grad_gate = (grad_hidden * up_f * sig * (1.0 + gate_f * (1.0 - sig))).astype(BF)
    grad_up = (grad_hidden * (gate_f * sig)).astype(BF)

    output = total_of(exchange(o.reshape(16, 64, 1024)))

    part = grad_of(pos, hid, near, rest, o, c, d, e)
    grad_weight = add(part, send(part, SWAP_CORE))
    return output, grad_gate, grad_up, grad_weight


def solution(mesh):
    mesh = Mesh(mesh.devices.reshape(DIMS), AXES)
    depth = ("zhi", "core")
    by_col, by_row = P(depth + ("col",), PLANE), P(depth + PLANE, "col")
    weight = P(PLANE, "col")
    return jax.shard_map(
        per_device,
        mesh=mesh,
        in_specs=(by_col, by_col, weight, by_row),
        out_specs=(by_row, by_col, by_col, weight),
        check_vma=False,
    )
```

time: 486 us -> 175 us (0.36)
  waiting for transfers between devices: 451 us -> 56.8 us
  starting transfers between devices: 0.2 us -> 59.5 us
  Pallas kernels: 0 us -> 23.6 us
  matrix products: 15.8 us -> 0 us
  local copies, waits for them, and re-layouts: 2.89 us -> 14.3 us
    psum x1 -> x0, waiting for transfers between devices: 159 us -> none  [per_device(): grad_weight = lax.psum(weight_term.astype(jnp.bfloat16), 'depth')]
    reduce_scatter x2 -> x0, waiting for transfers between devices: 158 us -> none  [the longest x1 85.9 us: per_device(): lax.psum_scatter(jnp.dot(plane_hidden, down_weight, preferred_element_typ...]
    all_gather x2 -> x1, waiting for transfers between devices: 133 us -> 20.9 us  [per_device(): hid = lax.all_gather(hidden_of(gate, up), RING, axis=0, tiled=True)]
    ppermute x0 -> x8, starting transfers between devices: none -> 36 us  [send(): return lax.ppermute(a, AXES, perm)]
    all_to_all x0 -> x3, waiting for transfers between devices: none -> 31.5 us  [exchange(): return lax.all_to_all(blocks, PLANE, 0, 0, tiled=True)]
    pallas_call x0 -> x8, Pallas kernels: none -> 23.6 us  [the longest x1 7.44 us: grad_of(): pl.pallas_call(grad_kernel, grid=(4,), out_shape=jax.ShapeDtypeStruct((89...]
    all_to_all x0 -> x3, starting transfers between devices: none -> 23.5 us  [exchange(): return lax.all_to_all(blocks, PLANE, 0, 0, tiled=True)]
    dot_general x3 -> x0, matrix products: 15.8 us -> none  [the longest x1 5.47 us: per_device(): lax.dot_general(plane_hidden, plane_grad, (((0,), (0,)), ((), ())), prefe...]
  transfers between devices with their start and end apart: 5 -> 12, of which waited for: 5 -> 5; matrix products, arithmetic and copies ran while one was open for 1% -> 1% of each run, Pallas kernels for 0% -> 13%
where the time goes in v2:
time: 175 us; the launch traced here: 174 us
  starting transfers between devices  59.5 us (34%)
  waiting for transfers between devices  56.8 us (32%)
  Pallas kernels  23.6 us (13%)
  local copies, waits for them, and re-layouts  14.3 us (8%)
  between operations  14.2 us (8%)
  other arithmetic  5.73 us (3%)
    ppermute x8, starting transfers between devices, send(): return lax.ppermute(a, AXES, perm)  36 us
    all_to_all x3, waiting for transfers between devices, exchange(): return lax.all_to_all(blocks, PLANE, 0, 0, tiled=True)  31.5 us
    all_to_all x3, starting transfers between devices, exchange(): return lax.all_to_all(blocks, PLANE, 0, 0, tiled=True)  23.5 us
    all_gather x1, waiting for transfers between devices, per_device(): hid = lax.all_gather(hidden_of(gate, up), RING, axis=0, tiled=True)  20.9 us
    unnamed x32, local copies, waits for them, and re-layouts  14.2 us
    pallas_call x1, Pallas kernels, grad_of(): pl.pallas_call(grad_kernel, grid=(4,), out_shape=jax.ShapeDtypeStruct((89...  7.44 us
    ppermute x8, waiting for transfers between devices, send(): return lax.ppermute(a, AXES, perm)  4.43 us
    pallas_call x1, Pallas kernels, out_of(): pl.pallas_call(out_kernel, out_shape=jax.ShapeDtypeStruct((1024, 1024), B...  4.19 us
  transfers between devices with their start and end apart: 12, of which 5 were waited for; matrix products, arithmetic and copies ran while one was open for 1% of the time, Pallas kernels for 13%

profile of v2, /device:TPU:6, one launch (start us, length us, event | category | flops | bytes accessed | tf_op | source)
XLA Modules:
  0.0 174.2 jit_solution(4382358853956632870)
XLA Ops:
  7.2 0.0 all-gather.2.cloned.1.call-start
  7.2 0.0 copy-start.6
  7.2 0.9 copy-done.6
  8.2 0.9 copy-done.8
  9.1 1.4 hidden.1
  10.4 0.0 all-gather.2.cloned.1.call-update
  10.5 15.7 %collective-permute-start = (bf16[64,1024]{1,0:T(8,128)(2,1)}, bf16[64,1024]{1,0:T(8,128)(2,1)S(1)}, u32[]{:S(2)}, u32[]{:S(2)}) collective-permute-start(bf16[64,1024]{1,0:T(8,128)(2,1)} %cot_ref.3), channel_id=1, source_target_pairs={{4,260},{5,261},{6,262},{7,263},{12,268},{13,269},{14,270},{15,271... | collective-permute-start | bytes 393224 | tf_op jit(solution)/shard_map/ppermute | solution.py:74
  26.2 0.1 stack.23.pos_ref
  26.3 3.6 %collective-permute-done.far_ref = bf16[64,1024]{1,0:T(8,128)(2,1)S(1)} collective-permute-done((bf16[64,1024]{1,0:T(8,128)(2,1)}, bf16[64,1024]{1,0:T(8,128)(2,1)S(1)}, u32[]{:S(2)}, u32[]{:S(2)}) %collective-permute-start) | collective-permute-done | bytes 131104 | tf_op jit(solution)/shard_map/ppermute | solution.py:74
  29.9 0.9 copy-done.10
  30.8 2.0 %copies.2 = bf16[16,64,1024]{2,1,0:T(8,128)(2,1)} custom-call(s32[5]{0:T(128)S(1)} %stack.23.pos_ref, bf16[64,1024]{1,0:T(8,128)(2,1)S(1)} %copy-done.10, bf16[64,1024]{1,0:T(8,128)(2,1)S(1)} %collective-permute-done.far_ref), custom_call_target="tpu_custom_call" | custom-call | bytes 2097152 | tf_op jit(solution)/shard_map/copies/pallas_call | solution.py:107
  32.8 7.6 %all-to-all-start.1 = ((bf16[16,64,1024]{2,1,0:T(8,128)(2,1)}), bf16[16,64,1024]{2,1,0:T(8,128)(2,1)S(1)}, u32[]{:S(2)}, u32[]{:S(2)}) async-start(bf16[16,64,1024]{2,1,0:T(8,128)(2,1)} %copies.2), calls=%async_computation.1 | async-start | bytes 4194304 | tf_op jit(solution)/shard_map/all_to_all | solution.py:119
  40.4 0.7 collective-permute-start.1
  41.1 0.0 collective-permute-done.1.far_ref
  41.1 26.4 %all-to-all-done.1.refs_0_.near_ref = bf16[16,64,1024]{2,1,0:T(8,128)(2,1)S(1)} async-done(((bf16[16,64,1024]{2,1,0:T(8,128)(2,1)}), bf16[16,64,1024]{2,1,0:T(8,128)(2,1)S(1)}, u32[]{:S(2)}, u32[]{:S(2)}) %all-to-all-start.1) | async-done | bytes 2097184 | tf_op jit(solution)/shard_map/all_to_all | solution.py:119
  67.5 0.7 copies.3.refs_0_
  68.2 1.3 copy-done
  69.6 6.5 %all-to-all-start.2 = ((bf16[16,64,1024]{2,1,0:T(8,128)(2,1)}), bf16[16,64,1024]{2,1,0:T(8,128)(2,1)}, u32[]{:S(2)}, u32[]{:S(2)}) async-start(bf16[16,64,1024]{2,1,0:T(8,128)(2,1)} %copy-done), calls=%async_computation.2 | async-start | bytes 4194304 | tf_op jit(solution)/shard_map/all_to_all | solution.py:119
  76.1 1.6 copy-done.1
  77.7 1.5 copy-done.4
  79.2 3.5 %hidden_terms.1 = (bf16[256,896]{1,0:T(8,128)(2,1)}, bf16[256,896]{1,0:T(8,128)(2,1)}, bf16[128,896]{1,0:T(8,128)(2,1)S(1)}, bf16[128,896]{1,0:T(8,128)(2,1)S(1)...) custom-call(s32[5]{0:T(128)S(1)} %stack.23.pos_ref, bf16[8,128,1024]{2,1,0:T(8,128)(2,1)S(1)} %bitcast.7, ...), custom_call_target="tpu_custom_call" | custom-call | flops 1879048192 | bytes 8388608 | tf_op jit(solution)/shard_map/hidden_terms/pallas_call | solution.py:143
  82.7 0.7 copy-done.12
  83.3 0.7 copy-done.14
  84.0 5.9 %collective-permute-start.3 = (bf16[256,896]{1,0:T(8,128)(2,1)}, bf16[256,896]{1,0:T(8,128)(2,1)S(1)}, u32[]{:S(2)}, u32[]{:S(2)}) collective-permute-start(bf16[256,896]{1,0:T(8,128)(2,1)} %get-tuple-element.15), channel_id=1, source_target_pairs={{0,2},{1,3},{2,4},{3,5},{4,6},{5,7},{6,256},{7,257},{8,10},{9,11},... | collective-permute-start | bytes 1376264 | tf_op jit(solution)/shard_map/ppermute | solution.py:74
  89.9 4.1 %collective-permute-start.2 = (bf16[256,896]{1,0:T(8,128)(2,1)}, bf16[256,896]{1,0:T(8,128)(2,1)S(1)}, u32[]{:S(2)}, u32[]{:S(2)}) collective-permute-start(bf16[256,896]{1,0:T(8,128)(2,1)} %get-tuple-element.14), channel_id=1, source_target_pairs={{0,262},{1,263},{2,0},{3,1},{4,2},{5,3},{6,4},{7,5},{8,270},{9,271... | collective-permute-start | bytes 1376264 | tf_op jit(solution)/shard_map/ppermute | solution.py:74
  94.0 20.9 %all-gather.2.cloned.1.call-done.hid_ref = bf16[2048,896]{1,0:T(8,128)(2,1)} async-done(((bf16[128,896]{1,0:T(8,128)(2,1)}), bf16[2048,896]{1,0:T(8,128)(2,1)}) %all-gather.2.cloned.1.call-update) | async-done | bytes 3670032 | tf_op jit(solution)/shard_map/all_gather | solution.py:249
  114.9 2.0 %copy-done.2 = bf16[2048,896]{1,0:T(8,128)(2,1)S(1)} copy-done((bf16[2048,896]{1,0:T(8,128)(2,1)S(1)}, bf16[2048,896]{1,0:T(8,128)(2,1)}, u32[]{:S(2)}) %copy-start.2) | copy-done | bytes 3670040
  116.9 1.5 copy-done.5
  118.4 4.2 %output_terms.1.refs_0_ = bf16[1024,1024]{1,0:T(8,128)(2,1)} custom-call(s32[5]{0:T(128)S(1)} %stack.23.pos_ref, bf16[2048,896]{1,0:T(8,128)(2,1)S(1)} %copy-done.2, bf16[896,1024]{1,0:T(8,128)(2,1)S(1)} %copy-done.5), custom_call_target="tpu_custom_call" | custom-call | flops 1879048192 | bytes 8388608 | tf_op jit(solution)/shard_map/output_terms/pallas_call | solution.py:162
  122.6 0.0 collective-permute-done.3.a_ref
  122.6 0.0 collective-permute-done.2.b_ref
  122.6 0.9 sums.1
  123.5 1.9 %collective-permute-start.6 = (bf16[128,896]{1,0:T(8,128)(2,1)}, bf16[128,896]{1,0:T(8,128)(2,1)S(1)}, u32[]{:S(2)}, u32[]{:S(2)}) collective-permute-start(bf16[128,896]{1,0:T(8,128)(2,1)} %get-tuple-element.21), channel_id=1, source_target_pairs={{0,263},{1,0},{2,1},{3,2},{4,3},{5,4},{6,5},{7,6},{8,271},{9,8},{1... | collective-permute-start | bytes 688136 | tf_op jit(solution)/shard_map/ppermute | solution.py:74
  125.4 3.9 %collective-permute-start.5 = (bf16[128,896]{1,0:T(8,128)(2,1)}, bf16[128,896]{1,0:T(8,128)(2,1)}, u32[]{:S(2)}, u32[]{:S(2)}) collective-permute-start(bf16[128,896]{1,0:T(8,128)(2,1)} %get-tuple-element.20), channel_id=1, source_target_pairs={{0,1},{1,2},{2,3},{3,4},{4,5},{5,6},{6,7},{7,256},{8,9},{9,10},{10... | collective-permute-start | bytes 688136 | tf_op jit(solution)/shard_map/ppermute | solution.py:74
  129.3 1.9 %collective-permute-start.4 = (bf16[128,896]{1,0:T(8,128)(2,1)}, bf16[128,896]{1,0:T(8,128)(2,1)}, u32[]{:S(2)}, u32[]{:S(2)}) collective-permute-start(bf16[128,896]{1,0:T(8,128)(2,1)} %get-tuple-element.19), channel_id=1, source_target_pairs={{0,2},{1,3},{2,4},{3,5},{4,6},{5,7},{6,256},{7,257},{8,10},{9,11},... | collective-permute-start | bytes 688136 | tf_op jit(solution)/shard_map/ppermute | solution.py:74
  131.3 0.0 all-to-all-done.2.rest_ref
  131.3 0.0 copy-start.7
  131.3 0.0 copy-start.9
  131.3 9.4 %all-to-all-start = ((bf16[16,64,1024]{2,1,0:T(8,128)(2,1)}), bf16[16,64,1024]{2,1,0:T(8,128)(2,1)}, u32[]{:S(2)}, u32[]{:S(2)}) async-start(bf16[16,64,1024]{2,1,0:T(8,128)(2,1)} %bitcast.5), calls=%async_computation | async-start | bytes 4194304 | tf_op jit(solution)/shard_map/all_to_all | solution.py:119
  140.8 0.0 collective-permute-done.6.refs_3_
  140.8 0.8 collective-permute-done.4.refs_1_
  141.6 2.0 %copy-done.3 = bf16[2048,896]{1,0:T(8,128)(2,1)S(1)} copy-done((bf16[2048,896]{1,0:T(8,128)(2,1)S(1)}, bf16[2048,896]{1,0:T(8,128)(2,1)}, u32[]{:S(2)}) %copy-start.3) | copy-done | bytes 3670040
  143.6 7.4 %weight_terms.1 = bf16[896,1024]{1,0:T(8,128)(2,1)} custom-call(s32[5]{0:T(128)S(1)} %stack.23.pos_ref, bf16[2048,896]{1,0:T(8,128)(2,1)S(1)} %copy-done.3, bf16[16,64,1024]{2,1,0:T(8,128)(2,1)S(1)} %all-to-all-done.1.refs_0_.near_ref, bf16[16,64,1024]{2,1,0:T(8,128)(2,1)} %all-to-all-done.2.rest_ref, bf16[1024,1024]{1,0:T(8,128)(2,1)} %output_terms.1.refs_0_, ...), custom_call_target="tpu_custom_call" | custom-call | flops 3758096384 | bytes 10485760 | tf_op jit(solution)/shard_map/weight_terms/pallas_call | solution.py:211
  151.1 1.9 %collective-permute-start.7 = (bf16[896,1024]{1,0:T(8,128)(2,1)}, bf16[896,1024]{1,0:T(8,128)(2,1)S(1)}, u32[]{:S(2)}, u32[]{:S(2)}) collective-permute-start(bf16[896,1024]{1,0:T(8,128)(2,1)} %weight_terms.1), channel_id=1, source_target_pairs={{0,128},{1,129},{2,130},{3,131},{4,132},{5,133},{6,134},{7,135},{8... | collective-permute-start | bytes 5505032 | tf_op jit(solution)/shard_map/ppermute | solution.py:74
  153.0 2.2 %fusion.7 = (bf16[128,896]{1,0:T(8,128)(2,1)}, bf16[128,896]{1,0:T(8,128)(2,1)}) fusion(bf16[128,896]{1,0:T(8,128)(2,1)S(1)} %copy-done.7, bf16[128,896]{1,0:T(8,128)(2,1)S(1)} %collective-permute-done.6.refs_3_, bf16[128,896]{1,0:T(8,128)(2,1)} %collective-permute-done.5.refs_2_, bf16[128,896]{1,0:T(8,128)(2,1)} %collective-permute-done.4.refs_1_, ...), kind=kLoop, calls=%fused_computation.11 | loop fusion | flops 2752512 | bytes 2064384 | tf_op jit(solution)/shard_map/convert_element_type | solution.py:266
  155.2 5.1 %all-to-all-done.got_ref = bf16[16,64,1024]{2,1,0:T(8,128)(2,1)} async-done(((bf16[16,64,1024]{2,1,0:T(8,128)(2,1)}), bf16[16,64,1024]{2,1,0:T(8,128)(2,1)}, u32[]{:S(2)}, u32[]{:S(2)}) %all-to-all-start) | async-done | bytes 2097184 | tf_op jit(solution)/shard_map/all_to_all | solution.py:119
  160.3 3.5 %output_sum.1 = bf16[64,1024]{1,0:T(8,128)(2,1)} custom-call(bf16[16,64,1024]{2,1,0:T(8,128)(2,1)} %all-to-all-done.got_ref), custom_call_target="tpu_custom_call" | custom-call | flops 1048576 | bytes 2097152 | tf_op jit(solution)/shard_map/output_sum/pallas_call | solution.py:181
  163.8 3.5 %add_convert_fusion = bf16[896,1024]{1,0:T(8,128)(2,1)} fusion(bf16[896,1024]{1,0:T(8,128)(2,1)S(1)} %collective-permute-done.7, bf16[896,1024]{1,0:T(8,128)(2,1)} %weight_terms.1), kind=kLoop, calls=%fused_computation | loop fusion | flops 3670016 | bytes 5505024 | tf_op jit(solution)/shard_map/convert_element_type | solution.py:225
  (20 shorter events, 0.0 us)
Async XLA Ops:
  7.2 107.7 %all-gather.2.cloned.1.call-start = ((), (), s32[]{:S(2)}) async-start(), calls=%async_computation.3 | async-start | bytes 3899392 | tf_op jit(solution)/shard_map/all_gather | solution.py:249
  7.2 0.9 copy-start.6
  8.2 0.9 copy-start.8
  10.5 19.4 %collective-permute-start = (bf16[64,1024]{1,0:T(8,128)(2,1)}, bf16[64,1024]{1,0:T(8,128)(2,1)S(1)}, u32[]{:S(2)}, u32[]{:S(2)}) collective-permute-start(bf16[64,1024]{1,0:T(8,128)(2,1)} %cot_ref.3), channel_id=1, source_target_pairs={{4,260},{5,261},{6,262},{7,263},{12,268},{13,269},{14,270},{15,271... | collective-permute-start | bytes 393224 | tf_op jit(solution)/shard_map/ppermute | solution.py:74
  29.9 0.9 copy-start.10
  32.8 7.6 %copy-start.11 = (bf16[64,1024]{1,0:T(8,128)(2,1)S(1)}, bf16[64,1024]{1,0:T(8,128)(2,1)}, u32[]{:S(2)}) copy-start(bf16[64,1024]{1,0:T(8,128)(2,1)} %cot_ref.3) | copy-start | bytes 393220
  32.8 34.7 %all-to-all-start.1 = ((bf16[16,64,1024]{2,1,0:T(8,128)(2,1)}), bf16[16,64,1024]{2,1,0:T(8,128)(2,1)S(1)}, u32[]{:S(2)}, u32[]{:S(2)}) async-start(bf16[16,64,1024]{2,1,0:T(8,128)(2,1)} %copies.2), calls=%async_computation.1 | async-start | bytes 4194304 | tf_op jit(solution)/shard_map/all_to_all | solution.py:119
  40.4 0.7 collective-permute-start.1
  68.2 1.4 copy-start
  69.6 61.7 %all-to-all-start.2 = ((bf16[16,64,1024]{2,1,0:T(8,128)(2,1)}), bf16[16,64,1024]{2,1,0:T(8,128)(2,1)}, u32[]{:S(2)}, u32[]{:S(2)}) async-start(bf16[16,64,1024]{2,1,0:T(8,128)(2,1)} %copy-done), calls=%async_computation.2 | async-start | bytes 4194304 | tf_op jit(solution)/shard_map/all_to_all | solution.py:119
  76.1 1.6 copy-start.1
  77.7 1.5 copy-start.4
  82.7 0.7 copy-start.12
  83.3 0.7 copy-start.14
  84.0 38.5 %collective-permute-start.3 = (bf16[256,896]{1,0:T(8,128)(2,1)}, bf16[256,896]{1,0:T(8,128)(2,1)S(1)}, u32[]{:S(2)}, u32[]{:S(2)}) collective-permute-start(bf16[256,896]{1,0:T(8,128)(2,1)} %get-tuple-element.15), channel_id=1, source_target_pairs={{0,2},{1,3},{2,4},{3,5},{4,6},{5,7},{6,256},{7,257},{8,10},{9,11},... | collective-permute-start | bytes 1376264 | tf_op jit(solution)/shard_map/ppermute | solution.py:74
  89.9 32.7 %collective-permute-start.2 = (bf16[256,896]{1,0:T(8,128)(2,1)}, bf16[256,896]{1,0:T(8,128)(2,1)S(1)}, u32[]{:S(2)}, u32[]{:S(2)}) collective-permute-start(bf16[256,896]{1,0:T(8,128)(2,1)} %get-tuple-element.14), channel_id=1, source_target_pairs={{0,262},{1,263},{2,0},{3,1},{4,2},{5,3},{6,4},{7,5},{8,270},{9,271... | collective-permute-start | bytes 1376264 | tf_op jit(solution)/shard_map/ppermute | solution.py:74
  114.9 2.0 %copy-start.2 = (bf16[2048,896]{1,0:T(8,128)(2,1)S(1)}, bf16[2048,896]{1,0:T(8,128)(2,1)}, u32[]{:S(2)}) copy-start(bf16[2048,896]{1,0:T(8,128)(2,1)} %all-gather.2.cloned.1.call-done.hid_ref) | copy-start | bytes 11010052
  116.9 1.5 copy-start.5
  118.4 4.2 %copy-start.13 = (bf16[128,896]{1,0:T(8,128)(2,1)S(1)}, bf16[128,896]{1,0:T(8,128)(2,1)}, u32[]{:S(2)}) copy-start(bf16[128,896]{1,0:T(8,128)(2,1)} %copy-done.12) | copy-start | bytes 688132
  123.5 17.3 %collective-permute-start.6 = (bf16[128,896]{1,0:T(8,128)(2,1)}, bf16[128,896]{1,0:T(8,128)(2,1)S(1)}, u32[]{:S(2)}, u32[]{:S(2)}) collective-permute-start(bf16[128,896]{1,0:T(8,128)(2,1)} %get-tuple-element.21), channel_id=1, source_target_pairs={{0,263},{1,0},{2,1},{3,2},{4,3},{5,4},{6,5},{7,6},{8,271},{9,8},{1... | collective-permute-start | bytes 688136 | tf_op jit(solution)/shard_map/ppermute | solution.py:74
  125.4 15.4 %collective-permute-start.5 = (bf16[128,896]{1,0:T(8,128)(2,1)}, bf16[128,896]{1,0:T(8,128)(2,1)}, u32[]{:S(2)}, u32[]{:S(2)}) collective-permute-start(bf16[128,896]{1,0:T(8,128)(2,1)} %get-tuple-element.20), channel_id=1, source_target_pairs={{0,1},{1,2},{2,3},{3,4},{4,5},{5,6},{6,7},{7,256},{8,9},{9,10},{10... | collective-permute-start | bytes 688136 | tf_op jit(solution)/shard_map/ppermute | solution.py:74
  129.3 12.2 %collective-permute-start.4 = (bf16[128,896]{1,0:T(8,128)(2,1)}, bf16[128,896]{1,0:T(8,128)(2,1)}, u32[]{:S(2)}, u32[]{:S(2)}) collective-permute-start(bf16[128,896]{1,0:T(8,128)(2,1)} %get-tuple-element.19), channel_id=1, source_target_pairs={{0,2},{1,3},{2,4},{3,5},{4,6},{5,7},{6,256},{7,257},{8,10},{9,11},... | collective-permute-start | bytes 688136 | tf_op jit(solution)/shard_map/ppermute | solution.py:74
  131.3 21.7 %copy-start.7 = (bf16[128,896]{1,0:T(8,128)(2,1)S(1)}, bf16[128,896]{1,0:T(8,128)(2,1)}, u32[]{:S(2)}) copy-start(bf16[128,896]{1,0:T(8,128)(2,1)} %gate_ref.1) | copy-start | bytes 688132
  131.3 21.7 %copy-start.9 = (bf16[128,896]{1,0:T(8,128)(2,1)S(1)}, bf16[128,896]{1,0:T(8,128)(2,1)}, u32[]{:S(2)}) copy-start(bf16[128,896]{1,0:T(8,128)(2,1)} %up_ref.1) | copy-start | bytes 688132
  131.3 21.7 %copy-start.15 = (bf16[128,896]{1,0:T(8,128)(2,1)S(1)}, bf16[128,896]{1,0:T(8,128)(2,1)}, u32[]{:S(2)}) copy-start(bf16[128,896]{1,0:T(8,128)(2,1)} %copy-done.14) | copy-start | bytes 688132
  131.3 29.0 %all-to-all-start = ((bf16[16,64,1024]{2,1,0:T(8,128)(2,1)}), bf16[16,64,1024]{2,1,0:T(8,128)(2,1)}, u32[]{:S(2)}, u32[]{:S(2)}) async-start(bf16[16,64,1024]{2,1,0:T(8,128)(2,1)} %bitcast.5), calls=%async_computation | async-start | bytes 4194304 | tf_op jit(solution)/shard_map/all_to_all | solution.py:119
  141.6 2.0 %copy-start.3 = (bf16[2048,896]{1,0:T(8,128)(2,1)S(1)}, bf16[2048,896]{1,0:T(8,128)(2,1)}, u32[]{:S(2)}) copy-start(bf16[2048,896]{1,0:T(8,128)(2,1)} %all-gather.2.cloned.1.call-done.hid_ref) | copy-start | bytes 11010052
  151.1 12.7 %collective-permute-start.7 = (bf16[896,1024]{1,0:T(8,128)(2,1)}, bf16[896,1024]{1,0:T(8,128)(2,1)S(1)}, u32[]{:S(2)}, u32[]{:S(2)}) collective-permute-start(bf16[896,1024]{1,0:T(8,128)(2,1)} %weight_terms.1), channel_id=1, source_target_pairs={{0,128},{1,129},{2,130},{3,131},{4,132},{5,133},{6,134},{7,135},{8... | collective-permute-start | bytes 5505032 | tf_op jit(solution)/shard_map/ppermute | solution.py:74
Sparse Core Ops, SparseCore 0:
  10.7 104.1 all-gather.1

commit v3 on v2

--- a/solution.py
+++ b/solution.py
@@ -221,8 +221,43 @@
     )(pos, hid, near, rest, *after)
 
 
-def add(a, b):
-    return (a.astype(F32) + b.astype(F32)).astype(BF)
+def pair_kernel(a_ref, b_ref, *refs):
+    refs[-1][...] = (a_ref[...].astype(F32) + b_ref[...].astype(F32)).astype(BF)
+
+
+def pair_of(a, b, *after):
+    block = pl.BlockSpec((224, 1024), lambda i: (i, 0))
+    return pl.pallas_call(
+        pair_kernel,
+        grid=(4,),
+        out_shape=jax.ShapeDtypeStruct((896, 1024), BF),
+        in_specs=[block] * 2 + [ANY] * len(after),
+        out_specs=block,
+        compiler_params=PARAMS,
+        cost_estimate=cost(2**20, 5),
+        name="weight_sum",
+    )(a, b, *after)
+
+
+def ends_kernel(gate_ref, up_ref, here_ref, b_ref, c_ref, d_ref, e_ref, *refs):
+    grad = here_ref[...].astype(F32) + b_ref[128:].astype(F32) + c_ref[...].astype(F32)
+    grad = grad + (d_ref[...].astype(F32) + e_ref[...].astype(F32))
+    g, u = gate_ref[...].astype(F32), up_ref[...].astype(F32)
+    sig = jax.nn.sigmoid(g)
+    refs[-2][...] = (grad * u * sig * (1.0 + g * (1.0 - sig))).astype(BF)
+    refs[-1][...] = (grad * (g * sig)).astype(BF)
+
+
+def ends_of(gate, up, here, b, c, d, e, *after):
+    return pl.pallas_call(
+        ends_kernel,
+        out_shape=[jax.ShapeDtypeStruct((128, 896), BF)] * 2,
+        in_specs=[VMEM] * 7 + [ANY] * len(after),
+        out_specs=[VMEM] * 2,
+        compiler_params=PARAMS,
+        cost_estimate=cost(2**21, 2),
+        name="gradients",
+    )(gate, up, here, b, c, d, e, *after)
 
 
 def sum_kernel(a_ref, b_ref, p2_ref, p1_ref, m1_ref, *refs):
@@ -255,20 +290,13 @@
     right, left, right2, left2 = ring_move(1), ring_move(-1), ring_move(2), ring_move(-2)
     a, b = send(p43, right2), send(m32, left2)
     o = out_of(pos, hid, w)
-    c, d, e = sums_of(a, b, p2, p1, m1, o)
+    c, d, e = sums_of(a, b, p2, p1, m1)
     c, d, e = send(c, right2), send(d, right), send(e, left)
-    grad_hidden = (
-        here.astype(F32) + b[128:].astype(F32) + c.astype(F32) + (d.astype(F32) + e.astype(F32))
-    )
-    gate_f, up_f = gate.astype(F32), up.astype(F32)
-    sig = jax.nn.sigmoid(gate_f)
-    grad_gate = (grad_hidden * up_f * sig * (1.0 + gate_f * (1.0 - sig))).astype(BF)
-    grad_up = (grad_hidden * (gate_f * sig)).astype(BF)
-
     output = total_of(exchange(o.reshape(16, 64, 1024)))
-
-    part = grad_of(pos, hid, near, rest, o, c, d, e)
-    grad_weight = add(part, send(part, SWAP_CORE))
+    grad_gate, grad_up = ends_of(gate, up, here, b, c, d, e, output)
+
+    part = grad_of(pos, hid, near, rest, o, a, b)
+    grad_weight = pair_of(part, send(part, SWAP_CORE), output)
     return output, grad_gate, grad_up, grad_weight
 
 

time: 175 us -> 173 us (0.989)
  other arithmetic: 5.73 us -> 0 us
  waiting for transfers between devices: 56.8 us -> 51.1 us
  local copies, waits for them, and re-layouts: 14.3 us -> 18.1 us
  Pallas kernels: 23.6 us -> 27.3 us
    convert_element_type x2 -> x0, other arithmetic: 5.73 us -> none  [the longest x1 3.55 us: add(): return (a.astype(F32) + b.astype(F32)).astype(BF)]
    all_to_all x3, waiting for transfers between devices: 31.5 us -> 26.4 us  [exchange(): return lax.all_to_all(blocks, PLANE, 0, 0, tiled=True)]
    pallas_call x0 -> x2, Pallas kernels: none -> 4.96 us  [the longest x1 3.89 us: pair_of(): pl.pallas_call(pair_kernel, grid=(4,), out_shape=jax.ShapeDtypeStruct((89...]
    unnamed x32 -> x38, local copies, waits for them, and re-layouts: 14.2 us -> 18 us
  transfers between devices with their start and end apart: 12 -> 12, of which waited for: 5 -> 4; matrix products, arithmetic and copies ran while one was open for 1% -> 0% of each run, Pallas kernels for 13% -> 14%
where the time goes in v3:
time: 173 us; the launch traced here: 172 us
  starting transfers between devices  61.2 us (35%)
  waiting for transfers between devices  51.1 us (30%)
  Pallas kernels  27.3 us (16%)
  local copies, waits for them, and re-layouts  18.1 us (10%)
  between operations  14.2 us (8%)
    ppermute x8, starting transfers between devices, send(): return lax.ppermute(a, AXES, perm)  37.2 us
    all_to_all x3, waiting for transfers between devices, exchange(): return lax.all_to_all(blocks, PLANE, 0, 0, tiled=True)  26.4 us
    all_to_all x3, starting transfers between devices, exchange(): return lax.all_to_all(blocks, PLANE, 0, 0, tiled=True)  24 us
    all_gather x1, waiting for transfers between devices, per_device(): hid = lax.all_gather(hidden_of(gate, up), RING, axis=0, tiled=True)  20.5 us
    unnamed x38, local copies, waits for them, and re-layouts  18 us
    pallas_call x1, Pallas kernels, grad_of(): pl.pallas_call(grad_kernel, grid=(4,), out_shape=jax.ShapeDtypeStruct((89...  7.53 us
    ppermute x8, waiting for transfers between devices, send(): return lax.ppermute(a, AXES, perm)  4.25 us
    pallas_call x1, Pallas kernels, pair_of(): pl.pallas_call(pair_kernel, grid=(4,), out_shape=jax.ShapeDtypeStruct((89...  3.89 us
  transfers between devices with their start and end apart: 12, of which 4 were waited for; matrix products, arithmetic and copies ran while one was open for 0% of the time, Pallas kernels for 14%

profile of v3, /device:TPU:6, one launch (start us, length us, event | category | flops | bytes accessed | tf_op | source)
XLA Modules:
  0.0 172.1 jit_solution(10343213829813112087)
XLA Ops:
  7.2 0.0 all-gather.2.cloned.1.call-start
  7.2 0.0 copy-start.9
  7.2 0.9 copy-done.9
  8.2 0.9 copy-done.11
  9.1 1.4 hidden.1
  10.4 0.0 all-gather.2.cloned.1.call-update
  10.5 15.7 %collective-permute-start = (bf16[64,1024]{1,0:T(8,128)(2,1)}, bf16[64,1024]{1,0:T(8,128)(2,1)S(1)}, u32[]{:S(2)}, u32[]{:S(2)}) collective-permute-start(bf16[64,1024]{1,0:T(8,128)(2,1)} %cot_ref.3), channel_id=1, source_target_pairs={{4,260},{5,261},{6,262},{7,263},{12,268},{13,269},{14,270},{15,271... | collective-permute-start | bytes 393224 | tf_op jit(solution)/shard_map/ppermute | solution.py:74
  26.2 0.1 stack.23.pos_ref
  26.3 3.6 %collective-permute-done.far_ref = bf16[64,1024]{1,0:T(8,128)(2,1)S(1)} collective-permute-done((bf16[64,1024]{1,0:T(8,128)(2,1)}, bf16[64,1024]{1,0:T(8,128)(2,1)S(1)}, u32[]{:S(2)}, u32[]{:S(2)}) %collective-permute-start) | collective-permute-done | bytes 131104 | tf_op jit(solution)/shard_map/ppermute | solution.py:74
  29.9 0.9 copy-done.13
  30.8 2.0 %copies.2 = bf16[16,64,1024]{2,1,0:T(8,128)(2,1)} custom-call(s32[5]{0:T(128)S(1)} %stack.23.pos_ref, bf16[64,1024]{1,0:T(8,128)(2,1)S(1)} %copy-done.13, bf16[64,1024]{1,0:T(8,128)(2,1)S(1)} %collective-permute-done.far_ref), custom_call_target="tpu_custom_call" | custom-call | bytes 2097152 | tf_op jit(solution)/shard_map/copies/pallas_call | solution.py:107
  32.8 7.6 %all-to-all-start.1 = ((bf16[16,64,1024]{2,1,0:T(8,128)(2,1)}), bf16[16,64,1024]{2,1,0:T(8,128)(2,1)S(1)}, u32[]{:S(2)}, u32[]{:S(2)}) async-start(bf16[16,64,1024]{2,1,0:T(8,128)(2,1)} %copies.2), calls=%async_computation.1 | async-start | bytes 4194304 | tf_op jit(solution)/shard_map/all_to_all | solution.py:119
  40.4 0.7 collective-permute-start.1
  41.1 0.0 collective-permute-done.1.far_ref
  41.1 26.4 %all-to-all-done.1.refs_0_.near_ref = bf16[16,64,1024]{2,1,0:T(8,128)(2,1)S(1)} async-done(((bf16[16,64,1024]{2,1,0:T(8,128)(2,1)}), bf16[16,64,1024]{2,1,0:T(8,128)(2,1)S(1)}, u32[]{:S(2)}, u32[]{:S(2)}) %all-to-all-start.1) | async-done | bytes 2097184 | tf_op jit(solution)/shard_map/all_to_all | solution.py:119
  67.5 0.7 copies.3.refs_0_
  68.2 1.3 copy-done
  69.5 6.5 %all-to-all-start.2 = ((bf16[16,64,1024]{2,1,0:T(8,128)(2,1)}), bf16[16,64,1024]{2,1,0:T(8,128)(2,1)}, u32[]{:S(2)}, u32[]{:S(2)}) async-start(bf16[16,64,1024]{2,1,0:T(8,128)(2,1)} %copy-done), calls=%async_computation.2 | async-start | bytes 4194304 | tf_op jit(solution)/shard_map/all_to_all | solution.py:119
  76.0 1.6 copy-done.1
  77.7 1.5 copy-done.6
  79.2 3.5 %hidden_terms.1 = (bf16[256,896]{1,0:T(8,128)(2,1)}, bf16[256,896]{1,0:T(8,128)(2,1)}, bf16[128,896]{1,0:T(8,128)(2,1)S(1)}, bf16[128,896]{1,0:T(8,128)(2,1)S(1)...) custom-call(s32[5]{0:T(128)S(1)} %stack.23.pos_ref, bf16[8,128,1024]{2,1,0:T(8,128)(2,1)S(1)} %bitcast.7, ...), custom_call_target="tpu_custom_call" | custom-call | flops 1879048192 | bytes 8388608 | tf_op jit(solution)/shard_map/hidden_terms/pallas_call | solution.py:143
  82.6 0.7 copy-done.15
  83.3 0.7 copy-done.17
  84.0 8.0 %collective-permute-start.2 = (bf16[256,896]{1,0:T(8,128)(2,1)}, bf16[256,896]{1,0:T(8,128)(2,1)S(1)}, u32[]{:S(2)}, u32[]{:S(2)}) collective-permute-start(bf16[256,896]{1,0:T(8,128)(2,1)} %get-tuple-element.16), channel_id=1, source_target_pairs={{0,262},{1,263},{2,0},{3,1},{4,2},{5,3},{6,4},{7,5},{8,270},{9,271... | collective-permute-start | bytes 1376264 | tf_op jit(solution)/shard_map/ppermute | solution.py:74
  92.1 1.9 %collective-permute-start.3 = (bf16[256,896]{1,0:T(8,128)(2,1)}, bf16[256,896]{1,0:T(8,128)(2,1)S(1)}, u32[]{:S(2)}, u32[]{:S(2)}) collective-permute-start(bf16[256,896]{1,0:T(8,128)(2,1)} %get-tuple-element.17), channel_id=1, source_target_pairs={{0,2},{1,3},{2,4},{3,5},{4,6},{5,7},{6,256},{7,257},{8,10},{9,11},... | collective-permute-start | bytes 1376264 | tf_op jit(solution)/shard_map/ppermute | solution.py:74
  94.0 20.5 %all-gather.2.cloned.1.call-done.hid_ref = bf16[2048,896]{1,0:T(8,128)(2,1)} async-done(((bf16[128,896]{1,0:T(8,128)(2,1)}), bf16[2048,896]{1,0:T(8,128)(2,1)}) %all-gather.2.cloned.1.call-update) | async-done | bytes 3670032 | tf_op jit(solution)/shard_map/all_gather | solution.py:284
  114.5 2.0 %copy-done.4 = bf16[2048,896]{1,0:T(8,128)(2,1)S(1)} copy-done((bf16[2048,896]{1,0:T(8,128)(2,1)S(1)}, bf16[2048,896]{1,0:T(8,128)(2,1)}, u32[]{:S(2)}) %copy-start.4) | copy-done | bytes 3670040
  116.5 1.5 copy-done.7
  118.0 2.9 %output_terms.1.refs_0_ = bf16[1024,1024]{1,0:T(8,128)(2,1)S(1)} custom-call(s32[5]{0:T(128)S(1)} %stack.23.pos_ref, bf16[2048,896]{1,0:T(8,128)(2,1)S(1)} %copy-done.4, bf16[896,1024]{1,0:T(8,128)(2,1)S(1)} %copy-done.7), custom_call_target="tpu_custom_call" | custom-call | flops 1879048192 | bytes 8388608 | tf_op jit(solution)/shard_map/output_terms/pallas_call | solution.py:162
  120.9 1.3 copy-done.2
  122.2 0.0 all-to-all-done.2.rest_ref
  122.2 10.0 %all-to-all-start = ((bf16[16,64,1024]{2,1,0:T(8,128)(2,1)}), bf16[16,64,1024]{2,1,0:T(8,128)(2,1)}, u32[]{:S(2)}, u32[]{:S(2)}) async-start(bf16[16,64,1024]{2,1,0:T(8,128)(2,1)} %bitcast.8), calls=%async_computation | async-start | bytes 4194304 | tf_op jit(solution)/shard_map/all_to_all | solution.py:119
  132.1 0.0 collective-permute-done.2.b_ref.refs_2_
  132.2 1.6 copy-done.3
  133.8 2.0 %copy-done.5 = bf16[2048,896]{1,0:T(8,128)(2,1)S(1)} copy-done((bf16[2048,896]{1,0:T(8,128)(2,1)S(1)}, bf16[2048,896]{1,0:T(8,128)(2,1)}, u32[]{:S(2)}) %copy-start.5) | copy-done | bytes 3670040
  135.8 7.5 %weight_terms.1.a_ref = bf16[896,1024]{1,0:T(8,128)(2,1)} custom-call(s32[5]{0:T(128)S(1)} %stack.23.pos_ref, bf16[2048,896]{1,0:T(8,128)(2,1)S(1)} %copy-done.5, bf16[16,64,1024]{2,1,0:T(8,128)(2,1)S(1)} %all-to-all-done.1.refs_0_.near_ref, bf16[16,64,1024]{2,1,0:T(8,128)(2,1)} %all-to-all-done.2.rest_ref, bf16[1024,1024]{1,0:T(8,128)(2,1)S(1)} %copy-done.3, ...), custom_call_target="tpu_custom_call" | custom-call | flops 3758096384 | bytes 10485760 | tf_op jit(solution)/shard_map/weight_terms/pallas_call | solution.py:211
  143.3 1.9 %collective-permute-start.7 = (bf16[896,1024]{1,0:T(8,128)(2,1)}, bf16[896,1024]{1,0:T(8,128)(2,1)S(1)}, u32[]{:S(2)}, u32[]{:S(2)}) collective-permute-start(bf16[896,1024]{1,0:T(8,128)(2,1)} %weight_terms.1.a_ref), channel_id=1, source_target_pairs={{0,128},{1,129},{2,130},{3,131},{4,132},{5,133},{6,134},{7,135},{8... | collective-permute-start | bytes 5505032 | tf_op jit(solution)/shard_map/ppermute | solution.py:74
  145.3 0.9 sums.1
  146.2 1.9 %collective-permute-start.4 = (bf16[128,896]{1,0:T(8,128)(2,1)}, bf16[128,896]{1,0:T(8,128)(2,1)S(1)}, u32[]{:S(2)}, u32[]{:S(2)}) collective-permute-start(bf16[128,896]{1,0:T(8,128)(2,1)} %get-tuple-element.21), channel_id=1, source_target_pairs={{0,2},{1,3},{2,4},{3,5},{4,6},{5,7},{6,256},{7,257},{8,10},{9,11},... | collective-permute-start | bytes 688136 | tf_op jit(solution)/shard_map/ppermute | solution.py:74
  148.1 1.9 %collective-permute-start.5 = (bf16[128,896]{1,0:T(8,128)(2,1)}, bf16[128,896]{1,0:T(8,128)(2,1)S(1)}, u32[]{:S(2)}, u32[]{:S(2)}) collective-permute-start(bf16[128,896]{1,0:T(8,128)(2,1)} %get-tuple-element.22), channel_id=1, source_target_pairs={{0,1},{1,2},{2,3},{3,4},{4,5},{5,6},{6,7},{7,256},{8,9},{9,10},{10... | collective-permute-start | bytes 688136 | tf_op jit(solution)/shard_map/ppermute | solution.py:74
  150.0 5.1 %collective-permute-start.6 = (bf16[128,896]{1,0:T(8,128)(2,1)}, bf16[128,896]{1,0:T(8,128)(2,1)S(1)}, u32[]{:S(2)}, u32[]{:S(2)}) collective-permute-start(bf16[128,896]{1,0:T(8,128)(2,1)} %get-tuple-element.23), channel_id=1, source_target_pairs={{0,263},{1,0},{2,1},{3,2},{4,3},{5,4},{6,5},{7,6},{8,271},{9,8},{1... | collective-permute-start | bytes 688136 | tf_op jit(solution)/shard_map/ppermute | solution.py:74
  155.2 0.0 all-to-all-done.got_ref
  155.2 3.5 %output_sum.1.refs_0_ = bf16[64,1024]{1,0:T(8,128)(2,1)} custom-call(bf16[16,64,1024]{2,1,0:T(8,128)(2,1)} %all-to-all-done.got_ref), custom_call_target="tpu_custom_call" | custom-call | flops 1048576 | bytes 2097152 | tf_op jit(solution)/shard_map/output_sum/pallas_call | solution.py:181
  158.7 0.9 copy-done.8
  159.6 3.9 %weight_sum.1 = bf16[896,1024]{1,0:T(8,128)(2,1)} custom-call(bf16[896,1024]{1,0:T(8,128)(2,1)} %weight_terms.1.a_ref, bf16[896,1024]{1,0:T(8,128)(2,1)S(1)} %collective-permute-done.7.b_ref, bf16[64,1024]{1,0:T(8,128)(2,1)S(1)} %copy-done.8), custom_call_target="tpu_custom_call" | custom-call | flops 1048576 | bytes 5242880 | tf_op jit(solution)/shard_map/weight_sum/pallas_call | solution.py:230
  163.5 0.0 collective-permute-done.4.c_ref
  163.5 0.6 collective-permute-done.5.d_ref
  164.1 1.1 gradients.1
  (26 shorter events, 0.0 us)
Async XLA Ops:
  7.2 107.3 %all-gather.2.cloned.1.call-start = ((), (), s32[]{:S(2)}) async-start(), calls=%async_computation.3 | async-start | bytes 3899392 | tf_op jit(solution)/shard_map/all_gather | solution.py:284
  7.2 0.9 copy-start.9
  8.2 0.9 copy-start.11
  10.5 19.4 %collective-permute-start = (bf16[64,1024]{1,0:T(8,128)(2,1)}, bf16[64,1024]{1,0:T(8,128)(2,1)S(1)}, u32[]{:S(2)}, u32[]{:S(2)}) collective-permute-start(bf16[64,1024]{1,0:T(8,128)(2,1)} %cot_ref.3), channel_id=1, source_target_pairs={{4,260},{5,261},{6,262},{7,263},{12,268},{13,269},{14,270},{15,271... | collective-permute-start | bytes 393224 | tf_op jit(solution)/shard_map/ppermute | solution.py:74
  29.9 0.9 copy-start.13
  32.8 7.6 %copy-start.14 = (bf16[64,1024]{1,0:T(8,128)(2,1)S(1)}, bf16[64,1024]{1,0:T(8,128)(2,1)}, u32[]{:S(2)}) copy-start(bf16[64,1024]{1,0:T(8,128)(2,1)} %cot_ref.3) | copy-start | bytes 393220
  32.8 34.7 %all-to-all-start.1 = ((bf16[16,64,1024]{2,1,0:T(8,128)(2,1)}), bf16[16,64,1024]{2,1,0:T(8,128)(2,1)S(1)}, u32[]{:S(2)}, u32[]{:S(2)}) async-start(bf16[16,64,1024]{2,1,0:T(8,128)(2,1)} %copies.2), calls=%async_computation.1 | async-start | bytes 4194304 | tf_op jit(solution)/shard_map/all_to_all | solution.py:119
  40.4 0.7 collective-permute-start.1
  68.2 1.3 copy-start
  69.5 52.6 %all-to-all-start.2 = ((bf16[16,64,1024]{2,1,0:T(8,128)(2,1)}), bf16[16,64,1024]{2,1,0:T(8,128)(2,1)}, u32[]{:S(2)}, u32[]{:S(2)}) async-start(bf16[16,64,1024]{2,1,0:T(8,128)(2,1)} %copy-done), calls=%async_computation.2 | async-start | bytes 4194304 | tf_op jit(solution)/shard_map/all_to_all | solution.py:119
  76.0 1.6 copy-start.1
  77.7 1.5 copy-start.6
  82.6 0.7 copy-start.15
  83.3 0.7 copy-start.17
  84.0 48.1 %collective-permute-start.2 = (bf16[256,896]{1,0:T(8,128)(2,1)}, bf16[256,896]{1,0:T(8,128)(2,1)S(1)}, u32[]{:S(2)}, u32[]{:S(2)}) collective-permute-start(bf16[256,896]{1,0:T(8,128)(2,1)} %get-tuple-element.16), channel_id=1, source_target_pairs={{0,262},{1,263},{2,0},{3,1},{4,2},{5,3},{6,4},{7,5},{8,270},{9,271... | collective-permute-start | bytes 1376264 | tf_op jit(solution)/shard_map/ppermute | solution.py:74
  92.1 40.1 %collective-permute-start.3 = (bf16[256,896]{1,0:T(8,128)(2,1)}, bf16[256,896]{1,0:T(8,128)(2,1)S(1)}, u32[]{:S(2)}, u32[]{:S(2)}) collective-permute-start(bf16[256,896]{1,0:T(8,128)(2,1)} %get-tuple-element.17), channel_id=1, source_target_pairs={{0,2},{1,3},{2,4},{3,5},{4,6},{5,7},{6,256},{7,257},{8,10},{9,11},... | collective-permute-start | bytes 1376264 | tf_op jit(solution)/shard_map/ppermute | solution.py:74
  114.5 2.0 %copy-start.4 = (bf16[2048,896]{1,0:T(8,128)(2,1)S(1)}, bf16[2048,896]{1,0:T(8,128)(2,1)}, u32[]{:S(2)}) copy-start(bf16[2048,896]{1,0:T(8,128)(2,1)} %all-gather.2.cloned.1.call-done.hid_ref) | copy-start | bytes 11010052
  116.5 1.5 copy-start.7
  120.9 1.3 copy-start.2
  122.2 33.0 %all-to-all-start = ((bf16[16,64,1024]{2,1,0:T(8,128)(2,1)}), bf16[16,64,1024]{2,1,0:T(8,128)(2,1)}, u32[]{:S(2)}, u32[]{:S(2)}) async-start(bf16[16,64,1024]{2,1,0:T(8,128)(2,1)} %bitcast.8), calls=%async_computation | async-start | bytes 4194304 | tf_op jit(solution)/shard_map/all_to_all | solution.py:119
  132.2 1.6 copy-start.3
  133.8 2.0 %copy-start.5 = (bf16[2048,896]{1,0:T(8,128)(2,1)S(1)}, bf16[2048,896]{1,0:T(8,128)(2,1)}, u32[]{:S(2)}) copy-start(bf16[2048,896]{1,0:T(8,128)(2,1)} %all-gather.2.cloned.1.call-done.hid_ref) | copy-start | bytes 11010052
  135.8 9.5 %copy-start.16 = (bf16[128,896]{1,0:T(8,128)(2,1)S(1)}, bf16[128,896]{1,0:T(8,128)(2,1)}, u32[]{:S(2)}) copy-start(bf16[128,896]{1,0:T(8,128)(2,1)} %copy-done.15) | copy-start | bytes 688132
  143.3 15.3 %collective-permute-start.7 = (bf16[896,1024]{1,0:T(8,128)(2,1)}, bf16[896,1024]{1,0:T(8,128)(2,1)S(1)}, u32[]{:S(2)}, u32[]{:S(2)}) collective-permute-start(bf16[896,1024]{1,0:T(8,128)(2,1)} %weight_terms.1.a_ref), channel_id=1, source_target_pairs={{0,128},{1,129},{2,130},{3,131},{4,132},{5,133},{6,134},{7,135},{8... | collective-permute-start | bytes 5505032 | tf_op jit(solution)/shard_map/ppermute | solution.py:74
  146.2 17.3 %collective-permute-start.4 = (bf16[128,896]{1,0:T(8,128)(2,1)}, bf16[128,896]{1,0:T(8,128)(2,1)S(1)}, u32[]{:S(2)}, u32[]{:S(2)}) collective-permute-start(bf16[128,896]{1,0:T(8,128)(2,1)} %get-tuple-element.21), channel_id=1, source_target_pairs={{0,2},{1,3},{2,4},{3,5},{4,6},{5,7},{6,256},{7,257},{8,10},{9,11},... | collective-permute-start | bytes 688136 | tf_op jit(solution)/shard_map/ppermute | solution.py:74
  148.1 16.0 %collective-permute-start.5 = (bf16[128,896]{1,0:T(8,128)(2,1)}, bf16[128,896]{1,0:T(8,128)(2,1)S(1)}, u32[]{:S(2)}, u32[]{:S(2)}) collective-permute-start(bf16[128,896]{1,0:T(8,128)(2,1)} %get-tuple-element.22), channel_id=1, source_target_pairs={{0,1},{1,2},{2,3},{3,4},{4,5},{5,6},{6,7},{7,256},{8,9},{9,10},{10... | collective-permute-start | bytes 688136 | tf_op jit(solution)/shard_map/ppermute | solution.py:74
  150.0 14.1 %collective-permute-start.6 = (bf16[128,896]{1,0:T(8,128)(2,1)}, bf16[128,896]{1,0:T(8,128)(2,1)S(1)}, u32[]{:S(2)}, u32[]{:S(2)}) collective-permute-start(bf16[128,896]{1,0:T(8,128)(2,1)} %get-tuple-element.23), channel_id=1, source_target_pairs={{0,263},{1,0},{2,1},{3,2},{4,3},{5,4},{6,5},{7,6},{8,271},{9,8},{1... | collective-permute-start | bytes 688136 | tf_op jit(solution)/shard_map/ppermute | solution.py:74
  158.7 0.9 copy-start.8
  159.6 4.5 %copy-start.10 = (bf16[128,896]{1,0:T(8,128)(2,1)S(1)}, bf16[128,896]{1,0:T(8,128)(2,1)}, u32[]{:S(2)}) copy-start(bf16[128,896]{1,0:T(8,128)(2,1)} %gate_ref.3) | copy-start | bytes 688132
  159.6 4.5 %copy-start.12 = (bf16[128,896]{1,0:T(8,128)(2,1)S(1)}, bf16[128,896]{1,0:T(8,128)(2,1)}, u32[]{:S(2)}) copy-start(bf16[128,896]{1,0:T(8,128)(2,1)} %up_ref.3) | copy-start | bytes 688132
  159.6 4.5 %copy-start.18 = (bf16[128,896]{1,0:T(8,128)(2,1)S(1)}, bf16[128,896]{1,0:T(8,128)(2,1)}, u32[]{:S(2)}) copy-start(bf16[128,896]{1,0:T(8,128)(2,1)} %copy-done.17) | copy-start | bytes 688132
Sparse Core Ops, SparseCore 0:
  10.7 103.7 all-gather.1

commit v4 on v3

--- a/solution.py
+++ b/solution.py
@@ -119,34 +119,27 @@
     return lax.all_to_all(blocks, PLANE, 0, 0, tiled=True)
 
 
-def term_kernel(pos_ref, near_ref, w_ref, *refs):
-    p43, m32, p2, p1, m1, here = refs[-6:]
-    col = pos_ref[4]
-
-    def dot(k, l):
-        a = jnp.concatenate([near_ref[(col + k + 8) % 8], near_ref[(col + l + 8) % 8]], axis=0)
-        return lax.dot_general(
-            a, w_ref[...], (((1,), (1,)), ((), ())), preferred_element_type=F32
+def term_kernel(parts, pos_ref, near_ref, w_ref, *refs):
+    outs = refs[len(refs) - len(parts) :]
+    for part, out in zip(parts, outs):
+        rows = [near_ref[(pos_ref[4] + k + 8) % 8] for k in part]
+        out[...] = lax.dot_general(
+            rows[0] if len(rows) == 1 else jnp.concatenate(rows, axis=0),
+            w_ref[...],
+            (((1,), (1,)), ((), ())),
+            preferred_element_type=F32,
         ).astype(BF)
 
-    p43[...] = dot(4, 3)
-    m32[...] = dot(-3, -2)
-    r = dot(2, 1)
-    p2[...] = r[:128]
-    p1[...] = r[128:]
-    r = dot(-1, 0)
-    m1[...] = r[:128]
-    here[...] = r[128:]
-
-
-def terms_of(pos, near, w, *after):
-    return pl.pallas_call(
-        term_kernel,
-        out_shape=[jax.ShapeDtypeStruct((n, 896), BF) for n in (256, 256, 128, 128, 128, 128)],
+
+def terms_of(parts, pos, near, w, *after):
+    n = sum(len(p) for p in parts)
+    return pl.pallas_call(
+        functools.partial(term_kernel, parts),
+        out_shape=[jax.ShapeDtypeStruct((128 * len(p), 896), BF) for p in parts],
         in_specs=[SMEM, VMEM, VMEM] + [ANY] * len(after),
-        out_specs=[VMEM] * 6,
-        compiler_params=PARAMS,
-        cost_estimate=cost(2 * 1024 * 896 * 1024, 8),
+        out_specs=[VMEM] * len(parts),
+        compiler_params=PARAMS,
+        cost_estimate=cost(2 * 128 * n * 896 * 1024, 4),
         name="hidden_terms",
     )(pos, near.reshape(8, 128, 1024), w, *after)
 
@@ -260,23 +253,21 @@
     )(gate, up, here, b, c, d, e, *after)
 
 
-def sum_kernel(a_ref, b_ref, p2_ref, p1_ref, m1_ref, *refs):
-    c, d, e = refs[-3:]
-    c[...] = (a_ref[:128].astype(F32) + p2_ref[...].astype(F32)).astype(BF)
-    d[...] = (a_ref[128:].astype(F32) + p1_ref[...].astype(F32)).astype(BF)
-    e[...] = (b_ref[:128].astype(F32) + m1_ref[...].astype(F32)).astype(BF)
-
-
-def sums_of(a, b, p2, p1, m1, *after):
+def sum_kernel(a_ref, p_ref, q_ref, c_ref, d_ref):
+    c_ref[...] = (a_ref[:128].astype(F32) + p_ref[...].astype(F32)).astype(BF)
+    d_ref[...] = (a_ref[128:].astype(F32) + q_ref[...].astype(F32)).astype(BF)
+
+
+def sums_of(a, p, q):
     return pl.pallas_call(
         sum_kernel,
-        out_shape=[jax.ShapeDtypeStruct((128, 896), BF)] * 3,
-        in_specs=[VMEM] * 5 + [ANY] * len(after),
-        out_specs=[VMEM] * 3,
+        out_shape=[jax.ShapeDtypeStruct((128, 896), BF)] * 2,
+        in_specs=[VMEM] * 3,
+        out_specs=[VMEM] * 2,
         compiler_params=PARAMS,
         cost_estimate=cost(2**18, 1),
         name="sums",
-    )(a, b, p2, p1, m1, *after)
+    )(a, p, q)
 
 
 def per_device(gate, up, w, cot):
@@ -284,18 +275,21 @@
     hid = lax.all_gather(hidden_of(gate, up), RING, axis=0, tiled=True)
     near = exchange(copies_of(pos, cot, False))
     rest = copies_of(pos, cot, True, near)
-    p43, m32, p2, p1, m1, here = terms_of(pos, near, w, rest)
+    p43, p2, p1, here = terms_of(((4, 3), (2,), (1,), (0,)), pos, near, w, rest)
     rest = exchange(rest)
 
     right, left, right2, left2 = ring_move(1), ring_move(-1), ring_move(2), ring_move(-2)
-    a, b = send(p43, right2), send(m32, left2)
+    a = send(p43, right2)
     o = out_of(pos, hid, w)
-    c, d, e = sums_of(a, b, p2, p1, m1)
+    m32, m1 = terms_of(((-3, -2), (-1,)), pos, near, w, o)
+    b = send(m32, left2)
+    c, d = sums_of(a, p2, p1)
+    e = (b[:128].astype(F32) + m1.astype(F32)).astype(BF)
     c, d, e = send(c, right2), send(d, right), send(e, left)
     output = total_of(exchange(o.reshape(16, 64, 1024)))
     grad_gate, grad_up = ends_of(gate, up, here, b, c, d, e, output)
 
-    part = grad_of(pos, hid, near, rest, o, a, b)
+    part = grad_of(pos, hid, near, rest, o, c, d)
     grad_weight = pair_of(part, send(part, SWAP_CORE), output)
     return output, grad_gate, grad_up, grad_weight
 

time: 173 us -> 198 us (1.14)
  waiting for transfers between devices: 51.1 us -> 73.6 us
  starting transfers between devices: 61.2 us -> 64.6 us
    ppermute x8, waiting for transfers between devices: 4.25 us -> 47.1 us  [send(): return lax.ppermute(a, AXES, perm)]
    all_gather x1, waiting for transfers between devices: 20.5 us -> 0.02 us  [per_device(): hid = lax.all_gather(hidden_of(gate, up), RING, axis=0, tiled=True)]
    ppermute x8, starting transfers between devices: 37.2 us -> 42.7 us  [send(): return lax.ppermute(a, AXES, perm)]
    all_to_all x3, starting transfers between devices: 24 us -> 21.8 us  [exchange(): return lax.all_to_all(blocks, PLANE, 0, 0, tiled=True)]
    pallas_call x1 -> x2, Pallas kernels: 3.45 us -> 4.7 us  [terms_of(): pl.pallas_call(functools.partial(term_kernel, parts), out_shape=[jax.Shap...]
    unnamed x38 -> x34, local copies, waits for them, and re-layouts: 18 us -> 18 us
  transfers between devices with their start and end apart: 12 -> 12, of which waited for: 4 -> 4; matrix products, arithmetic and copies ran while one was open for 0% -> 0% of each run, Pallas kernels for 14% -> 12%
where the time goes in v4:
time: 198 us; the launch traced here: 197 us
  waiting for transfers between devices  73.6 us (37%)
  starting transfers between devices  64.6 us (33%)
  Pallas kernels  26.8 us (14%)
  local copies, waits for them, and re-layouts  18.1 us (9%)
  between operations  14.3 us (7%)
    ppermute x8, waiting for transfers between devices, send(): return lax.ppermute(a, AXES, perm)  47.1 us
    ppermute x8, starting transfers between devices, send(): return lax.ppermute(a, AXES, perm)  42.7 us
    all_to_all x3, waiting for transfers between devices, exchange(): return lax.all_to_all(blocks, PLANE, 0, 0, tiled=True)  26.4 us
    all_to_all x3, starting transfers between devices, exchange(): return lax.all_to_all(blocks, PLANE, 0, 0, tiled=True)  21.8 us
    unnamed x34, local copies, waits for them, and re-layouts  18 us
    pallas_call x1, Pallas kernels, grad_of(): pl.pallas_call(grad_kernel, grid=(4,), out_shape=jax.ShapeDtypeStruct((89...  7.62 us
    pallas_call x2, Pallas kernels, terms_of(): pl.pallas_call(functools.partial(term_kernel, parts), out_shape=[jax.Shap...  4.7 us
    pallas_call x1, Pallas kernels, pair_of(): pl.pallas_call(pair_kernel, grid=(4,), out_shape=jax.ShapeDtypeStruct((89...  4.18 us
  transfers between devices with their start and end apart: 12, of which 4 were waited for; matrix products, arithmetic and copies ran while one was open for 0% of the time, Pallas kernels for 12%

profile of v4, /device:TPU:6, one launch (start us, length us, event | category | flops | bytes accessed | tf_op | source)
XLA Modules:
  0.0 197.4 jit_solution(14142490702204714754)
XLA Ops:
  7.2 0.0 all-gather.2.cloned.1.call-start
  7.2 0.0 copy-start.11
  7.2 0.9 copy-done.11
  8.2 0.9 copy-done.13
  9.1 1.4 hidden.1
  10.4 0.0 all-gather.2.cloned.1.call-update
  10.5 15.7 %collective-permute-start = (bf16[64,1024]{1,0:T(8,128)(2,1)}, bf16[64,1024]{1,0:T(8,128)(2,1)S(1)}, u32[]{:S(2)}, u32[]{:S(2)}) collective-permute-start(bf16[64,1024]{1,0:T(8,128)(2,1)} %cot_ref.3), channel_id=1, source_target_pairs={{4,260},{5,261},{6,262},{7,263},{12,268},{13,269},{14,270},{15,271... | collective-permute-start | bytes 393224 | tf_op jit(solution)/shard_map/ppermute | solution.py:74
  26.2 0.1 stack.23.pos_ref
  26.3 3.6 %collective-permute-done.far_ref = bf16[64,1024]{1,0:T(8,128)(2,1)S(1)} collective-permute-done((bf16[64,1024]{1,0:T(8,128)(2,1)}, bf16[64,1024]{1,0:T(8,128)(2,1)S(1)}, u32[]{:S(2)}, u32[]{:S(2)}) %collective-permute-start) | collective-permute-done | bytes 131104 | tf_op jit(solution)/shard_map/ppermute | solution.py:74
  29.9 0.9 copy-done.15
  30.8 0.7 copies.2
  31.5 1.3 copy-done.7
  32.8 7.6 %all-to-all-start.1 = ((bf16[16,64,1024]{2,1,0:T(8,128)(2,1)}), bf16[16,64,1024]{2,1,0:T(8,128)(2,1)S(1)}, u32[]{:S(2)}, u32[]{:S(2)}) async-start(bf16[16,64,1024]{2,1,0:T(8,128)(2,1)} %copy-done.7), calls=%async_computation.1 | async-start | bytes 4194304 | tf_op jit(solution)/shard_map/all_to_all | solution.py:119
  40.4 0.7 collective-permute-start.1
  41.1 26.4 %all-to-all-done.1.refs_0_.near_ref = bf16[16,64,1024]{2,1,0:T(8,128)(2,1)S(1)} async-done(((bf16[16,64,1024]{2,1,0:T(8,128)(2,1)}), bf16[16,64,1024]{2,1,0:T(8,128)(2,1)S(1)}, u32[]{:S(2)}, u32[]{:S(2)}) %all-to-all-start.1) | async-done | bytes 2097184 | tf_op jit(solution)/shard_map/all_to_all | solution.py:119
  67.5 0.7 copies.3.refs_0_
  68.2 1.3 copy-done
  69.6 6.5 %all-to-all-start.2 = ((bf16[16,64,1024]{2,1,0:T(8,128)(2,1)}), bf16[16,64,1024]{2,1,0:T(8,128)(2,1)}, u32[]{:S(2)}, u32[]{:S(2)}) async-start(bf16[16,64,1024]{2,1,0:T(8,128)(2,1)} %copy-done), calls=%async_computation.2 | async-start | bytes 4194304 | tf_op jit(solution)/shard_map/all_to_all | solution.py:119
  76.1 1.6 copy-done.1
  77.7 1.5 copy-done.4
  79.2 2.9 %hidden_terms.2 = (bf16[256,896]{1,0:T(8,128)(2,1)S(1)}, bf16[128,896]{1,0:T(8,128)(2,1)S(1)}, bf16[128,896]{1,0:T(8,128)(2,1)S(1)}, bf16[128,896]{1,0:T(8,128)(2,1)S(1)}) custom-call(s32[5]{0:T(128)S(1)} %stack.23.pos_ref, bf16[8,128,1024]{2,1,0:T(8,128)(2,1)S(1)} %bitcast.7, bf16[896,1024]{1,0:T(8,128)(2,1)S(1)} %copy-done.4, ...), custom_call_target="tpu_custom_call" | custom-call | flops 1174405120 | bytes 4194304 | tf_op jit(solution)/shard_map/hidden_terms/pallas_call | solution.py:136
  82.1 5.9 %collective-permute-start.3 = (bf16[256,896]{1,0:T(8,128)(2,1)S(1)}, bf16[256,896]{1,0:T(8,128)(2,1)S(1)}, u32[]{:S(2)}, u32[]{:S(2)}) collective-permute-start(bf16[256,896]{1,0:T(8,128)(2,1)S(1)} %get-tuple-element.16), channel_id=1, source_target_pairs={{0,2},{1,3},{2,4},{3,5},{4,6},{5,7},{6,256},{7,257},{8,10},{9,11},... | collective-permute-start | bytes 1376264 | tf_op jit(solution)/shard_map/ppermute | solution.py:74
  88.0 24.4 %collective-permute-done.3.a_ref = bf16[256,896]{1,0:T(8,128)(2,1)S(1)} collective-permute-done((bf16[256,896]{1,0:T(8,128)(2,1)S(1)}, bf16[256,896]{1,0:T(8,128)(2,1)S(1)}, u32[]{:S(2)}, u32[]{:S(2)}) %collective-permute-start.3) | collective-permute-done | bytes 458784 | tf_op jit(solution)/shard_map/ppermute | solution.py:74
  112.4 0.1 sums.1
  112.5 1.9 collective-permute-start.4
  114.4 4.5 %collective-permute-start.5 = (bf16[128,896]{1,0:T(8,128)(2,1)S(1)}, bf16[128,896]{1,0:T(8,128)(2,1)S(1)}, u32[]{:S(2)}, u32[]{:S(2)}) collective-permute-start(bf16[128,896]{1,0:T(8,128)(2,1)S(1)} %get-tuple-element.20), channel_id=1, source_target_pairs={{0,1},{1,2},{2,3},{3,4},{4,5},{5,6},{6,7},{7,256},{8,9},{9,10},{10... | collective-permute-start | bytes 688136 | tf_op jit(solution)/shard_map/ppermute | solution.py:74
  118.9 0.0 all-gather.2.cloned.1.call-done.hid_ref
  118.9 0.0 copy-start.5
  118.9 1.5 copy-done.5
  120.4 2.0 %copy-done.8 = bf16[2048,896]{1,0:T(8,128)(2,1)S(1)} copy-done((bf16[2048,896]{1,0:T(8,128)(2,1)S(1)}, bf16[2048,896]{1,0:T(8,128)(2,1)}, u32[]{:S(2)}) %copy-start.8) | copy-done | bytes 3670040
  122.5 2.9 %output_terms.1.refs_0_ = bf16[1024,1024]{1,0:T(8,128)(2,1)S(1)} custom-call(s32[5]{0:T(128)S(1)} %stack.23.pos_ref, bf16[2048,896]{1,0:T(8,128)(2,1)S(1)} %copy-done.8, bf16[896,1024]{1,0:T(8,128)(2,1)S(1)} %copy-done.5), custom_call_target="tpu_custom_call" | custom-call | flops 1879048192 | bytes 8388608 | tf_op jit(solution)/shard_map/output_terms/pallas_call | solution.py:155
  125.4 1.3 copy-done.2
  126.7 0.0 all-to-all-done.2.rest_ref
  126.7 7.8 %all-to-all-start = ((bf16[16,64,1024]{2,1,0:T(8,128)(2,1)}), bf16[16,64,1024]{2,1,0:T(8,128)(2,1)}, u32[]{:S(2)}, u32[]{:S(2)}) async-start(bf16[16,64,1024]{2,1,0:T(8,128)(2,1)} %bitcast.9), calls=%async_computation | async-start | bytes 4194304 | tf_op jit(solution)/shard_map/all_to_all | solution.py:119
  134.5 0.0 collective-permute-done.5.d_ref.refs_2_
  134.5 1.6 copy-done.3
  136.1 2.0 %copy-done.9 = bf16[2048,896]{1,0:T(8,128)(2,1)S(1)} copy-done((bf16[2048,896]{1,0:T(8,128)(2,1)S(1)}, bf16[2048,896]{1,0:T(8,128)(2,1)}, u32[]{:S(2)}) %copy-start.9) | copy-done | bytes 3670040
  138.1 7.6 %weight_terms.1.a_ref = bf16[896,1024]{1,0:T(8,128)(2,1)} custom-call(s32[5]{0:T(128)S(1)} %stack.23.pos_ref, bf16[2048,896]{1,0:T(8,128)(2,1)S(1)} %copy-done.9, bf16[16,64,1024]{2,1,0:T(8,128)(2,1)S(1)} %all-to-all-done.1.refs_0_.near_ref, bf16[16,64,1024]{2,1,0:T(8,128)(2,1)} %all-to-all-done.2.rest_ref, bf16[1024,1024]{1,0:T(8,128)(2,1)S(1)} %copy-done.3, ...), custom_call_target="tpu_custom_call" | custom-call | flops 3758096384 | bytes 10485760 | tf_op jit(solution)/shard_map/weight_terms/pallas_call | solution.py:204
  145.7 1.9 collective-permute-start.7
  147.7 1.8 hidden_terms.3
  149.5 6.0 %collective-permute-start.2 = (bf16[256,896]{1,0:T(8,128)(2,1)S(1)}, bf16[256,896]{1,0:T(8,128)(2,1)S(1)}, u32[]{:S(2)}, u32[]{:S(2)}) collective-permute-start(bf16[256,896]{1,0:T(8,128)(2,1)S(1)} %get-tuple-element.15), channel_id=1, source_target_pairs={{0,262},{1,263},{2,0},{3,1},{4,2},{5,3},{6,4},{7,5},{8,270},{9,271... | collective-permute-start | bytes 1376264 | tf_op jit(solution)/shard_map/ppermute | solution.py:74
  155.5 19.2 %collective-permute-done.2.b_ref = bf16[256,896]{1,0:T(8,128)(2,1)S(1)} collective-permute-done((bf16[256,896]{1,0:T(8,128)(2,1)S(1)}, bf16[256,896]{1,0:T(8,128)(2,1)S(1)}, u32[]{:S(2)}, u32[]{:S(2)}) %collective-permute-start.2) | collective-permute-done | bytes 458784 | tf_op jit(solution)/shard_map/ppermute | solution.py:74
  174.7 0.1 add_convert_fusion
  174.7 6.1 %collective-permute-start.6 = (bf16[128,896]{1,0:T(8,128)(2,1)S(1)}, bf16[128,896]{1,0:T(8,128)(2,1)S(1)}, u32[]{:S(2)}, u32[]{:S(2)}) collective-permute-start(bf16[128,896]{1,0:T(8,128)(2,1)S(1)} %add_convert_fusion), channel_id=1, source_target_pairs={{0,263},{1,0},{2,1},{3,2},{4,3},{5,4},{6,5},{7,6},{8,271},{9,8},{1... | collective-permute-start | bytes 688136 | tf_op jit(solution)/shard_map/ppermute | solution.py:74
  180.9 3.5 %output_sum.1.refs_0_ = bf16[64,1024]{1,0:T(8,128)(2,1)} custom-call(bf16[16,64,1024]{2,1,0:T(8,128)(2,1)} %all-to-all-done.got_ref), custom_call_target="tpu_custom_call" | custom-call | flops 1048576 | bytes 2097152 | tf_op jit(solution)/shard_map/output_sum/pallas_call | solution.py:174
  184.4 0.9 copy-done.10
  185.3 4.2 %weight_sum.1 = bf16[896,1024]{1,0:T(8,128)(2,1)} custom-call(bf16[896,1024]{1,0:T(8,128)(2,1)} %weight_terms.1.a_ref, bf16[896,1024]{1,0:T(8,128)(2,1)} %collective-permute-done.7.b_ref, bf16[64,1024]{1,0:T(8,128)(2,1)S(1)} %copy-done.10), custom_call_target="tpu_custom_call" | custom-call | flops 1048576 | bytes 5242880 | tf_op jit(solution)/shard_map/weight_sum/pallas_call | solution.py:223
  189.5 1.1 gradients.1
  (24 shorter events, 0.0 us)
Async XLA Ops:
  7.2 111.8 %all-gather.2.cloned.1.call-start = ((), (), s32[]{:S(2)}) async-start(), calls=%async_computation.3 | async-start | bytes 3899392 | tf_op jit(solution)/shard_map/all_gather | solution.py:275
  7.2 0.9 copy-start.11
  8.2 0.9 copy-start.13
  10.5 19.4 %collective-permute-start = (bf16[64,1024]{1,0:T(8,128)(2,1)}, bf16[64,1024]{1,0:T(8,128)(2,1)S(1)}, u32[]{:S(2)}, u32[]{:S(2)}) collective-permute-start(bf16[64,1024]{1,0:T(8,128)(2,1)} %cot_ref.3), channel_id=1, source_target_pairs={{4,260},{5,261},{6,262},{7,263},{12,268},{13,269},{14,270},{15,271... | collective-permute-start | bytes 393224 | tf_op jit(solution)/shard_map/ppermute | solution.py:74
  29.9 0.9 copy-start.15
  31.5 1.3 copy-start.7
  32.8 7.6 %copy-start.16 = (bf16[64,1024]{1,0:T(8,128)(2,1)S(1)}, bf16[64,1024]{1,0:T(8,128)(2,1)}, u32[]{:S(2)}) copy-start(bf16[64,1024]{1,0:T(8,128)(2,1)} %cot_ref.3) | copy-start | bytes 393220
  32.8 34.7 %all-to-all-start.1 = ((bf16[16,64,1024]{2,1,0:T(8,128)(2,1)}), bf16[16,64,1024]{2,1,0:T(8,128)(2,1)S(1)}, u32[]{:S(2)}, u32[]{:S(2)}) async-start(bf16[16,64,1024]{2,1,0:T(8,128)(2,1)} %copy-done.7), calls=%async_computation.1 | async-start | bytes 4194304 | tf_op jit(solution)/shard_map/all_to_all | solution.py:119
  40.4 0.7 collective-permute-start.1
  68.2 1.4 copy-start
  69.6 57.1 %all-to-all-start.2 = ((bf16[16,64,1024]{2,1,0:T(8,128)(2,1)}), bf16[16,64,1024]{2,1,0:T(8,128)(2,1)}, u32[]{:S(2)}, u32[]{:S(2)}) async-start(bf16[16,64,1024]{2,1,0:T(8,128)(2,1)} %copy-done), calls=%async_computation.2 | async-start | bytes 4194304 | tf_op jit(solution)/shard_map/all_to_all | solution.py:119
  76.0 1.6 copy-start.1
  77.7 1.5 copy-start.4
  82.1 30.3 %collective-permute-start.3 = (bf16[256,896]{1,0:T(8,128)(2,1)S(1)}, bf16[256,896]{1,0:T(8,128)(2,1)S(1)}, u32[]{:S(2)}, u32[]{:S(2)}) collective-permute-start(bf16[256,896]{1,0:T(8,128)(2,1)S(1)} %get-tuple-element.16), channel_id=1, source_target_pairs={{0,2},{1,3},{2,4},{3,5},{4,6},{5,7},{6,256},{7,257},{8,10},{9,11},... | collective-permute-start | bytes 1376264 | tf_op jit(solution)/shard_map/ppermute | solution.py:74
  112.5 22.0 %collective-permute-start.4 = (bf16[128,896]{1,0:T(8,128)(2,1)S(1)}, bf16[128,896]{1,0:T(8,128)(2,1)S(1)}, u32[]{:S(2)}, u32[]{:S(2)}) collective-permute-start(bf16[128,896]{1,0:T(8,128)(2,1)S(1)} %get-tuple-element.19), channel_id=1, source_target_pairs={{0,2},{1,3},{2,4},{3,5},{4,6},{5,7},{6,256},{7,257},{8,10},{9,11},... | collective-permute-start | bytes 688136 | tf_op jit(solution)/shard_map/ppermute | solution.py:74
  114.4 20.0 %collective-permute-start.5 = (bf16[128,896]{1,0:T(8,128)(2,1)S(1)}, bf16[128,896]{1,0:T(8,128)(2,1)S(1)}, u32[]{:S(2)}, u32[]{:S(2)}) collective-permute-start(bf16[128,896]{1,0:T(8,128)(2,1)S(1)} %get-tuple-element.20), channel_id=1, source_target_pairs={{0,1},{1,2},{2,3},{3,4},{4,5},{5,6},{6,7},{7,256},{8,9},{9,10},{10... | collective-permute-start | bytes 688136 | tf_op jit(solution)/shard_map/ppermute | solution.py:74
  118.9 1.5 copy-start.5
  120.4 2.0 %copy-start.8 = (bf16[2048,896]{1,0:T(8,128)(2,1)S(1)}, bf16[2048,896]{1,0:T(8,128)(2,1)}, u32[]{:S(2)}) copy-start(bf16[2048,896]{1,0:T(8,128)(2,1)} %all-gather.2.cloned.1.call-done.hid_ref) | copy-start | bytes 11010052
  125.3 1.3 copy-start.2
  126.7 54.2 %all-to-all-start = ((bf16[16,64,1024]{2,1,0:T(8,128)(2,1)}), bf16[16,64,1024]{2,1,0:T(8,128)(2,1)}, u32[]{:S(2)}, u32[]{:S(2)}) async-start(bf16[16,64,1024]{2,1,0:T(8,128)(2,1)} %bitcast.9), calls=%async_computation | async-start | bytes 4194304 | tf_op jit(solution)/shard_map/all_to_all | solution.py:119
  134.5 1.6 copy-start.3
  136.1 2.0 %copy-start.9 = (bf16[2048,896]{1,0:T(8,128)(2,1)S(1)}, bf16[2048,896]{1,0:T(8,128)(2,1)}, u32[]{:S(2)}) copy-start(bf16[2048,896]{1,0:T(8,128)(2,1)} %all-gather.2.cloned.1.call-done.hid_ref) | copy-start | bytes 11010052
  138.1 9.5 %copy-start.6 = (bf16[896,1024]{1,0:T(8,128)(2,1)S(1)}, bf16[896,1024]{1,0:T(8,128)(2,1)}, u32[]{:S(2)}) copy-start(bf16[896,1024]{1,0:T(8,128)(2,1)} %w_ref.5) | copy-start | bytes 5505028
  145.7 38.7 %collective-permute-start.7 = (bf16[896,1024]{1,0:T(8,128)(2,1)}, bf16[896,1024]{1,0:T(8,128)(2,1)}, u32[]{:S(2)}, u32[]{:S(2)}) collective-permute-start(bf16[896,1024]{1,0:T(8,128)(2,1)} %weight_terms.1.a_ref), channel_id=1, source_target_pairs={{0,128},{1,129},{2,130},{3,131},{4,132},{5,133},{6,134},{7,135},{8... | collective-permute-start | bytes 5505032 | tf_op jit(solution)/shard_map/ppermute | solution.py:74
  149.5 25.2 %collective-permute-start.2 = (bf16[256,896]{1,0:T(8,128)(2,1)S(1)}, bf16[256,896]{1,0:T(8,128)(2,1)S(1)}, u32[]{:S(2)}, u32[]{:S(2)}) collective-permute-start(bf16[256,896]{1,0:T(8,128)(2,1)S(1)} %get-tuple-element.15), channel_id=1, source_target_pairs={{0,262},{1,263},{2,0},{3,1},{4,2},{5,3},{6,4},{7,5},{8,270},{9,271... | collective-permute-start | bytes 1376264 | tf_op jit(solution)/shard_map/ppermute | solution.py:74
  174.7 14.8 %collective-permute-start.6 = (bf16[128,896]{1,0:T(8,128)(2,1)S(1)}, bf16[128,896]{1,0:T(8,128)(2,1)S(1)}, u32[]{:S(2)}, u32[]{:S(2)}) collective-permute-start(bf16[128,896]{1,0:T(8,128)(2,1)S(1)} %add_convert_fusion), channel_id=1, source_target_pairs={{0,263},{1,0},{2,1},{3,2},{4,3},{5,4},{6,5},{7,6},{8,271},{9,8},{1... | collective-permute-start | bytes 688136 | tf_op jit(solution)/shard_map/ppermute | solution.py:74
  184.4 0.9 copy-start.10
  185.3 4.2 %copy-start.12 = (bf16[128,896]{1,0:T(8,128)(2,1)S(1)}, bf16[128,896]{1,0:T(8,128)(2,1)}, u32[]{:S(2)}) copy-start(bf16[128,896]{1,0:T(8,128)(2,1)} %gate_ref.3) | copy-start | bytes 688132
  185.3 4.2 %copy-start.14 = (bf16[128,896]{1,0:T(8,128)(2,1)S(1)}, bf16[128,896]{1,0:T(8,128)(2,1)}, u32[]{:S(2)}) copy-start(bf16[128,896]{1,0:T(8,128)(2,1)} %up_ref.3) | copy-start | bytes 688132
Sparse Core Ops, SparseCore 0:
  10.7 101.4 all-gather.1

commit v5 on v4

--- a/solution.py
+++ b/solution.py
@@ -103,7 +103,7 @@
     pl.when(jnp.logical_not(mine) if far_wanted else mine)(lambda: fill(cot_ref))
 
 
-def copies_of(pos, cot, far_wanted, *after):
+def copies_of(pos, cot, far, far_wanted, *after):
     return pl.pallas_call(
         functools.partial(copies_kernel, far_wanted),
         out_shape=jax.ShapeDtypeStruct((16, 64, 1024), BF),
@@ -112,7 +112,7 @@
         compiler_params=PARAMS,
         cost_estimate=cost(0, 2),
         name="copies",
-    )(pos, cot, send(cot, swap_z(far_wanted)), *after)
+    )(pos, cot, far, *after)
 
 
 def exchange(blocks):
@@ -232,65 +232,69 @@
     )(a, b, *after)
 
 
-def ends_kernel(gate_ref, up_ref, here_ref, b_ref, c_ref, d_ref, e_ref, *refs):
-    grad = here_ref[...].astype(F32) + b_ref[128:].astype(F32) + c_ref[...].astype(F32)
-    grad = grad + (d_ref[...].astype(F32) + e_ref[...].astype(F32))
+def ends_kernel(gate_ref, up_ref, here_ref, a_ref, b_ref, *refs):
+    grad = here_ref[...].astype(F32) + a_ref[...].astype(F32) + b_ref[...].astype(F32)
     g, u = gate_ref[...].astype(F32), up_ref[...].astype(F32)
     sig = jax.nn.sigmoid(g)
     refs[-2][...] = (grad * u * sig * (1.0 + g * (1.0 - sig))).astype(BF)
     refs[-1][...] = (grad * (g * sig)).astype(BF)
 
 
-def ends_of(gate, up, here, b, c, d, e, *after):
+def ends_of(gate, up, here, a, b, *after):
     return pl.pallas_call(
         ends_kernel,
         out_shape=[jax.ShapeDtypeStruct((128, 896), BF)] * 2,
-        in_specs=[VMEM] * 7 + [ANY] * len(after),
+        in_specs=[VMEM] * 5 + [ANY] * len(after),
         out_specs=[VMEM] * 2,
         compiler_params=PARAMS,
         cost_estimate=cost(2**21, 2),
         name="gradients",
-    )(gate, up, here, b, c, d, e, *after)
-
-
-def sum_kernel(a_ref, p_ref, q_ref, c_ref, d_ref):
-    c_ref[...] = (a_ref[:128].astype(F32) + p_ref[...].astype(F32)).astype(BF)
-    d_ref[...] = (a_ref[128:].astype(F32) + q_ref[...].astype(F32)).astype(BF)
-
-
-def sums_of(a, p, q):
-    return pl.pallas_call(
-        sum_kernel,
-        out_shape=[jax.ShapeDtypeStruct((128, 896), BF)] * 2,
-        in_specs=[VMEM] * 3,
-        out_specs=[VMEM] * 2,
+    )(gate, up, here, a, b, *after)
+
+
+def add_kernel(*refs):
+    n = len(refs) // 3
+    for i in range(n):
+        refs[2 * n + i][...] = (refs[2 * i][...].astype(F32) + refs[2 * i + 1][...].astype(F32)).astype(BF)
+
+
+def add(*pairs_of):
+    out = pl.pallas_call(
+        add_kernel,
+        out_shape=[jax.ShapeDtypeStruct((128, 896), BF)] * len(pairs_of),
+        in_specs=[VMEM] * (2 * len(pairs_of)),
+        out_specs=[VMEM] * len(pairs_of),
         compiler_params=PARAMS,
         cost_estimate=cost(2**18, 1),
         name="sums",
-    )(a, p, q)
+    )(*[v for p in pairs_of for v in p])
+    return out
 
 
 def per_device(gate, up, w, cot):
     pos = jnp.stack([lax.axis_index(a) for a in AXES]).astype(jnp.int32)
     hid = lax.all_gather(hidden_of(gate, up), RING, axis=0, tiled=True)
-    near = exchange(copies_of(pos, cot, False))
-    rest = copies_of(pos, cot, True, near)
-    p43, p2, p1, here = terms_of(((4, 3), (2,), (1,), (0,)), pos, near, w, rest)
-    rest = exchange(rest)
-
-    right, left, right2, left2 = ring_move(1), ring_move(-1), ring_move(2), ring_move(-2)
-    a = send(p43, right2)
+    near = exchange(copies_of(pos, cot, send(cot, swap_z(False)), False))
+    far = send(cot, swap_z(True))
+    parts = ((4,), (3,), (-3,), (2,), (-2,), (1,), (-1,), (0,))
+    p4, p3, m3, p2, m2, p1, m1, here = terms_of(parts, pos, near, w, far)
+
+    right, left = ring_move(1), ring_move(-1)
+    a = send(p4, right)
+    a, = add((a, p3))
+    a, b = send(a, right), send(m3, left)
+    rest = exchange(copies_of(pos, cot, far, True, a))
+    a, b = add((a, p2), (b, m2))
+    a, b = send(a, right), send(b, left)
+    a, b = add((a, p1), (b, m1))
+    a, b = send(a, right), send(b, left)
+
     o = out_of(pos, hid, w)
-    m32, m1 = terms_of(((-3, -2), (-1,)), pos, near, w, o)
-    b = send(m32, left2)
-    c, d = sums_of(a, p2, p1)
-    e = (b[:128].astype(F32) + m1.astype(F32)).astype(BF)
-    c, d, e = send(c, right2), send(d, right), send(e, left)
     output = total_of(exchange(o.reshape(16, 64, 1024)))
-    grad_gate, grad_up = ends_of(gate, up, here, b, c, d, e, output)
-
-    part = grad_of(pos, hid, near, rest, o, c, d)
-    grad_weight = pair_of(part, send(part, SWAP_CORE), output)
+    grad_gate, grad_up = ends_of(gate, up, here, a, b, output)
+
+    part = grad_of(pos, hid, near, rest, o, a, b)
+    grad_weight = pair_of(part, send(part, SWAP_CORE))
     return output, grad_gate, grad_up, grad_weight
 
 

time: 198 us -> 192 us (0.970)
  waiting for transfers between devices: 73.6 us -> 67.2 us
  local copies, waits for them, and re-layouts: 18.1 us -> 21.3 us
  Pallas kernels: 26.8 us -> 24 us
    ppermute x8 -> x10, waiting for transfers between devices: 47.1 us -> 38.2 us  [send(): return lax.ppermute(a, AXES, perm)]
    unnamed x34 -> x44, local copies, waits for them, and re-layouts: 18 us -> 21.2 us
    ppermute x8 -> x10, starting transfers between devices: 42.7 us -> 39.8 us  [send(): return lax.ppermute(a, AXES, perm)]
    pallas_call x2, Pallas kernels: 1.41 us -> 4.1 us  [copies_of(): pl.pallas_call(functools.partial(copies_kernel, far_wanted), out_shape=ja...]
    all_to_all x3, waiting for transfers between devices: 26.4 us -> 29 us  [exchange(): return lax.all_to_all(blocks, PLANE, 0, 0, tiled=True)]
    pallas_call x1, Pallas kernels: 4.18 us -> 1.9 us  [pair_of(): pl.pallas_call(pair_kernel, grid=(4,), out_shape=jax.ShapeDtypeStruct((89...]
    pallas_call x2 -> x1, Pallas kernels: 4.7 us -> 5.19 us  [terms_of(): pl.pallas_call(functools.partial(term_kernel, parts), out_shape=[jax.Shap...]
  transfers between devices with their start and end apart: 12 -> 14, of which waited for: 4 -> 9; matrix products, arithmetic and copies ran while one was open for 0% -> 0% of each run, Pallas kernels for 12% -> 11%
where the time goes in v5:
time: 192 us; the launch traced here: 190 us
  waiting for transfers between devices  67.2 us (35%)
  starting transfers between devices  63.4 us (33%)
  Pallas kernels  24 us (12%)
  local copies, waits for them, and re-layouts  21.3 us (11%)
  between operations  14.3 us (7%)
    ppermute x10, starting transfers between devices, send(): return lax.ppermute(a, AXES, perm)  39.8 us
    ppermute x10, waiting for transfers between devices, send(): return lax.ppermute(a, AXES, perm)  38.2 us
    all_to_all x3, waiting for transfers between devices, exchange(): return lax.all_to_all(blocks, PLANE, 0, 0, tiled=True)  29 us
    all_to_all x3, starting transfers between devices, exchange(): return lax.all_to_all(blocks, PLANE, 0, 0, tiled=True)  23.6 us
    unnamed x44, local copies, waits for them, and re-layouts  21.2 us
    pallas_call x1, Pallas kernels, grad_of(): pl.pallas_call(grad_kernel, grid=(4,), out_shape=jax.ShapeDtypeStruct((89...  5.74 us
    pallas_call x1, Pallas kernels, terms_of(): pl.pallas_call(functools.partial(term_kernel, parts), out_shape=[jax.Shap...  5.19 us
    pallas_call x2, Pallas kernels, copies_of(): pl.pallas_call(functools.partial(copies_kernel, far_wanted), out_shape=ja...  4.1 us
  transfers between devices with their start and end apart: 14, of which 9 were waited for; matrix products, arithmetic and copies ran while one was open for 0% of the time, Pallas kernels for 11%

profile of v5, /device:TPU:6, one launch (start us, length us, event | category | flops | bytes accessed | tf_op | source)
XLA Modules:
  0.0 190.2 jit_solution(6957052733943739676)
XLA Ops:
  7.2 0.9 copy-done.10
  8.2 0.9 copy-done.12
  9.1 1.4 hidden.1
  10.5 15.7 %collective-permute-start = (bf16[64,1024]{1,0:T(8,128)(2,1)}, bf16[64,1024]{1,0:T(8,128)(2,1)S(1)}, u32[]{:S(2)}, u32[]{:S(2)}) collective-permute-start(bf16[64,1024]{1,0:T(8,128)(2,1)} %cot_ref.3), channel_id=1, source_target_pairs={{4,260},{5,261},{6,262},{7,263},{12,268},{13,269},{14,270},{15,271... | collective-permute-start | bytes 393224 | tf_op jit(solution)/shard_map/ppermute | solution.py:74
  26.3 3.6 %collective-permute-done.far_ref = bf16[64,1024]{1,0:T(8,128)(2,1)S(1)} collective-permute-done((bf16[64,1024]{1,0:T(8,128)(2,1)}, bf16[64,1024]{1,0:T(8,128)(2,1)S(1)}, u32[]{:S(2)}, u32[]{:S(2)}) %collective-permute-start) | collective-permute-done | bytes 131104 | tf_op jit(solution)/shard_map/ppermute | solution.py:74
  29.9 0.9 copy-done.14
  30.8 2.0 %copies.2 = bf16[16,64,1024]{2,1,0:T(8,128)(2,1)} custom-call(s32[5]{0:T(128)S(1)} %stack.23.pos_ref, bf16[64,1024]{1,0:T(8,128)(2,1)S(1)} %copy-done.14, bf16[64,1024]{1,0:T(8,128)(2,1)S(1)} %collective-permute-done.far_ref), custom_call_target="tpu_custom_call" | custom-call | bytes 2097152 | tf_op jit(solution)/shard_map/copies/pallas_call | solution.py:107
  32.8 7.6 %all-to-all-start.1 = ((bf16[16,64,1024]{2,1,0:T(8,128)(2,1)}), bf16[16,64,1024]{2,1,0:T(8,128)(2,1)S(1)}, u32[]{:S(2)}, u32[]{:S(2)}) async-start(bf16[16,64,1024]{2,1,0:T(8,128)(2,1)} %copies.2), calls=%async_computation.1 | async-start | bytes 4194304 | tf_op jit(solution)/shard_map/all_to_all | solution.py:119
  40.4 0.7 collective-permute-start.1
  41.1 0.6 copy-done.19
  41.7 25.8 %all-to-all-done.1.near_ref = bf16[16,64,1024]{2,1,0:T(8,128)(2,1)S(1)} async-done(((bf16[16,64,1024]{2,1,0:T(8,128)(2,1)}), bf16[16,64,1024]{2,1,0:T(8,128)(2,1)S(1)}, u32[]{:S(2)}, u32[]{:S(2)}) %all-to-all-start.1) | async-done | bytes 2097184 | tf_op jit(solution)/shard_map/all_to_all | solution.py:119
  67.5 2.3 %copy-done.8 = bf16[896,1024]{1,0:T(8,128)(2,1)S(1)} copy-done((bf16[896,1024]{1,0:T(8,128)(2,1)S(1)}, bf16[896,1024]{1,0:T(8,128)(2,1)}, u32[]{:S(2)}) %copy-start.8) | copy-done | bytes 1835032
  69.8 0.9 copy-done.20
  70.7 5.2 %hidden_terms.1 = (bf16[128,896]{1,0:T(8,128)(2,1)S(1)}, bf16[128,896]{1,0:T(8,128)(2,1)S(1)}, bf16[128,896]{1,0:T(8,128)(2,1)S(1)}, bf16[128,896]{1,0:T(8,128)(...) custom-call(s32[5]{0:T(128)S(1)} %stack.23.pos_ref, ...), custom_call_target="tpu_custom_call" | custom-call | flops 1879048192 | bytes 4194304 | tf_op jit(solution)/shard_map/hidden_terms/pallas_call | solution.py:136
  75.9 0.7 copy-done.17
  76.6 2.7 %collective-permute-start.2 = (bf16[128,896]{1,0:T(8,128)(2,1)S(1)}, bf16[128,896]{1,0:T(8,128)(2,1)S(1)}, u32[]{:S(2)}, u32[]{:S(2)}) collective-permute-start(bf16[128,896]{1,0:T(8,128)(2,1)S(1)} %get-tuple-element.19), channel_id=1, source_target_pairs={{0,1},{1,2},{2,3},{3,4},{4,5},{5,6},{6,7},{7,256},{8,9},{9,10},{10... | collective-permute-start | bytes 688136 | tf_op jit(solution)/shard_map/ppermute | solution.py:74
  79.2 13.6 %collective-permute-done.2.refs_0_ = bf16[128,896]{1,0:T(8,128)(2,1)S(1)} collective-permute-done((bf16[128,896]{1,0:T(8,128)(2,1)S(1)}, bf16[128,896]{1,0:T(8,128)(2,1)S(1)}, u32[]{:S(2)}, u32[]{:S(2)}) %collective-permute-start.2) | collective-permute-done | bytes 229408 | tf_op jit(solution)/shard_map/ppermute | solution.py:74
  92.9 1.9 %collective-permute-start.3 = (bf16[128,896]{1,0:T(8,128)(2,1)S(1)}, bf16[128,896]{1,0:T(8,128)(2,1)S(1)}, u32[]{:S(2)}, u32[]{:S(2)}) collective-permute-start(bf16[128,896]{1,0:T(8,128)(2,1)S(1)} %sums.3), channel_id=1, source_target_pairs={{0,1},{1,2},{2,3},{3,4},{4,5},{5,6},{6,7},{7,256},{8,9},{9,10},{10... | collective-permute-start | bytes 688136 | tf_op jit(solution)/shard_map/ppermute | solution.py:74
  94.8 7.9 %collective-permute-done.3.refs_0_ = bf16[128,896]{1,0:T(8,128)(2,1)S(1)} collective-permute-done((bf16[128,896]{1,0:T(8,128)(2,1)S(1)}, bf16[128,896]{1,0:T(8,128)(2,1)S(1)}, u32[]{:S(2)}, u32[]{:S(2)}) %collective-permute-start.3) | collective-permute-done | bytes 229408 | tf_op jit(solution)/shard_map/ppermute | solution.py:74
  102.7 2.1 %copies.3 = bf16[16,64,1024]{2,1,0:T(8,128)(2,1)} custom-call(s32[5]{0:T(128)S(1)} %stack.23.pos_ref, bf16[64,1024]{1,0:T(8,128)(2,1)S(1)} %copy-done.15, bf16[64,1024]{1,0:T(8,128)(2,1)S(1)} %copy-done.20, bf16[128,896]{1,0:T(8,128)(2,1)S(1)} %collective-permute-done.3.refs_0_), custom_call_target="tpu_custom_call" | custom-call | bytes 2097152 | tf_op jit(solution)/shard_map/copies/pallas_call | solution.py:107
  104.8 8.8 %all-to-all-start.2 = ((bf16[16,64,1024]{2,1,0:T(8,128)(2,1)}), bf16[16,64,1024]{2,1,0:T(8,128)(2,1)S(1)}, u32[]{:S(2)}, u32[]{:S(2)}) async-start(bf16[16,64,1024]{2,1,0:T(8,128)(2,1)} %copies.3), calls=%async_computation.2 | async-start | bytes 4194304 | tf_op jit(solution)/shard_map/all_to_all | solution.py:119
  113.6 2.3 %collective-permute-start.4 = (bf16[128,896]{1,0:T(8,128)(2,1)}, bf16[128,896]{1,0:T(8,128)(2,1)S(1)}, u32[]{:S(2)}, u32[]{:S(2)}) collective-permute-start(bf16[128,896]{1,0:T(8,128)(2,1)} %copy-done.21), channel_id=1, source_target_pairs={{0,263},{1,0},{2,1},{3,2},{4,3},{5,4},{6,5},{7,6},{8,271},{9,8},{1... | collective-permute-start | bytes 688136 | tf_op jit(solution)/shard_map/ppermute | solution.py:74
  115.9 5.9 %collective-permute-done.4.refs_2_ = bf16[128,896]{1,0:T(8,128)(2,1)S(1)} collective-permute-done((bf16[128,896]{1,0:T(8,128)(2,1)}, bf16[128,896]{1,0:T(8,128)(2,1)S(1)}, u32[]{:S(2)}, u32[]{:S(2)}) %collective-permute-start.4) | collective-permute-done | bytes 229408 | tf_op jit(solution)/shard_map/ppermute | solution.py:74
  121.7 0.1 sums.4
  121.9 1.9 %collective-permute-start.5 = (bf16[128,896]{1,0:T(8,128)(2,1)S(1)}, bf16[128,896]{1,0:T(8,128)(2,1)S(1)}, u32[]{:S(2)}, u32[]{:S(2)}) collective-permute-start(bf16[128,896]{1,0:T(8,128)(2,1)S(1)} %get-tuple-element.24), channel_id=1, source_target_pairs={{0,1},{1,2},{2,3},{3,4},{4,5},{5,6},{6,7},{7,256},{8,9},{9,10},{10... | collective-permute-start | bytes 688136 | tf_op jit(solution)/shard_map/ppermute | solution.py:74
  123.8 5.1 %collective-permute-start.6 = (bf16[128,896]{1,0:T(8,128)(2,1)S(1)}, bf16[128,896]{1,0:T(8,128)(2,1)S(1)}, u32[]{:S(2)}, u32[]{:S(2)}) collective-permute-start(bf16[128,896]{1,0:T(8,128)(2,1)S(1)} %get-tuple-element.26), channel_id=1, source_target_pairs={{0,263},{1,0},{2,1},{3,2},{4,3},{5,4},{6,5},{7,6},{8,271},{9,8},{1... | collective-permute-start | bytes 688136 | tf_op jit(solution)/shard_map/ppermute | solution.py:74
  128.9 2.1 %collective-permute-done.5.refs_0_ = bf16[128,896]{1,0:T(8,128)(2,1)S(1)} collective-permute-done((bf16[128,896]{1,0:T(8,128)(2,1)S(1)}, bf16[128,896]{1,0:T(8,128)(2,1)S(1)}, u32[]{:S(2)}, u32[]{:S(2)}) %collective-permute-start.5) | collective-permute-done | bytes 229408 | tf_op jit(solution)/shard_map/ppermute | solution.py:74
  131.0 1.5 collective-permute-done.6.refs_2_
  132.6 1.9 %collective-permute-start.7 = (bf16[128,896]{1,0:T(8,128)(2,1)S(1)}, bf16[128,896]{1,0:T(8,128)(2,1)S(1)}, u32[]{:S(2)}, u32[]{:S(2)}) collective-permute-start(bf16[128,896]{1,0:T(8,128)(2,1)S(1)} %get-tuple-element.28), channel_id=1, source_target_pairs={{0,1},{1,2},{2,3},{3,4},{4,5},{5,6},{6,7},{7,256},{8,9},{9,10},{10... | collective-permute-start | bytes 688136 | tf_op jit(solution)/shard_map/ppermute | solution.py:74
  134.5 5.6 %collective-permute-start.8 = (bf16[128,896]{1,0:T(8,128)(2,1)S(1)}, bf16[128,896]{1,0:T(8,128)(2,1)S(1)}, u32[]{:S(2)}, u32[]{:S(2)}) collective-permute-start(bf16[128,896]{1,0:T(8,128)(2,1)S(1)} %get-tuple-element.29), channel_id=1, source_target_pairs={{0,263},{1,0},{2,1},{3,2},{4,3},{5,4},{6,5},{7,6},{8,271},{9,8},{1... | collective-permute-start | bytes 688136 | tf_op jit(solution)/shard_map/ppermute | solution.py:74
  140.1 2.0 %copy-done.2 = bf16[2048,896]{1,0:T(8,128)(2,1)S(1)} copy-done((bf16[2048,896]{1,0:T(8,128)(2,1)S(1)}, bf16[2048,896]{1,0:T(8,128)(2,1)}, u32[]{:S(2)}) %copy-start.2) | copy-done | bytes 3670040
  142.2 1.5 copy-done.9
  143.7 2.9 %output_terms.1.refs_0_ = bf16[1024,1024]{1,0:T(8,128)(2,1)S(1)} custom-call(s32[5]{0:T(128)S(1)} %stack.23.pos_ref, bf16[2048,896]{1,0:T(8,128)(2,1)S(1)} %copy-done.2, bf16[896,1024]{1,0:T(8,128)(2,1)S(1)} %copy-done.9), custom_call_target="tpu_custom_call" | custom-call | flops 1879048192 | bytes 8388608 | tf_op jit(solution)/shard_map/output_terms/pallas_call | solution.py:155
  146.5 1.3 copy-done
  147.9 1.4 copy-done.6
  149.2 7.2 %all-to-all-start = ((bf16[16,64,1024]{2,1,0:T(8,128)(2,1)}), bf16[16,64,1024]{2,1,0:T(8,128)(2,1)S(1)}, u32[]{:S(2)}, u32[]{:S(2)}) async-start(bf16[16,64,1024]{2,1,0:T(8,128)(2,1)} %bitcast.7), calls=%async_computation | async-start | bytes 4194304 | tf_op jit(solution)/shard_map/all_to_all | solution.py:119
  156.5 1.6 copy-done.1
  158.1 2.0 %copy-done.3 = bf16[2048,896]{1,0:T(8,128)(2,1)S(1)} copy-done((bf16[2048,896]{1,0:T(8,128)(2,1)S(1)}, bf16[2048,896]{1,0:T(8,128)(2,1)}, u32[]{:S(2)}) %copy-start.3) | copy-done | bytes 3670040
  160.1 1.6 copy-done.5
  161.7 1.6 copy-done.7
  163.3 5.7 %weight_terms.1.a_ref = bf16[896,1024]{1,0:T(8,128)(2,1)S(1)} custom-call(s32[5]{0:T(128)S(1)} %stack.23.pos_ref, bf16[2048,896]{1,0:T(8,128)(2,1)S(1)} %copy-done.3, bf16[16,64,1024]{2,1,0:T(8,128)(2,1)S(1)} %copy-done.5, bf16[16,64,1024]{2,1,0:T(8,128)(2,1)S(1)} %copy-done.7, bf16[1024,1024]{1,0:T(8,128)(2,1)S(1)} %copy-done.1, ...), custom_call_target="tpu_custom_call" | custom-call | flops 3758096384 | bytes 10485760 | tf_op jit(solution)/shard_map/weight_terms/pallas_call | solution.py:204
  169.1 1.9 %collective-permute-start.9 = (bf16[896,1024]{1,0:T(8,128)(2,1)S(1)}, bf16[896,1024]{1,0:T(8,128)(2,1)S(1)}, u32[]{:S(2)}, u32[]{:S(2)}) collective-permute-start(bf16[896,1024]{1,0:T(8,128)(2,1)S(1)} %weight_terms.1.a_ref), channel_id=1, source_target_pairs={{0,128},{1,129},{2,130},{3,131},{4,132},{5,133},{6,134},{7,135},{8... | collective-permute-start | bytes 5505032 | tf_op jit(solution)/shard_map/ppermute | solution.py:74
  171.0 3.8 %collective-permute-done.9.b_ref = bf16[896,1024]{1,0:T(8,128)(2,1)S(1)} collective-permute-done((bf16[896,1024]{1,0:T(8,128)(2,1)S(1)}, bf16[896,1024]{1,0:T(8,128)(2,1)S(1)}, u32[]{:S(2)}, u32[]{:S(2)}) %collective-permute-start.9) | collective-permute-done | bytes 1835040 | tf_op jit(solution)/shard_map/ppermute | solution.py:74
  174.7 1.9 weight_sum.1
  176.6 3.2 %all-to-all-done.got_ref = bf16[16,64,1024]{2,1,0:T(8,128)(2,1)S(1)} async-done(((bf16[16,64,1024]{2,1,0:T(8,128)(2,1)}), bf16[16,64,1024]{2,1,0:T(8,128)(2,1)S(1)}, u32[]{:S(2)}, u32[]{:S(2)}) %all-to-all-start) | async-done | bytes 2097184 | tf_op jit(solution)/shard_map/all_to_all | solution.py:119
  179.9 1.6 output_sum.1.refs_0_
  181.5 0.9 copy-done.16
  182.4 1.0 gradients.1
  (38 shorter events, 0.4 us)
Async XLA Ops:
  7.2 133.0 %all-gather.2.cloned.1.call-start = ((), (), s32[]{:S(2)}) async-start(), calls=%async_computation.3 | async-start | bytes 3899392 | tf_op jit(solution)/shard_map/all_gather | solution.py:276
  7.2 0.9 copy-start.10
  8.2 0.9 copy-start.12
  10.5 19.4 %collective-permute-start = (bf16[64,1024]{1,0:T(8,128)(2,1)}, bf16[64,1024]{1,0:T(8,128)(2,1)S(1)}, u32[]{:S(2)}, u32[]{:S(2)}) collective-permute-start(bf16[64,1024]{1,0:T(8,128)(2,1)} %cot_ref.3), channel_id=1, source_target_pairs={{4,260},{5,261},{6,262},{7,263},{12,268},{13,269},{14,270},{15,271... | collective-permute-start | bytes 393224 | tf_op jit(solution)/shard_map/ppermute | solution.py:74
  29.9 0.9 copy-start.14
  32.8 7.6 %copy-start.15 = (bf16[64,1024]{1,0:T(8,128)(2,1)S(1)}, bf16[64,1024]{1,0:T(8,128)(2,1)}, u32[]{:S(2)}) copy-start(bf16[64,1024]{1,0:T(8,128)(2,1)} %cot_ref.3) | copy-start | bytes 393220
  32.8 34.7 %all-to-all-start.1 = ((bf16[16,64,1024]{2,1,0:T(8,128)(2,1)}), bf16[16,64,1024]{2,1,0:T(8,128)(2,1)S(1)}, u32[]{:S(2)}, u32[]{:S(2)}) async-start(bf16[16,64,1024]{2,1,0:T(8,128)(2,1)} %copies.2), calls=%async_computation.1 | async-start | bytes 4194304 | tf_op jit(solution)/shard_map/all_to_all | solution.py:119
  40.4 0.7 collective-permute-start.1
  41.1 0.7 copy-start.19
  67.5 8.4 %copy-start.4 = (bf16[16,64,1024]{2,1,0:T(8,128)(2,1)}, bf16[16,64,1024]{2,1,0:T(8,128)(2,1)S(1)}, u32[]{:S(2)}) copy-start(bf16[16,64,1024]{2,1,0:T(8,128)(2,1)S(1)} %all-to-all-done.1.near_ref) | copy-start | bytes 6291460
  67.5 2.3 %copy-start.8 = (bf16[896,1024]{1,0:T(8,128)(2,1)S(1)}, bf16[896,1024]{1,0:T(8,128)(2,1)}, u32[]{:S(2)}) copy-start(bf16[896,1024]{1,0:T(8,128)(2,1)} %w_ref.3) | copy-start | bytes 5505028
  69.8 0.9 copy-start.20
  75.9 0.7 copy-start.17
  76.6 26.1 %copy-start.21 = (bf16[128,896]{1,0:T(8,128)(2,1)}, bf16[128,896]{1,0:T(8,128)(2,1)S(1)}, u32[]{:S(2)}) copy-start(bf16[128,896]{1,0:T(8,128)(2,1)S(1)} %get-tuple-element.22) | copy-start | bytes 688132
  76.6 16.3 %collective-permute-start.2 = (bf16[128,896]{1,0:T(8,128)(2,1)S(1)}, bf16[128,896]{1,0:T(8,128)(2,1)S(1)}, u32[]{:S(2)}, u32[]{:S(2)}) collective-permute-start(bf16[128,896]{1,0:T(8,128)(2,1)S(1)} %get-tuple-element.19), channel_id=1, source_target_pairs={{0,1},{1,2},{2,3},{3,4},{4,5},{5,6},{6,7},{7,256},{8,9},{9,10},{10... | collective-permute-start | bytes 688136 | tf_op jit(solution)/shard_map/ppermute | solution.py:74
  92.9 9.8 %collective-permute-start.3 = (bf16[128,896]{1,0:T(8,128)(2,1)S(1)}, bf16[128,896]{1,0:T(8,128)(2,1)S(1)}, u32[]{:S(2)}, u32[]{:S(2)}) collective-permute-start(bf16[128,896]{1,0:T(8,128)(2,1)S(1)} %sums.3), channel_id=1, source_target_pairs={{0,1},{1,2},{2,3},{3,4},{4,5},{5,6},{6,7},{7,256},{8,9},{9,10},{10... | collective-permute-start | bytes 688136 | tf_op jit(solution)/shard_map/ppermute | solution.py:74
  104.8 17.0 %copy-start.18 = (bf16[128,896]{1,0:T(8,128)(2,1)S(1)}, bf16[128,896]{1,0:T(8,128)(2,1)}, u32[]{:S(2)}) copy-start(bf16[128,896]{1,0:T(8,128)(2,1)} %copy-done.17) | copy-start | bytes 688132
  104.8 43.1 %all-to-all-start.2 = ((bf16[16,64,1024]{2,1,0:T(8,128)(2,1)}), bf16[16,64,1024]{2,1,0:T(8,128)(2,1)S(1)}, u32[]{:S(2)}, u32[]{:S(2)}) async-start(bf16[16,64,1024]{2,1,0:T(8,128)(2,1)} %copies.3), calls=%async_computation.2 | async-start | bytes 4194304 | tf_op jit(solution)/shard_map/all_to_all | solution.py:119
  113.6 8.1 %collective-permute-start.4 = (bf16[128,896]{1,0:T(8,128)(2,1)}, bf16[128,896]{1,0:T(8,128)(2,1)S(1)}, u32[]{:S(2)}, u32[]{:S(2)}) collective-permute-start(bf16[128,896]{1,0:T(8,128)(2,1)} %copy-done.21), channel_id=1, source_target_pairs={{0,263},{1,0},{2,1},{3,2},{4,3},{5,4},{6,5},{7,6},{8,271},{9,8},{1... | collective-permute-start | bytes 688136 | tf_op jit(solution)/shard_map/ppermute | solution.py:74
  121.9 9.1 %collective-permute-start.5 = (bf16[128,896]{1,0:T(8,128)(2,1)S(1)}, bf16[128,896]{1,0:T(8,128)(2,1)S(1)}, u32[]{:S(2)}, u32[]{:S(2)}) collective-permute-start(bf16[128,896]{1,0:T(8,128)(2,1)S(1)} %get-tuple-element.24), channel_id=1, source_target_pairs={{0,1},{1,2},{2,3},{3,4},{4,5},{5,6},{6,7},{7,256},{8,9},{9,10},{10... | collective-permute-start | bytes 688136 | tf_op jit(solution)/shard_map/ppermute | solution.py:74
  123.8 8.7 %collective-permute-start.6 = (bf16[128,896]{1,0:T(8,128)(2,1)S(1)}, bf16[128,896]{1,0:T(8,128)(2,1)S(1)}, u32[]{:S(2)}, u32[]{:S(2)}) collective-permute-start(bf16[128,896]{1,0:T(8,128)(2,1)S(1)} %get-tuple-element.26), channel_id=1, source_target_pairs={{0,263},{1,0},{2,1},{3,2},{4,3},{5,4},{6,5},{7,6},{8,271},{9,8},{1... | collective-permute-start | bytes 688136 | tf_op jit(solution)/shard_map/ppermute | solution.py:74
  132.6 23.9 %collective-permute-start.7 = (bf16[128,896]{1,0:T(8,128)(2,1)S(1)}, bf16[128,896]{1,0:T(8,128)(2,1)S(1)}, u32[]{:S(2)}, u32[]{:S(2)}) collective-permute-start(bf16[128,896]{1,0:T(8,128)(2,1)S(1)} %get-tuple-element.28), channel_id=1, source_target_pairs={{0,1},{1,2},{2,3},{3,4},{4,5},{5,6},{6,7},{7,256},{8,9},{9,10},{10... | collective-permute-start | bytes 688136 | tf_op jit(solution)/shard_map/ppermute | solution.py:74
  134.5 22.0 %collective-permute-start.8 = (bf16[128,896]{1,0:T(8,128)(2,1)S(1)}, bf16[128,896]{1,0:T(8,128)(2,1)S(1)}, u32[]{:S(2)}, u32[]{:S(2)}) collective-permute-start(bf16[128,896]{1,0:T(8,128)(2,1)S(1)} %get-tuple-element.29), channel_id=1, source_target_pairs={{0,263},{1,0},{2,1},{3,2},{4,3},{5,4},{6,5},{7,6},{8,271},{9,8},{1... | collective-permute-start | bytes 688136 | tf_op jit(solution)/shard_map/ppermute | solution.py:74
  140.1 2.0 %copy-start.2 = (bf16[2048,896]{1,0:T(8,128)(2,1)S(1)}, bf16[2048,896]{1,0:T(8,128)(2,1)}, u32[]{:S(2)}) copy-start(bf16[2048,896]{1,0:T(8,128)(2,1)} %all-gather.2.cloned.1.call-done.hid_ref) | copy-start | bytes 11010052
  142.2 1.5 copy-start.9
  146.5 1.3 copy-start
  147.9 1.4 copy-start.6
  149.2 30.6 %all-to-all-start = ((bf16[16,64,1024]{2,1,0:T(8,128)(2,1)}), bf16[16,64,1024]{2,1,0:T(8,128)(2,1)S(1)}, u32[]{:S(2)}, u32[]{:S(2)}) async-start(bf16[16,64,1024]{2,1,0:T(8,128)(2,1)} %bitcast.7), calls=%async_computation | async-start | bytes 4194304 | tf_op jit(solution)/shard_map/all_to_all | solution.py:119
  156.5 1.6 copy-start.1
  158.1 2.0 %copy-start.3 = (bf16[2048,896]{1,0:T(8,128)(2,1)S(1)}, bf16[2048,896]{1,0:T(8,128)(2,1)}, u32[]{:S(2)}) copy-start(bf16[2048,896]{1,0:T(8,128)(2,1)} %all-gather.2.cloned.1.call-done.hid_ref) | copy-start | bytes 11010052
  160.1 1.6 copy-start.5
  161.7 1.6 copy-start.7
  169.1 5.7 %collective-permute-start.9 = (bf16[896,1024]{1,0:T(8,128)(2,1)S(1)}, bf16[896,1024]{1,0:T(8,128)(2,1)S(1)}, u32[]{:S(2)}, u32[]{:S(2)}) collective-permute-start(bf16[896,1024]{1,0:T(8,128)(2,1)S(1)} %weight_terms.1.a_ref), channel_id=1, source_target_pairs={{0,128},{1,129},{2,130},{3,131},{4,132},{5,133},{6,134},{7,135},{8... | collective-permute-start | bytes 5505032 | tf_op jit(solution)/shard_map/ppermute | solution.py:74
  176.6 4.8 %copy-start.11 = (bf16[128,896]{1,0:T(8,128)(2,1)S(1)}, bf16[128,896]{1,0:T(8,128)(2,1)}, u32[]{:S(2)}) copy-start(bf16[128,896]{1,0:T(8,128)(2,1)} %gate_ref.3) | copy-start | bytes 688132
  176.6 4.8 %copy-start.13 = (bf16[128,896]{1,0:T(8,128)(2,1)S(1)}, bf16[128,896]{1,0:T(8,128)(2,1)}, u32[]{:S(2)}) copy-start(bf16[128,896]{1,0:T(8,128)(2,1)} %up_ref.3) | copy-start | bytes 688132
  181.5 0.9 copy-start.16
Sparse Core Ops, SparseCore 0:
  10.7 92.2 all-gather.1

commit v6 on v3

--- a/solution.py
+++ b/solution.py
@@ -64,6 +64,7 @@
 VMEM = pl.BlockSpec(memory_space=pltpu.VMEM)
 ANY = pl.BlockSpec(memory_space=pl.ANY)
 PARAMS = pltpu.CompilerParams(vmem_limit_bytes=VMEM_LIMIT)
+ALONE = pltpu.CompilerParams(vmem_limit_bytes=60 * 2**20)
 
 
 def cost(flops, mib):
@@ -74,19 +75,36 @@
     return lax.ppermute(a, AXES, perm)
 
 
-def hidden_kernel(gate_ref, up_ref, out_ref):
-    g = gate_ref[...].astype(F32)
-    out_ref[...] = (g * jax.nn.sigmoid(g) * up_ref[...].astype(F32)).astype(BF)
+def started(moves):
+    for m in moves:
+        m.start()
+    return moves
+
+
+def hidden_kernel(gate_ref, up_ref, out_ref, g_ref, u_ref, sems):
+    moves = started(
+        [
+            pltpu.make_async_copy(src.at[pl.ds(64 * i, 64)], dst.at[pl.ds(64 * i, 64)], sems.at[2 * i + n])
+            for i in range(2)
+            for n, (src, dst) in enumerate(((gate_ref, g_ref), (up_ref, u_ref)))
+        ]
+    )
+    for i in range(2):
+        moves[2 * i].wait()
+        moves[2 * i + 1].wait()
+        s = slice(64 * i, 64 * i + 64)
+        g = g_ref[s].astype(F32)
+        out_ref[s] = (g * jax.nn.sigmoid(g) * u_ref[s].astype(F32)).astype(BF)
 
 
 def hidden_of(gate, up):
     return pl.pallas_call(
         hidden_kernel,
         out_shape=jax.ShapeDtypeStruct(gate.shape, BF),
-        grid=(4,),
-        in_specs=[pl.BlockSpec((32, 896), lambda i: (i, 0))] * 2,
-        out_specs=pl.BlockSpec((32, 896), lambda i: (i, 0)),
-        compiler_params=PARAMS,
+        in_specs=[ANY, ANY],
+        out_specs=VMEM,
+        scratch_shapes=[pltpu.VMEM((128, 896), BF), pltpu.VMEM((128, 896), BF), pltpu.SemaphoreType.DMA((4,))],
+        compiler_params=ALONE,
         cost_estimate=cost(2**20, 1),
         name="hidden",
     )(gate, up)
@@ -296,7 +314,7 @@
     grad_gate, grad_up = ends_of(gate, up, here, b, c, d, e, output)
 
     part = grad_of(pos, hid, near, rest, o, a, b)
-    grad_weight = pair_of(part, send(part, SWAP_CORE), output)
+    grad_weight = pair_of(part, send(part, SWAP_CORE))
     return output, grad_gate, grad_up, grad_weight
 
 

time: 173 us -> 173 us (level)
  waiting for transfers between devices: 51.1 us -> 56.9 us
  Pallas kernels: 27.3 us -> 24.5 us
  local copies, waits for them, and re-layouts: 18.1 us -> 16.3 us
    ppermute x8, waiting for transfers between devices: 4.25 us -> 9.27 us  [send(): return lax.ppermute(a, AXES, perm)]
    all_to_all x3, starting transfers between devices: 24 us -> 21.9 us  [exchange(): return lax.all_to_all(blocks, PLANE, 0, 0, tiled=True)]
    pallas_call x1, Pallas kernels: 3.89 us -> 1.93 us  [pair_of(): pl.pallas_call(pair_kernel, grid=(4,), out_shape=jax.ShapeDtypeStruct((89...]
    unnamed x38 -> x34, local copies, waits for them, and re-layouts: 18 us -> 16.2 us
  transfers between devices with their start and end apart: 12 -> 12, of which waited for: 4 -> 5; matrix products, arithmetic and copies ran while one was open for 0% -> 0% of each run, Pallas kernels for 14% -> 13%
where the time goes in v6:
time: 173 us; the launch traced here: 172 us
  starting transfers between devices  59.6 us (34%)
  waiting for transfers between devices  56.9 us (33%)
  Pallas kernels  24.5 us (14%)
  local copies, waits for them, and re-layouts  16.3 us (9%)
  between operations  14.2 us (8%)
    ppermute x8, starting transfers between devices, send(): return lax.ppermute(a, AXES, perm)  37.7 us
    all_to_all x3, waiting for transfers between devices, exchange(): return lax.all_to_all(blocks, PLANE, 0, 0, tiled=True)  26.4 us
    all_to_all x3, starting transfers between devices, exchange(): return lax.all_to_all(blocks, PLANE, 0, 0, tiled=True)  21.9 us
    all_gather x1, waiting for transfers between devices, per_device(): hid = lax.all_gather(hidden_of(gate, up), RING, axis=0, tiled=True)  21.2 us
    unnamed x34, local copies, waits for them, and re-layouts  16.2 us
    ppermute x8, waiting for transfers between devices, send(): return lax.ppermute(a, AXES, perm)  9.27 us
    pallas_call x1, Pallas kernels, grad_of(): pl.pallas_call(grad_kernel, grid=(4,), out_shape=jax.ShapeDtypeStruct((89...  6.85 us
    pallas_call x1, Pallas kernels, total_of(): pl.pallas_call(total_kernel, grid=(4,), out_shape=jax.ShapeDtypeStruct((6...  3.58 us
  transfers between devices with their start and end apart: 12, of which 5 were waited for; matrix products, arithmetic and copies ran while one was open for 0% of the time, Pallas kernels for 13%

profile of v6, /device:TPU:6, one launch (start us, length us, event | category | flops | bytes accessed | tf_op | source)
XLA Modules:
  0.0 171.6 jit_solution(11330097347081312882)
XLA Ops:
  7.2 0.0 all-gather.2.cloned.1.call-start
  7.2 1.8 %hidden.1 = bf16[128,896]{1,0:T(8,128)(2,1)} custom-call(bf16[128,896]{1,0:T(8,128)(2,1)} %gate_ref.3, bf16[128,896]{1,0:T(8,128)(2,1)} %up_ref.3), custom_call_target="tpu_custom_call" | custom-call | flops 1048576 | bytes 1048576 | tf_op jit(solution)/shard_map/hidden/pallas_call | solution.py:101
  9.1 0.0 all-gather.2.cloned.1.call-update
  9.1 15.7 %collective-permute-start = (bf16[64,1024]{1,0:T(8,128)(2,1)}, bf16[64,1024]{1,0:T(8,128)(2,1)S(1)}, u32[]{:S(2)}, u32[]{:S(2)}) collective-permute-start(bf16[64,1024]{1,0:T(8,128)(2,1)} %cot_ref.3), channel_id=1, source_target_pairs={{4,260},{5,261},{6,262},{7,263},{12,268},{13,269},{14,270},{15,271... | collective-permute-start | bytes 393224 | tf_op jit(solution)/shard_map/ppermute | solution.py:75
  24.8 0.1 stack.23.pos_ref
  24.9 3.6 %collective-permute-done.far_ref = bf16[64,1024]{1,0:T(8,128)(2,1)S(1)} collective-permute-done((bf16[64,1024]{1,0:T(8,128)(2,1)}, bf16[64,1024]{1,0:T(8,128)(2,1)S(1)}, u32[]{:S(2)}, u32[]{:S(2)}) %collective-permute-start) | collective-permute-done | bytes 131104 | tf_op jit(solution)/shard_map/ppermute | solution.py:75
  28.5 0.9 copy-done.10
  29.4 2.0 %copies.2 = bf16[16,64,1024]{2,1,0:T(8,128)(2,1)} custom-call(s32[5]{0:T(128)S(1)} %stack.23.pos_ref, bf16[64,1024]{1,0:T(8,128)(2,1)S(1)} %copy-done.10, bf16[64,1024]{1,0:T(8,128)(2,1)S(1)} %collective-permute-done.far_ref), custom_call_target="tpu_custom_call" | custom-call | bytes 2097152 | tf_op jit(solution)/shard_map/copies/pallas_call | solution.py:125
  31.4 7.6 %all-to-all-start.1 = ((bf16[16,64,1024]{2,1,0:T(8,128)(2,1)}), bf16[16,64,1024]{2,1,0:T(8,128)(2,1)S(1)}, u32[]{:S(2)}, u32[]{:S(2)}) async-start(bf16[16,64,1024]{2,1,0:T(8,128)(2,1)} %copies.2), calls=%async_computation.1 | async-start | bytes 4194304 | tf_op jit(solution)/shard_map/all_to_all | solution.py:137
  39.0 0.7 collective-permute-start.1
  39.7 0.0 collective-permute-done.1.far_ref
  39.7 26.4 %all-to-all-done.1.refs_0_.near_ref = bf16[16,64,1024]{2,1,0:T(8,128)(2,1)S(1)} async-done(((bf16[16,64,1024]{2,1,0:T(8,128)(2,1)}), bf16[16,64,1024]{2,1,0:T(8,128)(2,1)S(1)}, u32[]{:S(2)}, u32[]{:S(2)}) %all-to-all-start.1) | async-done | bytes 2097184 | tf_op jit(solution)/shard_map/all_to_all | solution.py:137
  66.1 0.7 copies.3.refs_0_
  66.8 1.3 copy-done
  68.2 6.5 %all-to-all-start.2 = ((bf16[16,64,1024]{2,1,0:T(8,128)(2,1)}), bf16[16,64,1024]{2,1,0:T(8,128)(2,1)}, u32[]{:S(2)}, u32[]{:S(2)}) async-start(bf16[16,64,1024]{2,1,0:T(8,128)(2,1)} %copy-done), calls=%async_computation.2 | async-start | bytes 4194304 | tf_op jit(solution)/shard_map/all_to_all | solution.py:137
  74.7 1.6 copy-done.1
  76.3 1.5 copy-done.6
  77.8 3.5 %hidden_terms.1 = (bf16[256,896]{1,0:T(8,128)(2,1)}, bf16[256,896]{1,0:T(8,128)(2,1)}, bf16[128,896]{1,0:T(8,128)(2,1)S(1)}, bf16[128,896]{1,0:T(8,128)(2,1)S(1)...) custom-call(s32[5]{0:T(128)S(1)} %stack.23.pos_ref, bf16[8,128,1024]{2,1,0:T(8,128)(2,1)S(1)} %bitcast.7, ...), custom_call_target="tpu_custom_call" | custom-call | flops 1879048192 | bytes 8388608 | tf_op jit(solution)/shard_map/hidden_terms/pallas_call | solution.py:161
  81.3 0.7 copy-done.13
  82.0 0.7 copy-done.15
  82.7 8.1 %collective-permute-start.2 = (bf16[256,896]{1,0:T(8,128)(2,1)}, bf16[256,896]{1,0:T(8,128)(2,1)S(1)}, u32[]{:S(2)}, u32[]{:S(2)}) collective-permute-start(bf16[256,896]{1,0:T(8,128)(2,1)} %get-tuple-element.16), channel_id=1, source_target_pairs={{0,262},{1,263},{2,0},{3,1},{4,2},{5,3},{6,4},{7,5},{8,270},{9,271... | collective-permute-start | bytes 1376264 | tf_op jit(solution)/shard_map/ppermute | solution.py:75
  90.8 1.9 %collective-permute-start.3 = (bf16[256,896]{1,0:T(8,128)(2,1)}, bf16[256,896]{1,0:T(8,128)(2,1)S(1)}, u32[]{:S(2)}, u32[]{:S(2)}) collective-permute-start(bf16[256,896]{1,0:T(8,128)(2,1)} %get-tuple-element.17), channel_id=1, source_target_pairs={{0,2},{1,3},{2,4},{3,5},{4,6},{5,7},{6,256},{7,257},{8,10},{9,11},... | collective-permute-start | bytes 1376264 | tf_op jit(solution)/shard_map/ppermute | solution.py:75
  92.7 21.2 %all-gather.2.cloned.1.call-done.hid_ref = bf16[2048,896]{1,0:T(8,128)(2,1)} async-done(((bf16[128,896]{1,0:T(8,128)(2,1)}), bf16[2048,896]{1,0:T(8,128)(2,1)}) %all-gather.2.cloned.1.call-update) | async-done | bytes 3670032 | tf_op jit(solution)/shard_map/all_gather | solution.py:302
  113.9 2.0 %copy-done.4 = bf16[2048,896]{1,0:T(8,128)(2,1)S(1)} copy-done((bf16[2048,896]{1,0:T(8,128)(2,1)S(1)}, bf16[2048,896]{1,0:T(8,128)(2,1)}, u32[]{:S(2)}) %copy-start.4) | copy-done | bytes 3670040
  116.0 1.5 copy-done.7
  117.5 2.9 %output_terms.1.refs_0_ = bf16[1024,1024]{1,0:T(8,128)(2,1)S(1)} custom-call(s32[5]{0:T(128)S(1)} %stack.23.pos_ref, bf16[2048,896]{1,0:T(8,128)(2,1)S(1)} %copy-done.4, bf16[896,1024]{1,0:T(8,128)(2,1)S(1)} %copy-done.7), custom_call_target="tpu_custom_call" | custom-call | flops 1879048192 | bytes 8388608 | tf_op jit(solution)/shard_map/output_terms/pallas_call | solution.py:180
  120.4 1.3 copy-done.2
  121.7 0.0 all-to-all-done.2.rest_ref
  121.7 7.9 %all-to-all-start = ((bf16[16,64,1024]{2,1,0:T(8,128)(2,1)}), bf16[16,64,1024]{2,1,0:T(8,128)(2,1)}, u32[]{:S(2)}, u32[]{:S(2)}) async-start(bf16[16,64,1024]{2,1,0:T(8,128)(2,1)} %bitcast.8), calls=%async_computation | async-start | bytes 4194304 | tf_op jit(solution)/shard_map/all_to_all | solution.py:137
  129.6 0.0 collective-permute-done.2.b_ref.refs_2_
  129.6 0.0 collective-permute-done.3.a_ref.refs_1_
  129.6 1.6 copy-done.3
  131.2 2.0 %copy-done.5 = bf16[2048,896]{1,0:T(8,128)(2,1)S(1)} copy-done((bf16[2048,896]{1,0:T(8,128)(2,1)S(1)}, bf16[2048,896]{1,0:T(8,128)(2,1)}, u32[]{:S(2)}) %copy-start.5) | copy-done | bytes 3670040
  133.2 6.9 %weight_terms.1.a_ref = bf16[896,1024]{1,0:T(8,128)(2,1)S(1)} custom-call(s32[5]{0:T(128)S(1)} %stack.23.pos_ref, bf16[2048,896]{1,0:T(8,128)(2,1)S(1)} %copy-done.5, bf16[16,64,1024]{2,1,0:T(8,128)(2,1)S(1)} %all-to-all-done.1.refs_0_.near_ref, bf16[16,64,1024]{2,1,0:T(8,128)(2,1)} %all-to-all-done.2.rest_ref, bf16[1024,1024]{1,0:T(8,128)(2,1)S(1)} %copy-done.3, ...), custom_call_target="tpu_custom_call" | custom-call | flops 3758096384 | bytes 10485760 | tf_op jit(solution)/shard_map/weight_terms/pallas_call | solution.py:229
  140.1 1.9 %collective-permute-start.7 = (bf16[896,1024]{1,0:T(8,128)(2,1)S(1)}, bf16[896,1024]{1,0:T(8,128)(2,1)S(1)}, u32[]{:S(2)}, u32[]{:S(2)}) collective-permute-start(bf16[896,1024]{1,0:T(8,128)(2,1)S(1)} %weight_terms.1.a_ref), channel_id=1, source_target_pairs={{0,128},{1,129},{2,130},{3,131},{4,132},{5,133},{6,134},{7,135},{8... | collective-permute-start | bytes 5505032 | tf_op jit(solution)/shard_map/ppermute | solution.py:75
  142.0 0.2 sums.1
  142.2 2.3 %collective-permute-start.4 = (bf16[128,896]{1,0:T(8,128)(2,1)S(1)}, bf16[128,896]{1,0:T(8,128)(2,1)S(1)}, u32[]{:S(2)}, u32[]{:S(2)}) collective-permute-start(bf16[128,896]{1,0:T(8,128)(2,1)S(1)} %get-tuple-element.21), channel_id=1, source_target_pairs={{0,2},{1,3},{2,4},{3,5},{4,6},{5,7},{6,256},{7,257},{8,10},{9,11},... | collective-permute-start | bytes 688136 | tf_op jit(solution)/shard_map/ppermute | solution.py:75
  144.5 2.0 %collective-permute-start.5 = (bf16[128,896]{1,0:T(8,128)(2,1)S(1)}, bf16[128,896]{1,0:T(8,128)(2,1)S(1)}, u32[]{:S(2)}, u32[]{:S(2)}) collective-permute-start(bf16[128,896]{1,0:T(8,128)(2,1)S(1)} %get-tuple-element.22), channel_id=1, source_target_pairs={{0,1},{1,2},{2,3},{3,4},{4,5},{5,6},{6,7},{7,256},{8,9},{9,10},{10... | collective-permute-start | bytes 688136 | tf_op jit(solution)/shard_map/ppermute | solution.py:75
  146.5 5.0 %collective-permute-start.6 = (bf16[128,896]{1,0:T(8,128)(2,1)S(1)}, bf16[128,896]{1,0:T(8,128)(2,1)S(1)}, u32[]{:S(2)}, u32[]{:S(2)}) collective-permute-start(bf16[128,896]{1,0:T(8,128)(2,1)S(1)} %get-tuple-element.23), channel_id=1, source_target_pairs={{0,263},{1,0},{2,1},{3,2},{4,3},{5,4},{6,5},{7,6},{8,271},{9,8},{1... | collective-permute-start | bytes 688136 | tf_op jit(solution)/shard_map/ppermute | solution.py:75
  151.6 1.9 %weight_sum.1 = bf16[896,1024]{1,0:T(8,128)(2,1)} custom-call(bf16[896,1024]{1,0:T(8,128)(2,1)S(1)} %weight_terms.1.a_ref, bf16[896,1024]{1,0:T(8,128)(2,1)S(1)} %collective-permute-done.7.b_ref), custom_call_target="tpu_custom_call" | custom-call | flops 1048576 | bytes 5242880 | tf_op jit(solution)/shard_map/weight_sum/pallas_call | solution.py:248
  153.5 0.0 all-to-all-done.got_ref
  153.5 3.6 %output_sum.1.refs_0_ = bf16[64,1024]{1,0:T(8,128)(2,1)} custom-call(bf16[16,64,1024]{2,1,0:T(8,128)(2,1)} %all-to-all-done.got_ref), custom_call_target="tpu_custom_call" | custom-call | flops 1048576 | bytes 2097152 | tf_op jit(solution)/shard_map/output_sum/pallas_call | solution.py:199
  157.1 2.5 %collective-permute-done.4.c_ref = bf16[128,896]{1,0:T(8,128)(2,1)S(1)} collective-permute-done((bf16[128,896]{1,0:T(8,128)(2,1)S(1)}, bf16[128,896]{1,0:T(8,128)(2,1)S(1)}, u32[]{:S(2)}, u32[]{:S(2)}) %collective-permute-start.4) | collective-permute-done | bytes 229408 | tf_op jit(solution)/shard_map/ppermute | solution.py:75
  159.5 3.2 %collective-permute-done.5.d_ref = bf16[128,896]{1,0:T(8,128)(2,1)S(1)} collective-permute-done((bf16[128,896]{1,0:T(8,128)(2,1)S(1)}, bf16[128,896]{1,0:T(8,128)(2,1)S(1)}, u32[]{:S(2)}, u32[]{:S(2)}) %collective-permute-start.5) | collective-permute-done | bytes 229408 | tf_op jit(solution)/shard_map/ppermute | solution.py:75
  162.7 0.0 collective-permute-done.6.e_ref
  162.8 0.0 copy-start.12
  162.8 0.9 copy-done.12
  163.7 1.1 gradients.1
  (22 shorter events, 0.0 us)
Async XLA Ops:
  7.2 106.8 %all-gather.2.cloned.1.call-start = ((), (), s32[]{:S(2)}) async-start(), calls=%async_computation.3 | async-start | bytes 3899392 | tf_op jit(solution)/shard_map/all_gather | solution.py:302
  9.1 19.4 %collective-permute-start = (bf16[64,1024]{1,0:T(8,128)(2,1)}, bf16[64,1024]{1,0:T(8,128)(2,1)S(1)}, u32[]{:S(2)}, u32[]{:S(2)}) collective-permute-start(bf16[64,1024]{1,0:T(8,128)(2,1)} %cot_ref.3), channel_id=1, source_target_pairs={{4,260},{5,261},{6,262},{7,263},{12,268},{13,269},{14,270},{15,271... | collective-permute-start | bytes 393224 | tf_op jit(solution)/shard_map/ppermute | solution.py:75
  28.5 0.9 copy-start.10
  31.4 7.6 %copy-start.11 = (bf16[64,1024]{1,0:T(8,128)(2,1)S(1)}, bf16[64,1024]{1,0:T(8,128)(2,1)}, u32[]{:S(2)}) copy-start(bf16[64,1024]{1,0:T(8,128)(2,1)} %cot_ref.3) | copy-start | bytes 393220
  31.4 34.7 %all-to-all-start.1 = ((bf16[16,64,1024]{2,1,0:T(8,128)(2,1)}), bf16[16,64,1024]{2,1,0:T(8,128)(2,1)S(1)}, u32[]{:S(2)}, u32[]{:S(2)}) async-start(bf16[16,64,1024]{2,1,0:T(8,128)(2,1)} %copies.2), calls=%async_computation.1 | async-start | bytes 4194304 | tf_op jit(solution)/shard_map/all_to_all | solution.py:137
  39.0 0.7 collective-permute-start.1
  66.8 1.4 copy-start
  68.2 53.5 %all-to-all-start.2 = ((bf16[16,64,1024]{2,1,0:T(8,128)(2,1)}), bf16[16,64,1024]{2,1,0:T(8,128)(2,1)}, u32[]{:S(2)}, u32[]{:S(2)}) async-start(bf16[16,64,1024]{2,1,0:T(8,128)(2,1)} %copy-done), calls=%async_computation.2 | async-start | bytes 4194304 | tf_op jit(solution)/shard_map/all_to_all | solution.py:137
  74.7 1.6 copy-start.1
  76.3 1.5 copy-start.6
  81.3 0.7 copy-start.13
  82.0 0.7 copy-start.15
  82.7 46.9 %collective-permute-start.2 = (bf16[256,896]{1,0:T(8,128)(2,1)}, bf16[256,896]{1,0:T(8,128)(2,1)S(1)}, u32[]{:S(2)}, u32[]{:S(2)}) collective-permute-start(bf16[256,896]{1,0:T(8,128)(2,1)} %get-tuple-element.16), channel_id=1, source_target_pairs={{0,262},{1,263},{2,0},{3,1},{4,2},{5,3},{6,4},{7,5},{8,270},{9,271... | collective-permute-start | bytes 1376264 | tf_op jit(solution)/shard_map/ppermute | solution.py:75
  90.8 38.8 %collective-permute-start.3 = (bf16[256,896]{1,0:T(8,128)(2,1)}, bf16[256,896]{1,0:T(8,128)(2,1)S(1)}, u32[]{:S(2)}, u32[]{:S(2)}) collective-permute-start(bf16[256,896]{1,0:T(8,128)(2,1)} %get-tuple-element.17), channel_id=1, source_target_pairs={{0,2},{1,3},{2,4},{3,5},{4,6},{5,7},{6,256},{7,257},{8,10},{9,11},... | collective-permute-start | bytes 1376264 | tf_op jit(solution)/shard_map/ppermute | solution.py:75
  113.9 2.0 %copy-start.4 = (bf16[2048,896]{1,0:T(8,128)(2,1)S(1)}, bf16[2048,896]{1,0:T(8,128)(2,1)}, u32[]{:S(2)}) copy-start(bf16[2048,896]{1,0:T(8,128)(2,1)} %all-gather.2.cloned.1.call-done.hid_ref) | copy-start | bytes 11010052
  116.0 1.5 copy-start.7
  120.4 1.3 copy-start.2
  121.7 31.8 %all-to-all-start = ((bf16[16,64,1024]{2,1,0:T(8,128)(2,1)}), bf16[16,64,1024]{2,1,0:T(8,128)(2,1)}, u32[]{:S(2)}, u32[]{:S(2)}) async-start(bf16[16,64,1024]{2,1,0:T(8,128)(2,1)} %bitcast.8), calls=%async_computation | async-start | bytes 4194304 | tf_op jit(solution)/shard_map/all_to_all | solution.py:137
  129.6 1.6 copy-start.3
  131.2 2.0 %copy-start.5 = (bf16[2048,896]{1,0:T(8,128)(2,1)S(1)}, bf16[2048,896]{1,0:T(8,128)(2,1)}, u32[]{:S(2)}) copy-start(bf16[2048,896]{1,0:T(8,128)(2,1)} %all-gather.2.cloned.1.call-done.hid_ref) | copy-start | bytes 11010052
  133.2 8.8 %copy-start.14 = (bf16[128,896]{1,0:T(8,128)(2,1)S(1)}, bf16[128,896]{1,0:T(8,128)(2,1)}, u32[]{:S(2)}) copy-start(bf16[128,896]{1,0:T(8,128)(2,1)} %copy-done.13) | copy-start | bytes 688132
  140.1 11.4 %collective-permute-start.7 = (bf16[896,1024]{1,0:T(8,128)(2,1)S(1)}, bf16[896,1024]{1,0:T(8,128)(2,1)S(1)}, u32[]{:S(2)}, u32[]{:S(2)}) collective-permute-start(bf16[896,1024]{1,0:T(8,128)(2,1)S(1)} %weight_terms.1.a_ref), channel_id=1, source_target_pairs={{0,128},{1,129},{2,130},{3,131},{4,132},{5,133},{6,134},{7,135},{8... | collective-permute-start | bytes 5505032 | tf_op jit(solution)/shard_map/ppermute | solution.py:75
  142.2 17.3 %collective-permute-start.4 = (bf16[128,896]{1,0:T(8,128)(2,1)S(1)}, bf16[128,896]{1,0:T(8,128)(2,1)S(1)}, u32[]{:S(2)}, u32[]{:S(2)}) collective-permute-start(bf16[128,896]{1,0:T(8,128)(2,1)S(1)} %get-tuple-element.21), channel_id=1, source_target_pairs={{0,2},{1,3},{2,4},{3,5},{4,6},{5,7},{6,256},{7,257},{8,10},{9,11},... | collective-permute-start | bytes 688136 | tf_op jit(solution)/shard_map/ppermute | solution.py:75
  144.5 18.3 %collective-permute-start.5 = (bf16[128,896]{1,0:T(8,128)(2,1)S(1)}, bf16[128,896]{1,0:T(8,128)(2,1)S(1)}, u32[]{:S(2)}, u32[]{:S(2)}) collective-permute-start(bf16[128,896]{1,0:T(8,128)(2,1)S(1)} %get-tuple-element.22), channel_id=1, source_target_pairs={{0,1},{1,2},{2,3},{3,4},{4,5},{5,6},{6,7},{7,256},{8,9},{9,10},{10... | collective-permute-start | bytes 688136 | tf_op jit(solution)/shard_map/ppermute | solution.py:75
  146.5 16.2 %collective-permute-start.6 = (bf16[128,896]{1,0:T(8,128)(2,1)S(1)}, bf16[128,896]{1,0:T(8,128)(2,1)S(1)}, u32[]{:S(2)}, u32[]{:S(2)}) collective-permute-start(bf16[128,896]{1,0:T(8,128)(2,1)S(1)} %get-tuple-element.23), channel_id=1, source_target_pairs={{0,263},{1,0},{2,1},{3,2},{4,3},{5,4},{6,5},{7,6},{8,271},{9,8},{1... | collective-permute-start | bytes 688136 | tf_op jit(solution)/shard_map/ppermute | solution.py:75
  153.5 9.3 %copy-start.8 = (bf16[128,896]{1,0:T(8,128)(2,1)S(1)}, bf16[128,896]{1,0:T(8,128)(2,1)}, u32[]{:S(2)}) copy-start(bf16[128,896]{1,0:T(8,128)(2,1)} %gate_ref.3) | copy-start | bytes 688132
  153.5 9.3 %copy-start.9 = (bf16[128,896]{1,0:T(8,128)(2,1)S(1)}, bf16[128,896]{1,0:T(8,128)(2,1)}, u32[]{:S(2)}) copy-start(bf16[128,896]{1,0:T(8,128)(2,1)} %up_ref.3) | copy-start | bytes 688132
  153.5 9.3 %copy-start.16 = (bf16[128,896]{1,0:T(8,128)(2,1)S(1)}, bf16[128,896]{1,0:T(8,128)(2,1)}, u32[]{:S(2)}) copy-start(bf16[128,896]{1,0:T(8,128)(2,1)} %copy-done.15) | copy-start | bytes 688132
  162.8 0.9 copy-start.12
Sparse Core Ops, SparseCore 0:
  10.7 103.2 all-gather.1

commit v7 on v5

--- a/solution.py
+++ b/solution.py
@@ -64,6 +64,7 @@
 VMEM = pl.BlockSpec(memory_space=pltpu.VMEM)
 ANY = pl.BlockSpec(memory_space=pl.ANY)
 PARAMS = pltpu.CompilerParams(vmem_limit_bytes=VMEM_LIMIT)
+ALONE = pltpu.CompilerParams(vmem_limit_bytes=60 * 2**20)
 
 
 def cost(flops, mib):
@@ -74,19 +75,36 @@
     return lax.ppermute(a, AXES, perm)
 
 
-def hidden_kernel(gate_ref, up_ref, out_ref):
-    g = gate_ref[...].astype(F32)
-    out_ref[...] = (g * jax.nn.sigmoid(g) * up_ref[...].astype(F32)).astype(BF)
+def started(moves):
+    for m in moves:
+        m.start()
+    return moves
+
+
+def hidden_kernel(gate_ref, up_ref, out_ref, g_ref, u_ref, sems):
+    moves = started(
+        [
+            pltpu.make_async_copy(src.at[pl.ds(64 * i, 64)], dst.at[pl.ds(64 * i, 64)], sems.at[2 * i + n])
+            for i in range(2)
+            for n, (src, dst) in enumerate(((gate_ref, g_ref), (up_ref, u_ref)))
+        ]
+    )
+    for i in range(2):
+        moves[2 * i].wait()
+        moves[2 * i + 1].wait()
+        s = slice(64 * i, 64 * i + 64)
+        g = g_ref[s].astype(F32)
+        out_ref[s] = (g * jax.nn.sigmoid(g) * u_ref[s].astype(F32)).astype(BF)
 
 
 def hidden_of(gate, up):
     return pl.pallas_call(
         hidden_kernel,
         out_shape=jax.ShapeDtypeStruct(gate.shape, BF),
-        grid=(4,),
-        in_specs=[pl.BlockSpec((32, 896), lambda i: (i, 0))] * 2,
-        out_specs=pl.BlockSpec((32, 896), lambda i: (i, 0)),
-        compiler_params=PARAMS,
+        in_specs=[ANY, ANY],
+        out_specs=VMEM,
+        scratch_shapes=[pltpu.VMEM((128, 896), BF), pltpu.VMEM((128, 896), BF), pltpu.SemaphoreType.DMA((4,))],
+        compiler_params=ALONE,
         cost_estimate=cost(2**20, 1),
         name="hidden",
     )(gate, up)
@@ -103,7 +121,7 @@
     pl.when(jnp.logical_not(mine) if far_wanted else mine)(lambda: fill(cot_ref))
 
 
-def copies_of(pos, cot, far, far_wanted, *after):
+def copies_of(pos, cot, far_wanted, *after):
     return pl.pallas_call(
         functools.partial(copies_kernel, far_wanted),
         out_shape=jax.ShapeDtypeStruct((16, 64, 1024), BF),
@@ -112,7 +130,7 @@
         compiler_params=PARAMS,
         cost_estimate=cost(0, 2),
         name="copies",
-    )(pos, cot, far, *after)
+    )(pos, cot, send(cot, swap_z(far_wanted)), *after)
 
 
 def exchange(blocks):
@@ -252,48 +270,47 @@
     )(gate, up, here, a, b, *after)
 
 
-def add_kernel(*refs):
-    n = len(refs) // 3
+def add_kernel(n, *refs):
+    outs = refs[len(refs) - n :]
     for i in range(n):
-        refs[2 * n + i][...] = (refs[2 * i][...].astype(F32) + refs[2 * i + 1][...].astype(F32)).astype(BF)
-
-
-def add(*pairs_of):
+        outs[i][...] = (refs[2 * i][...].astype(F32) + refs[2 * i + 1][...].astype(F32)).astype(BF)
+
+
+def add(pairs_of, *after):
     out = pl.pallas_call(
-        add_kernel,
+        functools.partial(add_kernel, len(pairs_of)),
         out_shape=[jax.ShapeDtypeStruct((128, 896), BF)] * len(pairs_of),
-        in_specs=[VMEM] * (2 * len(pairs_of)),
+        in_specs=[VMEM] * (2 * len(pairs_of)) + [ANY] * len(after),
         out_specs=[VMEM] * len(pairs_of),
         compiler_params=PARAMS,
         cost_estimate=cost(2**18, 1),
         name="sums",
-    )(*[v for p in pairs_of for v in p])
+    )(*[v for p in pairs_of for v in p], *after)
     return out
 
 
 def per_device(gate, up, w, cot):
     pos = jnp.stack([lax.axis_index(a) for a in AXES]).astype(jnp.int32)
     hid = lax.all_gather(hidden_of(gate, up), RING, axis=0, tiled=True)
-    near = exchange(copies_of(pos, cot, send(cot, swap_z(False)), False))
-    far = send(cot, swap_z(True))
-    parts = ((4,), (3,), (-3,), (2,), (-2,), (1,), (-1,), (0,))
-    p4, p3, m3, p2, m2, p1, m1, here = terms_of(parts, pos, near, w, far)
+    near = exchange(copies_of(pos, cot, False))
+    rest = copies_of(pos, cot, True, near)
+    parts = ((4,), (-3,), (3,), (-2,), (2,), (-1,), (1,), (0,))
+    p4, m3, p3, m2, p2, m1, p1, here = terms_of(parts, pos, near, w, rest)
+    rest = exchange(rest)
 
     right, left = ring_move(1), ring_move(-1)
-    a = send(p4, right)
-    a, = add((a, p3))
-    a, b = send(a, right), send(m3, left)
-    rest = exchange(copies_of(pos, cot, far, True, a))
-    a, b = add((a, p2), (b, m2))
-    a, b = send(a, right), send(b, left)
-    a, b = add((a, p1), (b, m1))
-    a, b = send(a, right), send(b, left)
-
     o = out_of(pos, hid, w)
+    a1, b1 = send(p4, right), send(m3, left)
+    a, b = add(((a1, p3), (b1, m2)))
+    a2, b2 = send(a, right), send(b, left)
+    a, b = add(((a2, p2), (b2, m1)))
+    a3, b = send(a, right), send(b, left)
+    (a,) = add(((a3, p1),), o)
+    a = send(a, right)
     output = total_of(exchange(o.reshape(16, 64, 1024)))
     grad_gate, grad_up = ends_of(gate, up, here, a, b, output)
 
-    part = grad_of(pos, hid, near, rest, o, a, b)
+    part = grad_of(pos, hid, near, rest, o, a3, b)
     grad_weight = pair_of(part, send(part, SWAP_CORE))
     return output, grad_gate, grad_up, grad_weight
 

time: 192 us -> 170 us (0.89)
  waiting for transfers between devices: 67.2 us -> 46.6 us
  local copies, waits for them, and re-layouts: 21.3 us -> 12 us
  Pallas kernels: 24 us -> 27.5 us
  starting transfers between devices: 63.4 us -> 66.7 us
    ppermute x10, waiting for transfers between devices: 38.2 us -> 13.1 us  [send(): return lax.ppermute(a, AXES, perm)]
    unnamed x44 -> x22, local copies, waits for them, and re-layouts: 21.2 us -> 11.9 us
    ppermute x10, starting transfers between devices: 39.8 us -> 45.2 us  [send(): return lax.ppermute(a, AXES, perm)]
    all_to_all x3, waiting for transfers between devices: 29 us -> 33.5 us  [exchange(): return lax.all_to_all(blocks, PLANE, 0, 0, tiled=True)]
    all_to_all x3, starting transfers between devices: 23.6 us -> 21.4 us  [exchange(): return lax.all_to_all(blocks, PLANE, 0, 0, tiled=True)]
  transfers between devices with their start and end apart: 14 -> 14, of which waited for: 9 -> 8; matrix products, arithmetic and copies ran while one was open for 0% -> 0% of each run, Pallas kernels for 11% -> 15%
where the time goes in v7:
time: 170 us; the launch traced here: 167 us
  starting transfers between devices  66.7 us (39%)
  waiting for transfers between devices  46.6 us (27%)
  Pallas kernels  27.5 us (16%)
  between operations  14.2 us (8%)
  local copies, waits for them, and re-layouts  12 us (7%)
    ppermute x10, starting transfers between devices, send(): return lax.ppermute(a, AXES, perm)  45.2 us
    all_to_all x3, waiting for transfers between devices, exchange(): return lax.all_to_all(blocks, PLANE, 0, 0, tiled=True)  33.5 us
    all_to_all x3, starting transfers between devices, exchange(): return lax.all_to_all(blocks, PLANE, 0, 0, tiled=True)  21.4 us
    ppermute x10, waiting for transfers between devices, send(): return lax.ppermute(a, AXES, perm)  13.1 us
    unnamed x22, local copies, waits for them, and re-layouts  11.9 us
    pallas_call x1, Pallas kernels, grad_of(): pl.pallas_call(grad_kernel, grid=(4,), out_shape=jax.ShapeDtypeStruct((89...  6.81 us
    pallas_call x1, Pallas kernels, terms_of(): pl.pallas_call(functools.partial(term_kernel, parts), out_shape=[jax.Shap...  5.19 us
    pallas_call x1, Pallas kernels, out_of(): pl.pallas_call(out_kernel, out_shape=jax.ShapeDtypeStruct((1024, 1024), B...  4.21 us
  transfers between devices with their start and end apart: 14, of which 8 were waited for; matrix products, arithmetic and copies ran while one was open for 0% of the time, Pallas kernels for 15%

profile of v7, /device:TPU:6, one launch (start us, length us, event | category | flops | bytes accessed | tf_op | source)
XLA Modules:
  0.0 167.0 jit_solution(12407473532021279446)
XLA Ops:
  7.2 0.0 all-gather.2.cloned.1.call-start
  7.2 1.8 %hidden.1 = bf16[128,896]{1,0:T(8,128)(2,1)} custom-call(bf16[128,896]{1,0:T(8,128)(2,1)} %gate_ref.3, bf16[128,896]{1,0:T(8,128)(2,1)} %up_ref.3), custom_call_target="tpu_custom_call" | custom-call | flops 1048576 | bytes 1048576 | tf_op jit(solution)/shard_map/hidden/pallas_call | solution.py:101
  9.1 0.0 all-gather.2.cloned.1.call-update
  9.1 15.7 %collective-permute-start = (bf16[64,1024]{1,0:T(8,128)(2,1)}, bf16[64,1024]{1,0:T(8,128)(2,1)S(1)}, u32[]{:S(2)}, u32[]{:S(2)}) collective-permute-start(bf16[64,1024]{1,0:T(8,128)(2,1)} %cot_ref.3), channel_id=1, source_target_pairs={{4,260},{5,261},{6,262},{7,263},{12,268},{13,269},{14,270},{15,271... | collective-permute-start | bytes 393224 | tf_op jit(solution)/shard_map/ppermute | solution.py:75
  24.8 0.1 stack.23.pos_ref
  24.9 3.6 %collective-permute-done.far_ref = bf16[64,1024]{1,0:T(8,128)(2,1)S(1)} collective-permute-done((bf16[64,1024]{1,0:T(8,128)(2,1)}, bf16[64,1024]{1,0:T(8,128)(2,1)S(1)}, u32[]{:S(2)}, u32[]{:S(2)}) %collective-permute-start) | collective-permute-done | bytes 131104 | tf_op jit(solution)/shard_map/ppermute | solution.py:75
  28.5 0.9 copy-done.8
  29.4 2.0 %copies.2 = bf16[16,64,1024]{2,1,0:T(8,128)(2,1)} custom-call(s32[5]{0:T(128)S(1)} %stack.23.pos_ref, bf16[64,1024]{1,0:T(8,128)(2,1)S(1)} %copy-done.8, bf16[64,1024]{1,0:T(8,128)(2,1)S(1)} %collective-permute-done.far_ref), custom_call_target="tpu_custom_call" | custom-call | bytes 2097152 | tf_op jit(solution)/shard_map/copies/pallas_call | solution.py:125
  31.4 7.6 %all-to-all-start.1 = ((bf16[16,64,1024]{2,1,0:T(8,128)(2,1)}), bf16[16,64,1024]{2,1,0:T(8,128)(2,1)S(1)}, u32[]{:S(2)}, u32[]{:S(2)}) async-start(bf16[16,64,1024]{2,1,0:T(8,128)(2,1)} %copies.2), calls=%async_computation.1 | async-start | bytes 4194304 | tf_op jit(solution)/shard_map/all_to_all | solution.py:137
  39.0 0.7 collective-permute-start.1
  39.7 0.0 collective-permute-done.1.far_ref
  39.7 26.4 %all-to-all-done.1.refs_0_.near_ref = bf16[16,64,1024]{2,1,0:T(8,128)(2,1)S(1)} async-done(((bf16[16,64,1024]{2,1,0:T(8,128)(2,1)}), bf16[16,64,1024]{2,1,0:T(8,128)(2,1)S(1)}, u32[]{:S(2)}, u32[]{:S(2)}) %all-to-all-start.1) | async-done | bytes 2097184 | tf_op jit(solution)/shard_map/all_to_all | solution.py:137
  66.1 0.7 copies.3.refs_0_
  66.8 1.4 copy-done
  68.2 6.5 %all-to-all-start.2 = ((bf16[16,64,1024]{2,1,0:T(8,128)(2,1)}), bf16[16,64,1024]{2,1,0:T(8,128)(2,1)}, u32[]{:S(2)}, u32[]{:S(2)}) async-start(bf16[16,64,1024]{2,1,0:T(8,128)(2,1)} %copy-done), calls=%async_computation.2 | async-start | bytes 4194304 | tf_op jit(solution)/shard_map/all_to_all | solution.py:137
  74.7 1.6 copy-done.1
  76.3 1.5 copy-done.4
  77.8 5.2 %hidden_terms.1 = (bf16[128,896]{1,0:T(8,128)(2,1)S(1)}, bf16[128,896]{1,0:T(8,128)(2,1)S(1)}, bf16[128,896]{1,0:T(8,128)(2,1)S(1)}, bf16[128,896]{1,0:T(8,128)(...) custom-call(s32[5]{0:T(128)S(1)} %stack.23.pos_ref, ...), custom_call_target="tpu_custom_call" | custom-call | flops 1879048192 | bytes 4194304 | tf_op jit(solution)/shard_map/hidden_terms/pallas_call | solution.py:154
  83.0 2.6 %collective-permute-start.2 = (bf16[128,896]{1,0:T(8,128)(2,1)S(1)}, bf16[128,896]{1,0:T(8,128)(2,1)S(1)}, u32[]{:S(2)}, u32[]{:S(2)}) collective-permute-start(bf16[128,896]{1,0:T(8,128)(2,1)S(1)} %get-tuple-element.19), channel_id=1, source_target_pairs={{0,1},{1,2},{2,3},{3,4},{4,5},{5,6},{6,7},{7,256},{8,9},{9,10},{10... | collective-permute-start | bytes 688136 | tf_op jit(solution)/shard_map/ppermute | solution.py:75
  85.7 7.3 %collective-permute-start.3 = (bf16[128,896]{1,0:T(8,128)(2,1)S(1)}, bf16[128,896]{1,0:T(8,128)(2,1)S(1)}, u32[]{:S(2)}, u32[]{:S(2)}) collective-permute-start(bf16[128,896]{1,0:T(8,128)(2,1)S(1)} %get-tuple-element.21), channel_id=1, source_target_pairs={{0,263},{1,0},{2,1},{3,2},{4,3},{5,4},{6,5},{7,6},{8,271},{9,8},{1... | collective-permute-start | bytes 688136 | tf_op jit(solution)/shard_map/ppermute | solution.py:75
  93.0 4.1 %collective-permute-done.2.refs_0_ = bf16[128,896]{1,0:T(8,128)(2,1)S(1)} collective-permute-done((bf16[128,896]{1,0:T(8,128)(2,1)S(1)}, bf16[128,896]{1,0:T(8,128)(2,1)S(1)}, u32[]{:S(2)}, u32[]{:S(2)}) %collective-permute-start.2) | collective-permute-done | bytes 229408 | tf_op jit(solution)/shard_map/ppermute | solution.py:75
  97.1 0.2 collective-permute-done.3.refs_2_
  97.2 0.1 sums.3
  97.3 2.8 %collective-permute-start.4 = (bf16[128,896]{1,0:T(8,128)(2,1)S(1)}, bf16[128,896]{1,0:T(8,128)(2,1)S(1)}, u32[]{:S(2)}, u32[]{:S(2)}) collective-permute-start(bf16[128,896]{1,0:T(8,128)(2,1)S(1)} %get-tuple-element.23), channel_id=1, source_target_pairs={{0,1},{1,2},{2,3},{3,4},{4,5},{5,6},{6,7},{7,256},{8,9},{9,10},{10... | collective-permute-start | bytes 688136 | tf_op jit(solution)/shard_map/ppermute | solution.py:75
  100.2 4.7 %collective-permute-start.5 = (bf16[128,896]{1,0:T(8,128)(2,1)S(1)}, bf16[128,896]{1,0:T(8,128)(2,1)S(1)}, u32[]{:S(2)}, u32[]{:S(2)}) collective-permute-start(bf16[128,896]{1,0:T(8,128)(2,1)S(1)} %get-tuple-element.25), channel_id=1, source_target_pairs={{0,263},{1,0},{2,1},{3,2},{4,3},{5,4},{6,5},{7,6},{8,271},{9,8},{1... | collective-permute-start | bytes 688136 | tf_op jit(solution)/shard_map/ppermute | solution.py:75
  104.9 2.1 %collective-permute-done.4.refs_0_ = bf16[128,896]{1,0:T(8,128)(2,1)S(1)} collective-permute-done((bf16[128,896]{1,0:T(8,128)(2,1)S(1)}, bf16[128,896]{1,0:T(8,128)(2,1)S(1)}, u32[]{:S(2)}, u32[]{:S(2)}) %collective-permute-start.4) | collective-permute-done | bytes 229408 | tf_op jit(solution)/shard_map/ppermute | solution.py:75
  106.9 1.5 collective-permute-done.5.refs_2_
  108.4 0.1 sums.4
  108.5 2.0 %collective-permute-start.6 = (bf16[128,896]{1,0:T(8,128)(2,1)S(1)}, bf16[128,896]{1,0:T(8,128)(2,1)S(1)}, u32[]{:S(2)}, u32[]{:S(2)}) collective-permute-start(bf16[128,896]{1,0:T(8,128)(2,1)S(1)} %get-tuple-element.27), channel_id=1, source_target_pairs={{0,1},{1,2},{2,3},{3,4},{4,5},{5,6},{6,7},{7,256},{8,9},{9,10},{10... | collective-permute-start | bytes 688136 | tf_op jit(solution)/shard_map/ppermute | solution.py:75
  110.5 5.6 %collective-permute-start.8 = (bf16[128,896]{1,0:T(8,128)(2,1)S(1)}, bf16[128,896]{1,0:T(8,128)(2,1)S(1)}, u32[]{:S(2)}, u32[]{:S(2)}) collective-permute-start(bf16[128,896]{1,0:T(8,128)(2,1)S(1)} %get-tuple-element.29), channel_id=1, source_target_pairs={{0,263},{1,0},{2,1},{3,2},{4,3},{5,4},{6,5},{7,6},{8,271},{9,8},{1... | collective-permute-start | bytes 688136 | tf_op jit(solution)/shard_map/ppermute | solution.py:75
  116.0 0.0 all-gather.2.cloned.1.call-done.hid_ref
  116.1 2.0 %copy-done.2 = bf16[2048,896]{1,0:T(8,128)(2,1)S(1)} copy-done((bf16[2048,896]{1,0:T(8,128)(2,1)S(1)}, bf16[2048,896]{1,0:T(8,128)(2,1)}, u32[]{:S(2)}) %copy-start.2) | copy-done | bytes 3670040
  118.1 1.5 copy-done.5
  119.6 4.2 %output_terms.1.refs_2_.refs_0_ = bf16[1024,1024]{1,0:T(8,128)(2,1)} custom-call(s32[5]{0:T(128)S(1)} %stack.23.pos_ref, bf16[2048,896]{1,0:T(8,128)(2,1)S(1)} %copy-done.2, bf16[896,1024]{1,0:T(8,128)(2,1)S(1)} %copy-done.5), custom_call_target="tpu_custom_call" | custom-call | flops 1879048192 | bytes 8388608 | tf_op jit(solution)/shard_map/output_terms/pallas_call | solution.py:173
  123.8 0.0 all-to-all-done.2.rest_ref
  123.8 7.4 %all-to-all-start = ((bf16[16,64,1024]{2,1,0:T(8,128)(2,1)}), bf16[16,64,1024]{2,1,0:T(8,128)(2,1)}, u32[]{:S(2)}, u32[]{:S(2)}) async-start(bf16[16,64,1024]{2,1,0:T(8,128)(2,1)} %bitcast.5), calls=%async_computation | async-start | bytes 4194304 | tf_op jit(solution)/shard_map/all_to_all | solution.py:137
  131.2 2.0 %copy-done.3 = bf16[2048,896]{1,0:T(8,128)(2,1)S(1)} copy-done((bf16[2048,896]{1,0:T(8,128)(2,1)S(1)}, bf16[2048,896]{1,0:T(8,128)(2,1)}, u32[]{:S(2)}) %copy-start.3) | copy-done | bytes 3670040
  133.3 6.8 %weight_terms.1.a_ref = bf16[896,1024]{1,0:T(8,128)(2,1)S(1)} custom-call(s32[5]{0:T(128)S(1)} %stack.23.pos_ref, bf16[2048,896]{1,0:T(8,128)(2,1)S(1)} %copy-done.3, bf16[16,64,1024]{2,1,0:T(8,128)(2,1)S(1)} %all-to-all-done.1.refs_0_.near_ref, bf16[16,64,1024]{2,1,0:T(8,128)(2,1)} %all-to-all-done.2.rest_ref, ...), custom_call_target="tpu_custom_call" | custom-call | flops 3758096384 | bytes 10485760 | tf_op jit(solution)/shard_map/weight_terms/pallas_call | solution.py:222
  140.1 1.9 %collective-permute-start.9 = (bf16[896,1024]{1,0:T(8,128)(2,1)S(1)}, bf16[896,1024]{1,0:T(8,128)(2,1)S(1)}, u32[]{:S(2)}, u32[]{:S(2)}) collective-permute-start(bf16[896,1024]{1,0:T(8,128)(2,1)S(1)} %weight_terms.1.a_ref), channel_id=1, source_target_pairs={{0,128},{1,129},{2,130},{3,131},{4,132},{5,133},{6,134},{7,135},{8... | collective-permute-start | bytes 5505032 | tf_op jit(solution)/shard_map/ppermute | solution.py:75
  142.0 0.1 sums.5
  142.1 1.9 %collective-permute-start.7 = (bf16[128,896]{1,0:T(8,128)(2,1)S(1)}, bf16[128,896]{1,0:T(8,128)(2,1)S(1)}, u32[]{:S(2)}, u32[]{:S(2)}) collective-permute-start(bf16[128,896]{1,0:T(8,128)(2,1)S(1)} %sums.5), channel_id=1, source_target_pairs={{0,1},{1,2},{2,3},{3,4},{4,5},{5,6},{6,7},{7,256},{8,9},{9,10},{10... | collective-permute-start | bytes 688136 | tf_op jit(solution)/shard_map/ppermute | solution.py:75
  144.0 1.8 %collective-permute-done.9.b_ref = bf16[896,1024]{1,0:T(8,128)(2,1)S(1)} collective-permute-done((bf16[896,1024]{1,0:T(8,128)(2,1)S(1)}, bf16[896,1024]{1,0:T(8,128)(2,1)S(1)}, u32[]{:S(2)}, u32[]{:S(2)}) %collective-permute-start.9) | collective-permute-done | bytes 1835040 | tf_op jit(solution)/shard_map/ppermute | solution.py:75
  145.8 1.9 %weight_sum.1 = bf16[896,1024]{1,0:T(8,128)(2,1)} custom-call(bf16[896,1024]{1,0:T(8,128)(2,1)S(1)} %weight_terms.1.a_ref, bf16[896,1024]{1,0:T(8,128)(2,1)S(1)} %collective-permute-done.9.b_ref), custom_call_target="tpu_custom_call" | custom-call | flops 1048576 | bytes 5242880 | tf_op jit(solution)/shard_map/weight_sum/pallas_call | solution.py:241
  147.7 7.0 %all-to-all-done.got_ref = bf16[16,64,1024]{2,1,0:T(8,128)(2,1)} async-done(((bf16[16,64,1024]{2,1,0:T(8,128)(2,1)}), bf16[16,64,1024]{2,1,0:T(8,128)(2,1)}, u32[]{:S(2)}, u32[]{:S(2)}) %all-to-all-start) | async-done | bytes 2097184 | tf_op jit(solution)/shard_map/all_to_all | solution.py:137
  154.7 3.5 %output_sum.1.refs_0_ = bf16[64,1024]{1,0:T(8,128)(2,1)} custom-call(bf16[16,64,1024]{2,1,0:T(8,128)(2,1)} %all-to-all-done.got_ref), custom_call_target="tpu_custom_call" | custom-call | flops 1048576 | bytes 2097152 | tf_op jit(solution)/shard_map/output_sum/pallas_call | solution.py:192
  158.2 0.0 copy-start.10
  158.2 0.9 copy-done.10
  159.1 1.0 gradients.1
  (16 shorter events, 0.0 us)
Async XLA Ops:
  7.2 108.9 %all-gather.2.cloned.1.call-start = ((), (), s32[]{:S(2)}) async-start(), calls=%async_computation.3 | async-start | bytes 3899392 | tf_op jit(solution)/shard_map/all_gather | solution.py:294
  9.1 19.4 %collective-permute-start = (bf16[64,1024]{1,0:T(8,128)(2,1)}, bf16[64,1024]{1,0:T(8,128)(2,1)S(1)}, u32[]{:S(2)}, u32[]{:S(2)}) collective-permute-start(bf16[64,1024]{1,0:T(8,128)(2,1)} %cot_ref.3), channel_id=1, source_target_pairs={{4,260},{5,261},{6,262},{7,263},{12,268},{13,269},{14,270},{15,271... | collective-permute-start | bytes 393224 | tf_op jit(solution)/shard_map/ppermute | solution.py:75
  28.5 0.9 copy-start.8
  31.4 7.6 %copy-start.9 = (bf16[64,1024]{1,0:T(8,128)(2,1)S(1)}, bf16[64,1024]{1,0:T(8,128)(2,1)}, u32[]{:S(2)}) copy-start(bf16[64,1024]{1,0:T(8,128)(2,1)} %cot_ref.3) | copy-start | bytes 393220
  31.4 34.7 %all-to-all-start.1 = ((bf16[16,64,1024]{2,1,0:T(8,128)(2,1)}), bf16[16,64,1024]{2,1,0:T(8,128)(2,1)S(1)}, u32[]{:S(2)}, u32[]{:S(2)}) async-start(bf16[16,64,1024]{2,1,0:T(8,128)(2,1)} %copies.2), calls=%async_computation.1 | async-start | bytes 4194304 | tf_op jit(solution)/shard_map/all_to_all | solution.py:137
  39.0 0.7 collective-permute-start.1
  66.8 1.4 copy-start
  68.2 55.6 %all-to-all-start.2 = ((bf16[16,64,1024]{2,1,0:T(8,128)(2,1)}), bf16[16,64,1024]{2,1,0:T(8,128)(2,1)}, u32[]{:S(2)}, u32[]{:S(2)}) async-start(bf16[16,64,1024]{2,1,0:T(8,128)(2,1)} %copy-done), calls=%async_computation.2 | async-start | bytes 4194304 | tf_op jit(solution)/shard_map/all_to_all | solution.py:137
  74.7 1.6 copy-start.1
  76.3 1.5 copy-start.4
  83.0 14.0 %collective-permute-start.2 = (bf16[128,896]{1,0:T(8,128)(2,1)S(1)}, bf16[128,896]{1,0:T(8,128)(2,1)S(1)}, u32[]{:S(2)}, u32[]{:S(2)}) collective-permute-start(bf16[128,896]{1,0:T(8,128)(2,1)S(1)} %get-tuple-element.19), channel_id=1, source_target_pairs={{0,1},{1,2},{2,3},{3,4},{4,5},{5,6},{6,7},{7,256},{8,9},{9,10},{10... | collective-permute-start | bytes 688136 | tf_op jit(solution)/shard_map/ppermute | solution.py:75
  85.7 11.5 %collective-permute-start.3 = (bf16[128,896]{1,0:T(8,128)(2,1)S(1)}, bf16[128,896]{1,0:T(8,128)(2,1)S(1)}, u32[]{:S(2)}, u32[]{:S(2)}) collective-permute-start(bf16[128,896]{1,0:T(8,128)(2,1)S(1)} %get-tuple-element.21), channel_id=1, source_target_pairs={{0,263},{1,0},{2,1},{3,2},{4,3},{5,4},{6,5},{7,6},{8,271},{9,8},{1... | collective-permute-start | bytes 688136 | tf_op jit(solution)/shard_map/ppermute | solution.py:75
  97.3 9.6 %collective-permute-start.4 = (bf16[128,896]{1,0:T(8,128)(2,1)S(1)}, bf16[128,896]{1,0:T(8,128)(2,1)S(1)}, u32[]{:S(2)}, u32[]{:S(2)}) collective-permute-start(bf16[128,896]{1,0:T(8,128)(2,1)S(1)} %get-tuple-element.23), channel_id=1, source_target_pairs={{0,1},{1,2},{2,3},{3,4},{4,5},{5,6},{6,7},{7,256},{8,9},{9,10},{10... | collective-permute-start | bytes 688136 | tf_op jit(solution)/shard_map/ppermute | solution.py:75
  100.2 8.2 %collective-permute-start.5 = (bf16[128,896]{1,0:T(8,128)(2,1)S(1)}, bf16[128,896]{1,0:T(8,128)(2,1)S(1)}, u32[]{:S(2)}, u32[]{:S(2)}) collective-permute-start(bf16[128,896]{1,0:T(8,128)(2,1)S(1)} %get-tuple-element.25), channel_id=1, source_target_pairs={{0,263},{1,0},{2,1},{3,2},{4,3},{5,4},{6,5},{7,6},{8,271},{9,8},{1... | collective-permute-start | bytes 688136 | tf_op jit(solution)/shard_map/ppermute | solution.py:75
  108.5 22.7 %collective-permute-start.6 = (bf16[128,896]{1,0:T(8,128)(2,1)S(1)}, bf16[128,896]{1,0:T(8,128)(2,1)S(1)}, u32[]{:S(2)}, u32[]{:S(2)}) collective-permute-start(bf16[128,896]{1,0:T(8,128)(2,1)S(1)} %get-tuple-element.27), channel_id=1, source_target_pairs={{0,1},{1,2},{2,3},{3,4},{4,5},{5,6},{6,7},{7,256},{8,9},{9,10},{10... | collective-permute-start | bytes 688136 | tf_op jit(solution)/shard_map/ppermute | solution.py:75
  110.5 20.8 %collective-permute-start.8 = (bf16[128,896]{1,0:T(8,128)(2,1)S(1)}, bf16[128,896]{1,0:T(8,128)(2,1)S(1)}, u32[]{:S(2)}, u32[]{:S(2)}) collective-permute-start(bf16[128,896]{1,0:T(8,128)(2,1)S(1)} %get-tuple-element.29), channel_id=1, source_target_pairs={{0,263},{1,0},{2,1},{3,2},{4,3},{5,4},{6,5},{7,6},{8,271},{9,8},{1... | collective-permute-start | bytes 688136 | tf_op jit(solution)/shard_map/ppermute | solution.py:75
  116.1 2.0 %copy-start.2 = (bf16[2048,896]{1,0:T(8,128)(2,1)S(1)}, bf16[2048,896]{1,0:T(8,128)(2,1)}, u32[]{:S(2)}) copy-start(bf16[2048,896]{1,0:T(8,128)(2,1)} %all-gather.2.cloned.1.call-done.hid_ref) | copy-start | bytes 11010052
  118.1 1.5 copy-start.5
  123.8 30.9 %all-to-all-start = ((bf16[16,64,1024]{2,1,0:T(8,128)(2,1)}), bf16[16,64,1024]{2,1,0:T(8,128)(2,1)}, u32[]{:S(2)}, u32[]{:S(2)}) async-start(bf16[16,64,1024]{2,1,0:T(8,128)(2,1)} %bitcast.5), calls=%async_computation | async-start | bytes 4194304 | tf_op jit(solution)/shard_map/all_to_all | solution.py:137
  131.2 2.0 %copy-start.3 = (bf16[2048,896]{1,0:T(8,128)(2,1)S(1)}, bf16[2048,896]{1,0:T(8,128)(2,1)}, u32[]{:S(2)}) copy-start(bf16[2048,896]{1,0:T(8,128)(2,1)} %all-gather.2.cloned.1.call-done.hid_ref) | copy-start | bytes 11010052
  140.1 5.7 %collective-permute-start.9 = (bf16[896,1024]{1,0:T(8,128)(2,1)S(1)}, bf16[896,1024]{1,0:T(8,128)(2,1)S(1)}, u32[]{:S(2)}, u32[]{:S(2)}) collective-permute-start(bf16[896,1024]{1,0:T(8,128)(2,1)S(1)} %weight_terms.1.a_ref), channel_id=1, source_target_pairs={{0,128},{1,129},{2,130},{3,131},{4,132},{5,133},{6,134},{7,135},{8... | collective-permute-start | bytes 5505032 | tf_op jit(solution)/shard_map/ppermute | solution.py:75
  142.1 16.1 %collective-permute-start.7 = (bf16[128,896]{1,0:T(8,128)(2,1)S(1)}, bf16[128,896]{1,0:T(8,128)(2,1)S(1)}, u32[]{:S(2)}, u32[]{:S(2)}) collective-permute-start(bf16[128,896]{1,0:T(8,128)(2,1)S(1)} %sums.5), channel_id=1, source_target_pairs={{0,1},{1,2},{2,3},{3,4},{4,5},{5,6},{6,7},{7,256},{8,9},{9,10},{10... | collective-permute-start | bytes 688136 | tf_op jit(solution)/shard_map/ppermute | solution.py:75
  147.7 10.6 %copy-start.6 = (bf16[128,896]{1,0:T(8,128)(2,1)S(1)}, bf16[128,896]{1,0:T(8,128)(2,1)}, u32[]{:S(2)}) copy-start(bf16[128,896]{1,0:T(8,128)(2,1)} %gate_ref.3) | copy-start | bytes 688132
  147.7 10.6 %copy-start.7 = (bf16[128,896]{1,0:T(8,128)(2,1)S(1)}, bf16[128,896]{1,0:T(8,128)(2,1)}, u32[]{:S(2)}) copy-start(bf16[128,896]{1,0:T(8,128)(2,1)} %up_ref.3) | copy-start | bytes 688132
  158.2 0.9 copy-start.10
Sparse Core Ops, SparseCore 0:
  10.7 90.5 all-gather.1

commit v8 on v7

--- a/solution.py
+++ b/solution.py
@@ -305,12 +305,12 @@
     a2, b2 = send(a, right), send(b, left)
     a, b = add(((a2, p2), (b2, m1)))
     a3, b = send(a, right), send(b, left)
-    (a,) = add(((a3, p1),), o)
+    (a,) = add(((a3, p1),))
     a = send(a, right)
     output = total_of(exchange(o.reshape(16, 64, 1024)))
     grad_gate, grad_up = ends_of(gate, up, here, a, b, output)
 
-    part = grad_of(pos, hid, near, rest, o, a3, b)
+    part = grad_of(pos, hid, near, rest, o, a2, b2)
     grad_weight = pair_of(part, send(part, SWAP_CORE))
     return output, grad_gate, grad_up, grad_weight
 

time: 170 us -> 164 us (0.965); the launches traced: 167 us -> 163 us
  waiting for transfers between devices: 46.6 us -> 41.4 us
  local copies, waits for them, and re-layouts: 12 us -> 14.9 us
    all_to_all x3, waiting for transfers between devices: 33.5 us -> 26.4 us  [exchange(): return lax.all_to_all(blocks, PLANE, 0, 0, tiled=True)]
    unnamed x22 -> x26, local copies, waits for them, and re-layouts: 11.9 us -> 14.8 us
    ppermute x10, waiting for transfers between devices: 13.1 us -> 15 us  [send(): return lax.ppermute(a, AXES, perm)]
  transfers between devices with their start and end apart: 14 -> 14, of which waited for: 8 -> 6; matrix products, arithmetic and copies ran while one was open for 0% -> 0% of each run, Pallas kernels for 15% -> 15%
where the time goes in v8:
time: 164 us; the launch traced here: 163 us
  starting transfers between devices  66 us (40%)
  waiting for transfers between devices  41.4 us (25%)
  Pallas kernels  26.9 us (16%)
  local copies, waits for them, and re-layouts  14.9 us (9%)
  between operations  14.3 us (9%)
    ppermute x10, starting transfers between devices, send(): return lax.ppermute(a, AXES, perm)  44.7 us
    all_to_all x3, waiting for transfers between devices, exchange(): return lax.all_to_all(blocks, PLANE, 0, 0, tiled=True)  26.4 us
    all_to_all x3, starting transfers between devices, exchange(): return lax.all_to_all(blocks, PLANE, 0, 0, tiled=True)  21.2 us
    ppermute x10, waiting for transfers between devices, send(): return lax.ppermute(a, AXES, perm)  15 us
    unnamed x26, local copies, waits for them, and re-layouts  14.8 us
    pallas_call x1, Pallas kernels, grad_of(): pl.pallas_call(grad_kernel, grid=(4,), out_shape=jax.ShapeDtypeStruct((89...  6.81 us
    pallas_call x1, Pallas kernels, terms_of(): pl.pallas_call(functools.partial(term_kernel, parts), out_shape=[jax.Shap...  5.2 us
    pallas_call x1, Pallas kernels, total_of(): pl.pallas_call(total_kernel, grid=(4,), out_shape=jax.ShapeDtypeStruct((6...  3.56 us
  transfers between devices with their start and end apart: 14, of which 6 were waited for; matrix products, arithmetic and copies ran while one was open for 0% of the time, Pallas kernels for 15%

profile of v8, /device:TPU:6, one launch (start us, length us, event | category | flops | bytes accessed | tf_op | source)
XLA Modules:
  0.0 163.5 jit_solution(9618643145057126214)
XLA Ops:
  7.2 0.0 all-gather.2.cloned.1.call-start
  7.2 1.8 %hidden.1 = bf16[128,896]{1,0:T(8,128)(2,1)} custom-call(bf16[128,896]{1,0:T(8,128)(2,1)} %gate_ref.3, bf16[128,896]{1,0:T(8,128)(2,1)} %up_ref.3), custom_call_target="tpu_custom_call" | custom-call | flops 1048576 | bytes 1048576 | tf_op jit(solution)/shard_map/hidden/pallas_call | solution.py:101
  9.1 0.0 all-gather.2.cloned.1.call-update
  9.1 15.7 %collective-permute-start = (bf16[64,1024]{1,0:T(8,128)(2,1)}, bf16[64,1024]{1,0:T(8,128)(2,1)S(1)}, u32[]{:S(2)}, u32[]{:S(2)}) collective-permute-start(bf16[64,1024]{1,0:T(8,128)(2,1)} %cot_ref.3), channel_id=1, source_target_pairs={{4,260},{5,261},{6,262},{7,263},{12,268},{13,269},{14,270},{15,271... | collective-permute-start | bytes 393224 | tf_op jit(solution)/shard_map/ppermute | solution.py:75
  24.8 0.1 stack.23.pos_ref
  24.9 3.6 %collective-permute-done.far_ref = bf16[64,1024]{1,0:T(8,128)(2,1)S(1)} collective-permute-done((bf16[64,1024]{1,0:T(8,128)(2,1)}, bf16[64,1024]{1,0:T(8,128)(2,1)S(1)}, u32[]{:S(2)}, u32[]{:S(2)}) %collective-permute-start) | collective-permute-done | bytes 131104 | tf_op jit(solution)/shard_map/ppermute | solution.py:75
  28.5 0.9 copy-done.10
  29.4 2.0 %copies.2 = bf16[16,64,1024]{2,1,0:T(8,128)(2,1)} custom-call(s32[5]{0:T(128)S(1)} %stack.23.pos_ref, bf16[64,1024]{1,0:T(8,128)(2,1)S(1)} %copy-done.10, bf16[64,1024]{1,0:T(8,128)(2,1)S(1)} %collective-permute-done.far_ref), custom_call_target="tpu_custom_call" | custom-call | bytes 2097152 | tf_op jit(solution)/shard_map/copies/pallas_call | solution.py:125
  31.4 7.6 %all-to-all-start.1 = ((bf16[16,64,1024]{2,1,0:T(8,128)(2,1)}), bf16[16,64,1024]{2,1,0:T(8,128)(2,1)S(1)}, u32[]{:S(2)}, u32[]{:S(2)}) async-start(bf16[16,64,1024]{2,1,0:T(8,128)(2,1)} %copies.2), calls=%async_computation.1 | async-start | bytes 4194304 | tf_op jit(solution)/shard_map/all_to_all | solution.py:137
  39.0 0.7 collective-permute-start.1
  39.7 26.4 %all-to-all-done.1.refs_0_.near_ref = bf16[16,64,1024]{2,1,0:T(8,128)(2,1)S(1)} async-done(((bf16[16,64,1024]{2,1,0:T(8,128)(2,1)}), bf16[16,64,1024]{2,1,0:T(8,128)(2,1)S(1)}, u32[]{:S(2)}, u32[]{:S(2)}) %all-to-all-start.1) | async-done | bytes 2097184 | tf_op jit(solution)/shard_map/all_to_all | solution.py:137
  66.1 0.7 copies.3.refs_0_
  66.8 1.3 copy-done
  68.2 6.5 %all-to-all-start.2 = ((bf16[16,64,1024]{2,1,0:T(8,128)(2,1)}), bf16[16,64,1024]{2,1,0:T(8,128)(2,1)}, u32[]{:S(2)}, u32[]{:S(2)}) async-start(bf16[16,64,1024]{2,1,0:T(8,128)(2,1)} %copy-done), calls=%async_computation.2 | async-start | bytes 4194304 | tf_op jit(solution)/shard_map/all_to_all | solution.py:137
  74.7 1.6 copy-done.1
  76.3 1.5 copy-done.6
  77.8 5.2 %hidden_terms.1 = (bf16[128,896]{1,0:T(8,128)(2,1)S(1)}, bf16[128,896]{1,0:T(8,128)(2,1)S(1)}, bf16[128,896]{1,0:T(8,128)(2,1)S(1)}, bf16[128,896]{1,0:T(8,128)(...) custom-call(s32[5]{0:T(128)S(1)} %stack.23.pos_ref, ...), custom_call_target="tpu_custom_call" | custom-call | flops 1879048192 | bytes 4194304 | tf_op jit(solution)/shard_map/hidden_terms/pallas_call | solution.py:154
  83.0 2.6 %collective-permute-start.2 = (bf16[128,896]{1,0:T(8,128)(2,1)S(1)}, bf16[128,896]{1,0:T(8,128)(2,1)S(1)}, u32[]{:S(2)}, u32[]{:S(2)}) collective-permute-start(bf16[128,896]{1,0:T(8,128)(2,1)S(1)} %get-tuple-element.19), channel_id=1, source_target_pairs={{0,1},{1,2},{2,3},{3,4},{4,5},{5,6},{6,7},{7,256},{8,9},{9,10},{10... | collective-permute-start | bytes 688136 | tf_op jit(solution)/shard_map/ppermute | solution.py:75
  85.7 7.3 %collective-permute-start.3 = (bf16[128,896]{1,0:T(8,128)(2,1)S(1)}, bf16[128,896]{1,0:T(8,128)(2,1)S(1)}, u32[]{:S(2)}, u32[]{:S(2)}) collective-permute-start(bf16[128,896]{1,0:T(8,128)(2,1)S(1)} %get-tuple-element.21), channel_id=1, source_target_pairs={{0,263},{1,0},{2,1},{3,2},{4,3},{5,4},{6,5},{7,6},{8,271},{9,8},{1... | collective-permute-start | bytes 688136 | tf_op jit(solution)/shard_map/ppermute | solution.py:75
  92.9 4.1 %collective-permute-done.2.refs_0_ = bf16[128,896]{1,0:T(8,128)(2,1)S(1)} collective-permute-done((bf16[128,896]{1,0:T(8,128)(2,1)S(1)}, bf16[128,896]{1,0:T(8,128)(2,1)S(1)}, u32[]{:S(2)}, u32[]{:S(2)}) %collective-permute-start.2) | collective-permute-done | bytes 229408 | tf_op jit(solution)/shard_map/ppermute | solution.py:75
  97.0 0.2 collective-permute-done.3.refs_2_
  97.3 0.8 sums.3
  98.1 2.8 %collective-permute-start.4 = (bf16[128,896]{1,0:T(8,128)(2,1)}, bf16[128,896]{1,0:T(8,128)(2,1)S(1)}, u32[]{:S(2)}, u32[]{:S(2)}) collective-permute-start(bf16[128,896]{1,0:T(8,128)(2,1)} %get-tuple-element.23), channel_id=1, source_target_pairs={{0,1},{1,2},{2,3},{3,4},{4,5},{5,6},{6,7},{7,256},{8,9},{9,10},{10... | collective-permute-start | bytes 688136 | tf_op jit(solution)/shard_map/ppermute | solution.py:75
  100.9 4.7 %collective-permute-start.5 = (bf16[128,896]{1,0:T(8,128)(2,1)}, bf16[128,896]{1,0:T(8,128)(2,1)S(1)}, u32[]{:S(2)}, u32[]{:S(2)}) collective-permute-start(bf16[128,896]{1,0:T(8,128)(2,1)} %get-tuple-element.25), channel_id=1, source_target_pairs={{0,263},{1,0},{2,1},{3,2},{4,3},{5,4},{6,5},{7,6},{8,271},{9,8},{1... | collective-permute-start | bytes 688136 | tf_op jit(solution)/shard_map/ppermute | solution.py:75
  105.6 0.0 all-gather.2.cloned.1.call-done.hid_ref
  105.6 2.0 %copy-done.4 = bf16[2048,896]{1,0:T(8,128)(2,1)S(1)} copy-done((bf16[2048,896]{1,0:T(8,128)(2,1)S(1)}, bf16[2048,896]{1,0:T(8,128)(2,1)}, u32[]{:S(2)}) %copy-start.4) | copy-done | bytes 3670040
  107.7 1.5 copy-done.7
  109.2 2.9 %output_terms.1.refs_0_ = bf16[1024,1024]{1,0:T(8,128)(2,1)S(1)} custom-call(s32[5]{0:T(128)S(1)} %stack.23.pos_ref, bf16[2048,896]{1,0:T(8,128)(2,1)S(1)} %copy-done.4, bf16[896,1024]{1,0:T(8,128)(2,1)S(1)} %copy-done.7), custom_call_target="tpu_custom_call" | custom-call | flops 1879048192 | bytes 8388608 | tf_op jit(solution)/shard_map/output_terms/pallas_call | solution.py:173
  112.1 1.3 copy-done.2
  113.4 7.2 %all-to-all-start = ((bf16[16,64,1024]{2,1,0:T(8,128)(2,1)}), bf16[16,64,1024]{2,1,0:T(8,128)(2,1)}, u32[]{:S(2)}, u32[]{:S(2)}) async-start(bf16[16,64,1024]{2,1,0:T(8,128)(2,1)} %bitcast.8), calls=%async_computation | async-start | bytes 4194304 | tf_op jit(solution)/shard_map/all_to_all | solution.py:137
  120.6 0.0 collective-permute-done.5.refs_2_
  120.6 1.6 copy-done.3
  122.2 2.0 %copy-done.5 = bf16[2048,896]{1,0:T(8,128)(2,1)S(1)} copy-done((bf16[2048,896]{1,0:T(8,128)(2,1)S(1)}, bf16[2048,896]{1,0:T(8,128)(2,1)}, u32[]{:S(2)}) %copy-start.5) | copy-done | bytes 3670040
  124.2 6.8 %weight_terms.1.a_ref = bf16[896,1024]{1,0:T(8,128)(2,1)S(1)} custom-call(s32[5]{0:T(128)S(1)} %stack.23.pos_ref, bf16[2048,896]{1,0:T(8,128)(2,1)S(1)} %copy-done.5, bf16[16,64,1024]{2,1,0:T(8,128)(2,1)S(1)} %all-to-all-done.1.refs_0_.near_ref, bf16[16,64,1024]{2,1,0:T(8,128)(2,1)} %all-to-all-done.2.rest_ref, bf16[1024,1024]{1,0:T(8,128)(2,1)S(1)} %copy-done.3, ...), custom_call_target="tpu_custom_call" | custom-call | flops 3758096384 | bytes 10485760 | tf_op jit(solution)/shard_map/weight_terms/pallas_call | solution.py:222
  131.1 1.9 %collective-permute-start.9 = (bf16[896,1024]{1,0:T(8,128)(2,1)S(1)}, bf16[896,1024]{1,0:T(8,128)(2,1)S(1)}, u32[]{:S(2)}, u32[]{:S(2)}) collective-permute-start(bf16[896,1024]{1,0:T(8,128)(2,1)S(1)} %weight_terms.1.a_ref), channel_id=1, source_target_pairs={{0,128},{1,129},{2,130},{3,131},{4,132},{5,133},{6,134},{7,135},{8... | collective-permute-start | bytes 5505032 | tf_op jit(solution)/shard_map/ppermute | solution.py:75
  133.0 0.1 sums.4
  133.1 1.9 %collective-permute-start.6 = (bf16[128,896]{1,0:T(8,128)(2,1)S(1)}, bf16[128,896]{1,0:T(8,128)(2,1)S(1)}, u32[]{:S(2)}, u32[]{:S(2)}) collective-permute-start(bf16[128,896]{1,0:T(8,128)(2,1)S(1)} %get-tuple-element.27), channel_id=1, source_target_pairs={{0,1},{1,2},{2,3},{3,4},{4,5},{5,6},{6,7},{7,256},{8,9},{9,10},{10... | collective-permute-start | bytes 688136 | tf_op jit(solution)/shard_map/ppermute | solution.py:75
  135.0 5.1 %collective-permute-start.8 = (bf16[128,896]{1,0:T(8,128)(2,1)S(1)}, bf16[128,896]{1,0:T(8,128)(2,1)S(1)}, u32[]{:S(2)}, u32[]{:S(2)}) collective-permute-start(bf16[128,896]{1,0:T(8,128)(2,1)S(1)} %get-tuple-element.29), channel_id=1, source_target_pairs={{0,263},{1,0},{2,1},{3,2},{4,3},{5,4},{6,5},{7,6},{8,271},{9,8},{1... | collective-permute-start | bytes 688136 | tf_op jit(solution)/shard_map/ppermute | solution.py:75
  140.2 4.0 %collective-permute-done.6.refs_0_ = bf16[128,896]{1,0:T(8,128)(2,1)S(1)} collective-permute-done((bf16[128,896]{1,0:T(8,128)(2,1)S(1)}, bf16[128,896]{1,0:T(8,128)(2,1)S(1)}, u32[]{:S(2)}, u32[]{:S(2)}) %collective-permute-start.6) | collective-permute-done | bytes 229408 | tf_op jit(solution)/shard_map/ppermute | solution.py:75
  144.2 0.1 sums.5
  144.3 1.9 %collective-permute-start.7 = (bf16[128,896]{1,0:T(8,128)(2,1)S(1)}, bf16[128,896]{1,0:T(8,128)(2,1)S(1)}, u32[]{:S(2)}, u32[]{:S(2)}) collective-permute-start(bf16[128,896]{1,0:T(8,128)(2,1)S(1)} %sums.5), channel_id=1, source_target_pairs={{0,1},{1,2},{2,3},{3,4},{4,5},{5,6},{6,7},{7,256},{8,9},{9,10},{10... | collective-permute-start | bytes 688136 | tf_op jit(solution)/shard_map/ppermute | solution.py:75
  146.2 0.0 collective-permute-done.9.b_ref
  146.2 1.9 %weight_sum.1 = bf16[896,1024]{1,0:T(8,128)(2,1)} custom-call(bf16[896,1024]{1,0:T(8,128)(2,1)S(1)} %weight_terms.1.a_ref, bf16[896,1024]{1,0:T(8,128)(2,1)S(1)} %collective-permute-done.9.b_ref), custom_call_target="tpu_custom_call" | custom-call | flops 1048576 | bytes 5242880 | tf_op jit(solution)/shard_map/weight_sum/pallas_call | solution.py:241
  148.1 3.6 %output_sum.1.refs_0_ = bf16[64,1024]{1,0:T(8,128)(2,1)} custom-call(bf16[16,64,1024]{2,1,0:T(8,128)(2,1)} %all-to-all-done.got_ref), custom_call_target="tpu_custom_call" | custom-call | flops 1048576 | bytes 2097152 | tf_op jit(solution)/shard_map/output_sum/pallas_call | solution.py:192
  151.7 0.0 collective-permute-done.8.b_ref
  151.7 3.0 %collective-permute-done.7.a_ref = bf16[128,896]{1,0:T(8,128)(2,1)S(1)} collective-permute-done((bf16[128,896]{1,0:T(8,128)(2,1)S(1)}, bf16[128,896]{1,0:T(8,128)(2,1)S(1)}, u32[]{:S(2)}, u32[]{:S(2)}) %collective-permute-start.7) | collective-permute-done | bytes 229408 | tf_op jit(solution)/shard_map/ppermute | solution.py:75
  154.7 0.9 copy-done.12
  155.6 1.0 gradients.1
  (20 shorter events, 0.0 us)
Async XLA Ops:
  7.2 98.5 %all-gather.2.cloned.1.call-start = ((), (), s32[]{:S(2)}) async-start(), calls=%async_computation.3 | async-start | bytes 3899392 | tf_op jit(solution)/shard_map/all_gather | solution.py:294
  9.1 19.4 %collective-permute-start = (bf16[64,1024]{1,0:T(8,128)(2,1)}, bf16[64,1024]{1,0:T(8,128)(2,1)S(1)}, u32[]{:S(2)}, u32[]{:S(2)}) collective-permute-start(bf16[64,1024]{1,0:T(8,128)(2,1)} %cot_ref.3), channel_id=1, source_target_pairs={{4,260},{5,261},{6,262},{7,263},{12,268},{13,269},{14,270},{15,271... | collective-permute-start | bytes 393224 | tf_op jit(solution)/shard_map/ppermute | solution.py:75
  28.5 0.9 copy-start.10
  31.4 7.6 %copy-start.11 = (bf16[64,1024]{1,0:T(8,128)(2,1)S(1)}, bf16[64,1024]{1,0:T(8,128)(2,1)}, u32[]{:S(2)}) copy-start(bf16[64,1024]{1,0:T(8,128)(2,1)} %cot_ref.3) | copy-start | bytes 393220
  31.4 34.7 %all-to-all-start.1 = ((bf16[16,64,1024]{2,1,0:T(8,128)(2,1)}), bf16[16,64,1024]{2,1,0:T(8,128)(2,1)S(1)}, u32[]{:S(2)}, u32[]{:S(2)}) async-start(bf16[16,64,1024]{2,1,0:T(8,128)(2,1)} %copies.2), calls=%async_computation.1 | async-start | bytes 4194304 | tf_op jit(solution)/shard_map/all_to_all | solution.py:137
  39.0 0.7 collective-permute-start.1
  66.8 1.4 copy-start
  68.2 45.2 %all-to-all-start.2 = ((bf16[16,64,1024]{2,1,0:T(8,128)(2,1)}), bf16[16,64,1024]{2,1,0:T(8,128)(2,1)}, u32[]{:S(2)}, u32[]{:S(2)}) async-start(bf16[16,64,1024]{2,1,0:T(8,128)(2,1)} %copy-done), calls=%async_computation.2 | async-start | bytes 4194304 | tf_op jit(solution)/shard_map/all_to_all | solution.py:137
  74.7 1.6 copy-start.1
  76.3 1.5 copy-start.6
  83.0 14.0 %collective-permute-start.2 = (bf16[128,896]{1,0:T(8,128)(2,1)S(1)}, bf16[128,896]{1,0:T(8,128)(2,1)S(1)}, u32[]{:S(2)}, u32[]{:S(2)}) collective-permute-start(bf16[128,896]{1,0:T(8,128)(2,1)S(1)} %get-tuple-element.19), channel_id=1, source_target_pairs={{0,1},{1,2},{2,3},{3,4},{4,5},{5,6},{6,7},{7,256},{8,9},{9,10},{10... | collective-permute-start | bytes 688136 | tf_op jit(solution)/shard_map/ppermute | solution.py:75
  85.7 11.6 %collective-permute-start.3 = (bf16[128,896]{1,0:T(8,128)(2,1)S(1)}, bf16[128,896]{1,0:T(8,128)(2,1)S(1)}, u32[]{:S(2)}, u32[]{:S(2)}) collective-permute-start(bf16[128,896]{1,0:T(8,128)(2,1)S(1)} %get-tuple-element.21), channel_id=1, source_target_pairs={{0,263},{1,0},{2,1},{3,2},{4,3},{5,4},{6,5},{7,6},{8,271},{9,8},{1... | collective-permute-start | bytes 688136 | tf_op jit(solution)/shard_map/ppermute | solution.py:75
  98.1 22.5 %collective-permute-start.4 = (bf16[128,896]{1,0:T(8,128)(2,1)}, bf16[128,896]{1,0:T(8,128)(2,1)S(1)}, u32[]{:S(2)}, u32[]{:S(2)}) collective-permute-start(bf16[128,896]{1,0:T(8,128)(2,1)} %get-tuple-element.23), channel_id=1, source_target_pairs={{0,1},{1,2},{2,3},{3,4},{4,5},{5,6},{6,7},{7,256},{8,9},{9,10},{10... | collective-permute-start | bytes 688136 | tf_op jit(solution)/shard_map/ppermute | solution.py:75
  100.9 19.7 %collective-permute-start.5 = (bf16[128,896]{1,0:T(8,128)(2,1)}, bf16[128,896]{1,0:T(8,128)(2,1)S(1)}, u32[]{:S(2)}, u32[]{:S(2)}) collective-permute-start(bf16[128,896]{1,0:T(8,128)(2,1)} %get-tuple-element.25), channel_id=1, source_target_pairs={{0,263},{1,0},{2,1},{3,2},{4,3},{5,4},{6,5},{7,6},{8,271},{9,8},{1... | collective-permute-start | bytes 688136 | tf_op jit(solution)/shard_map/ppermute | solution.py:75
  105.6 2.0 %copy-start.4 = (bf16[2048,896]{1,0:T(8,128)(2,1)S(1)}, bf16[2048,896]{1,0:T(8,128)(2,1)}, u32[]{:S(2)}) copy-start(bf16[2048,896]{1,0:T(8,128)(2,1)} %all-gather.2.cloned.1.call-done.hid_ref) | copy-start | bytes 11010052
  107.7 1.5 copy-start.7
  112.1 1.3 copy-start.2
  113.4 34.7 %all-to-all-start = ((bf16[16,64,1024]{2,1,0:T(8,128)(2,1)}), bf16[16,64,1024]{2,1,0:T(8,128)(2,1)}, u32[]{:S(2)}, u32[]{:S(2)}) async-start(bf16[16,64,1024]{2,1,0:T(8,128)(2,1)} %bitcast.8), calls=%async_computation | async-start | bytes 4194304 | tf_op jit(solution)/shard_map/all_to_all | solution.py:137
  120.6 1.6 copy-start.3
  122.2 2.0 %copy-start.5 = (bf16[2048,896]{1,0:T(8,128)(2,1)S(1)}, bf16[2048,896]{1,0:T(8,128)(2,1)}, u32[]{:S(2)}) copy-start(bf16[2048,896]{1,0:T(8,128)(2,1)} %all-gather.2.cloned.1.call-done.hid_ref) | copy-start | bytes 11010052
  131.1 15.2 %collective-permute-start.9 = (bf16[896,1024]{1,0:T(8,128)(2,1)S(1)}, bf16[896,1024]{1,0:T(8,128)(2,1)S(1)}, u32[]{:S(2)}, u32[]{:S(2)}) collective-permute-start(bf16[896,1024]{1,0:T(8,128)(2,1)S(1)} %weight_terms.1.a_ref), channel_id=1, source_target_pairs={{0,128},{1,129},{2,130},{3,131},{4,132},{5,133},{6,134},{7,135},{8... | collective-permute-start | bytes 5505032 | tf_op jit(solution)/shard_map/ppermute | solution.py:75
  133.1 11.1 %collective-permute-start.6 = (bf16[128,896]{1,0:T(8,128)(2,1)S(1)}, bf16[128,896]{1,0:T(8,128)(2,1)S(1)}, u32[]{:S(2)}, u32[]{:S(2)}) collective-permute-start(bf16[128,896]{1,0:T(8,128)(2,1)S(1)} %get-tuple-element.27), channel_id=1, source_target_pairs={{0,1},{1,2},{2,3},{3,4},{4,5},{5,6},{6,7},{7,256},{8,9},{9,10},{10... | collective-permute-start | bytes 688136 | tf_op jit(solution)/shard_map/ppermute | solution.py:75
  135.0 16.7 %collective-permute-start.8 = (bf16[128,896]{1,0:T(8,128)(2,1)S(1)}, bf16[128,896]{1,0:T(8,128)(2,1)S(1)}, u32[]{:S(2)}, u32[]{:S(2)}) collective-permute-start(bf16[128,896]{1,0:T(8,128)(2,1)S(1)} %get-tuple-element.29), channel_id=1, source_target_pairs={{0,263},{1,0},{2,1},{3,2},{4,3},{5,4},{6,5},{7,6},{8,271},{9,8},{1... | collective-permute-start | bytes 688136 | tf_op jit(solution)/shard_map/ppermute | solution.py:75
  144.3 10.4 %collective-permute-start.7 = (bf16[128,896]{1,0:T(8,128)(2,1)S(1)}, bf16[128,896]{1,0:T(8,128)(2,1)S(1)}, u32[]{:S(2)}, u32[]{:S(2)}) collective-permute-start(bf16[128,896]{1,0:T(8,128)(2,1)S(1)} %sums.5), channel_id=1, source_target_pairs={{0,1},{1,2},{2,3},{3,4},{4,5},{5,6},{6,7},{7,256},{8,9},{9,10},{10... | collective-permute-start | bytes 688136 | tf_op jit(solution)/shard_map/ppermute | solution.py:75
  148.1 6.6 %copy-start.8 = (bf16[128,896]{1,0:T(8,128)(2,1)S(1)}, bf16[128,896]{1,0:T(8,128)(2,1)}, u32[]{:S(2)}) copy-start(bf16[128,896]{1,0:T(8,128)(2,1)} %gate_ref.3) | copy-start | bytes 688132
  148.1 6.6 %copy-start.9 = (bf16[128,896]{1,0:T(8,128)(2,1)S(1)}, bf16[128,896]{1,0:T(8,128)(2,1)}, u32[]{:S(2)}) copy-start(bf16[128,896]{1,0:T(8,128)(2,1)} %up_ref.3) | copy-start | bytes 688132
  154.7 0.9 copy-start.12
Sparse Core Ops, SparseCore 0:
  10.7 90.3 all-gather.1
